TPU v7x, 32 devices: a whole 2x2x4 slice. The times are simulated.
32 devices in a mesh: head: 4 (over x, core), seq: 4 (over z), dp: 2 (over y).
Axes of the slice: x: 2, y: 2, z: 4, core: 2. Of those that a mesh axis runs over, the one named last changes fastest.
Arguments:
- tokens: bfloat16 [16, 1024, 768], P('dp', 'seq'), may hold values from -6 to 6
- lengths: int32 [16], P('dp'), may hold values from 129 to 1024, as said below
- expert_ids: int32 [16, 1024, 1], P('dp', 'seq'), may hold values from 0 to 15; in each aligned block of 256 rows (0 to 255, 256 to 511, ..., all dimensions but the last counted through in order) at most 20 rows name the same one
- attention_gain: bfloat16 [768], P(('seq', 'dp')), may hold values from 0.5 to 1.5
- query_weight: bfloat16 [768, 768], P(('seq', 'dp'), 'head'), may hold values from -0.0390625 to 0.0390625
- key_weight: bfloat16 [768, 768], P(('seq', 'dp'), 'head'), may hold values from -0.21875 to 0.21875
- value_weight: bfloat16 [768, 768], P(('seq', 'dp'), 'head'), may hold values from -0.21875 to 0.21875
- output_weight: bfloat16 [768, 768], P('head', ('seq', 'dp')), may hold values from -1.75 to 1.75
- position_bias: bfloat16 [32, 12], P(None, 'head'), may hold values from -1 to 1
- feedforward_gain: bfloat16 [768], P(('seq', 'dp')), may hold values from 0.5 to 1.5
- router_weight: bfloat16 [768, 16], P(('seq', 'dp')), may hold values from -0.109375 to 0.109375
- expert_up: bfloat16 [16, 768, 3072], P(('seq', 'dp'), None, 'head'), may hold values from -0.21875 to 0.21875
- expert_down: bfloat16 [16, 3072, 768], P(('seq', 'dp'), 'head'), may hold values from -6 to 6
- cotangent: bfloat16 [16, 1024, 768], P('dp', 'seq'), may hold values from -6 to 6
Outputs:
- output: bfloat16 [16, 1024, 768], P('dp', 'seq')
- tokens_grad: bfloat16 [16, 1024, 768], P('dp', 'seq')
- attention_gain_grad: float32 [768], P(('seq', 'dp'))
- query_weight_grad: float32 [768, 768], P(('seq', 'dp'), 'head')
- key_weight_grad: float32 [768, 768], P(('seq', 'dp'), 'head')
- value_weight_grad: float32 [768, 768], P(('seq', 'dp'), 'head')
- output_weight_grad: float32 [768, 768], P('head', ('seq', 'dp'))
- position_bias_grad: float32 [32, 12], P(None, 'head')
- feedforward_gain_grad: float32 [768], P(('seq', 'dp'))
- router_weight_grad: float32 [768, 16], P(('seq', 'dp'))
- expert_up_grad: float32 [16, 768, 3072], P(('seq', 'dp'), None, 'head')
- expert_down_grad: float32 [16, 3072, 768], P(('seq', 'dp'), 'head')
Inputs may be any that keep to these rules, and one draw needn't show every extreme that they name: `lengths`: each group of 8 sequences on one index of dp holds one sequence of full length 1024. `expert_ids`: in each aligned block of 256 positions of one sequence, no expert is named more than 20 times.
All inputs are finite; a program needn't handle non-finite values.
Results may differ from a plain program's by a relative error of at most 0.018.
Values may be sent and summed in bfloat16 or wider, within the bound.
A program may use at most 256 MiB of HBM per device.

v0:
```python
import jax
import jax.numpy as jnp
import numpy as np
from jax import lax
from jax.sharding import PartitionSpec as P

HEAD_DIM = 64


EPS = 1e-06
bucket_edges = np.array([1, 2, 3, 4, 5, 6, 7, 8, 12, 16, 23, 32, 46, 64, 91], np.int32)


def normalize(vector, scales):
    return vector * lax.rsqrt(jnp.mean(vector * vector, axis=-1, keepdims=True) + EPS) * scales


def gelu_tanh(vector):
    return jax.nn.gelu(vector)


def buckets(query_pos, key_pos, bucket_count):
    offset = key_pos[None, :] - query_pos[:, None]
    distance = jnp.abs(offset)
    edges = jnp.asarray(bucket_edges)
    magnitude = jnp.sum((distance[..., None] >= edges).astype(jnp.int32), axis=-1)
    return magnitude + bucket_count // 2 * (offset > 0).astype(jnp.int32)


def to_experts(outgoing):
    return lax.all_to_all(outgoing, ("seq", "dp"), split_axis=0, concat_axis=0, tiled=True)


def collect_rows(partial_value, flat_index, slot_total):
    shares = lax.psum_scatter(
        partial_value.astype(jnp.float32).astype(jnp.bfloat16),
        "head",
        scatter_dimension=2,
        tiled=True,
    ).astype(jnp.float32)
    moved = lax.all_to_all(shares, ("seq", "dp"), split_axis=0, concat_axis=0, tiled=True)
    picked = moved.reshape(slot_total, -1)[flat_index]
    return lax.all_gather(picked, "head", axis=1, tiled=True)


def body(
    tokens,
    lengths,
    expert_ids,
    attention_gain,
    query_weight,
    key_weight,
    value_weight,
    output_weight,
    position_bias,
    feedforward_gain,
    router_weight,
    expert_up,
    expert_down,
    cotangent,
):
    seq_count = lax.axis_size("seq")
    dp_count = lax.axis_size("dp")
    groups = seq_count * dp_count
    local_seqs, block_size, model_width = tokens.shape
    row_count = local_seqs * block_size
    query_full, key_full, value_full, router_full, gain_first, gain_second = (
        lax.all_gather(query_weight, ("seq", "dp"), axis=0, tiled=True),
        lax.all_gather(key_weight, ("seq", "dp"), axis=0, tiled=True),
        lax.all_gather(value_weight, ("seq", "dp"), axis=0, tiled=True),
        lax.all_gather(router_weight, ("seq", "dp"), axis=0, tiled=True),
        lax.all_gather(attention_gain, ("seq", "dp"), axis=0, tiled=True),
        lax.all_gather(feedforward_gain, ("seq", "dp"), axis=0, tiled=True),
    )
    output_full = lax.all_gather(output_weight, ("seq", "dp"), axis=1, tiled=True)
    local_width = query_full.shape[1]
    heads_local = position_bias.shape[1]
    bucket_count = position_bias.shape[0]
    gain_one = gain_first.astype(jnp.float32)
    gain_two = gain_second.astype(jnp.float32)
    inputs = tokens.reshape(row_count, model_width).astype(jnp.float32)
    attn_input = normalize(inputs, gain_one).astype(jnp.bfloat16)

    def project(weight):
        made = jnp.dot(attn_input, weight, preferred_element_type=jnp.float32)
        return made.astype(jnp.bfloat16).reshape(local_seqs, block_size, heads_local, HEAD_DIM)

    queries = project(query_full)
    key_rows = project(key_full)
    value_rows = project(value_full)
    all_keys, all_values = (
        lax.all_gather(key_rows, "seq", axis=1, tiled=True),
        lax.all_gather(value_rows, "seq", axis=1, tiled=True),
    )
    seq_length = all_keys.shape[1]
    query_pos = lax.axis_index("seq") * block_size + jnp.arange(block_size, dtype=jnp.int32)
    key_pos = jnp.arange(seq_length, dtype=jnp.int32)
    bucket = buckets(query_pos, key_pos, bucket_count)
    bucket_hot = (bucket[..., None] == jnp.arange(bucket_count, dtype=jnp.int32)).astype(
        jnp.bfloat16
    )
    bias_terms = jnp.einsum(
        "qkb,bh->hqk", bucket_hot, position_bias, preferred_element_type=jnp.float32
    )
    key_valid = key_pos[None, :] < lengths[:, None]

    def score_block(query_part, key_part):
        dotted = jnp.einsum(
            "jqhd,jkhd->jhqk", query_part, key_part, preferred_element_type=jnp.float32
        )
        return jnp.where(key_valid[:, None, None, :], dotted + bias_terms[None], -1e30)

    scores = score_block(queries, all_keys)
    row_max = jnp.max(scores, axis=-1, keepdims=True)
    exponent = jnp.exp(scores - row_max)
    denominator = jnp.sum(exponent, axis=-1, keepdims=True)
    weights = exponent / denominator
    log_total = row_max + jnp.log(denominator)
    heads_out = jnp.einsum(
        "jhqk,jkhd->jqhd",
        weights.astype(jnp.bfloat16),
        all_values,
        preferred_element_type=jnp.float32,
    )
    heads_out = heads_out.astype(jnp.bfloat16).reshape(row_count, local_width)
    heads_all = lax.all_gather(heads_out, "head", axis=1, tiled=True)
    output_all = lax.all_gather(output_full, "head", axis=0, tiled=True)
    attention = jnp.dot(heads_all, output_all, preferred_element_type=jnp.float32)
    hidden = inputs + attention
    ffn_input = normalize(hidden, gain_two).astype(jnp.bfloat16)
    logits = jnp.dot(ffn_input, router_full, preferred_element_type=jnp.float32)
    router_probs = jax.nn.softmax(logits, axis=-1)
    expert_count = router_full.shape[1]
    capacity = max(2, (5 * block_size + 4 * expert_count - 1) // (4 * expert_count))
    routed = expert_ids.reshape(local_seqs, block_size)
    routed_hot = (routed[..., None] == jnp.arange(expert_count, dtype=jnp.int32)).astype(jnp.int32)
    slot_index = jnp.sum((jnp.cumsum(routed_hot, axis=1) - routed_hot) * routed_hot, axis=-1)
    seq_local = jnp.arange(local_seqs, dtype=jnp.int32)[:, None]
    flat_index = (routed * (local_seqs * capacity) + seq_local * capacity + slot_index).reshape(
        row_count
    )
    hot_float = routed_hot.reshape(row_count, expert_count).astype(jnp.float32)
    gate_values = jnp.sum(router_probs * hot_float, axis=-1)
    slot_total = expert_count * local_seqs * capacity
    exp_local = expert_up.shape[0]

    def to_slots(rows_low):
        placed = jnp.zeros((slot_total, model_width), jnp.bfloat16).at[flat_index].set(rows_low)
        return placed.reshape(groups, slot_total // groups, model_width)

    received = to_experts(to_slots(ffn_input)).reshape(groups, exp_local, -1, model_width)
    hidden_pre = jnp.einsum(
        "sxrd,xdf->sxrf", received, expert_up, preferred_element_type=jnp.float32
    )
    activated = gelu_tanh(hidden_pre).astype(jnp.bfloat16)
    partial_out = jnp.einsum(
        "sxrf,xfd->sxrd", activated, expert_down, preferred_element_type=jnp.float32
    )
    partial_out = partial_out.astype(jnp.bfloat16).reshape(groups, -1, model_width)
    token_out = collect_rows(partial_out, flat_index, slot_total)
    result = hidden + gate_values[:, None] * token_out
    output = result.astype(jnp.bfloat16).reshape(tokens.shape)
    grad_out = cotangent.reshape(row_count, model_width).astype(jnp.float32)
    gate_grad = jnp.sum(grad_out * token_out, axis=-1)
    sent_grad = (gate_values[:, None] * grad_out).astype(jnp.bfloat16)
    grad_rows = to_experts(to_slots(sent_grad)).reshape(groups, exp_local, -1, model_width)
    act_grad = jnp.einsum(
        "sxrd,xfd->sxrf", grad_rows, expert_down, preferred_element_type=jnp.float32
    )
    gelu_value, gelu_pull = jax.vjp(gelu_tanh, hidden_pre)
    pre_grad = gelu_pull(act_grad)[0].astype(jnp.bfloat16)
    down_grad = jnp.einsum(
        "sxrf,sxrd->xfd", activated, grad_rows, preferred_element_type=jnp.float32
    )
    up_grad = jnp.einsum("sxrd,sxrf->xdf", received, pre_grad, preferred_element_type=jnp.float32)
    input_part = jnp.einsum(
        "sxrf,xdf->sxrd", pre_grad, expert_up, preferred_element_type=jnp.float32
    )
    input_part = input_part.astype(jnp.bfloat16).reshape(groups, -1, model_width)
    expert_input_grad = collect_rows(input_part, flat_index, slot_total)
    logit_grad = router_probs * (
        gate_grad[:, None] * hot_float - (gate_grad * gate_values)[:, None]
    )
    logit_low = logit_grad.astype(jnp.bfloat16)
    router_grad = jnp.einsum("td,te->de", ffn_input, logit_low, preferred_element_type=jnp.float32)
    ffn_input_grad = expert_input_grad + jnp.einsum(
        "te,de->td", logit_low, router_full, preferred_element_type=jnp.float32
    )
    norm_value, norm_pull = jax.vjp(normalize, hidden, gain_two)
    hidden_norm_grad, gain_two_grad = norm_pull(ffn_input_grad)
    hidden_grad = grad_out + hidden_norm_grad
    attn_grad = hidden_grad.astype(jnp.bfloat16)
    output_grad_part = jnp.einsum(
        "tk,td->kd", heads_out, attn_grad, preferred_element_type=jnp.float32
    )
    heads_grad = jnp.einsum("td,kd->tk", attn_grad, output_full, preferred_element_type=jnp.float32)
    heads_grad = heads_grad.astype(jnp.bfloat16).reshape(
        local_seqs, block_size, heads_local, HEAD_DIM
    )
    back_keys, back_values = (all_keys, all_values)
    again_weights = jnp.exp(score_block(queries, back_keys) - log_total)
    prob_grad = jnp.einsum(
        "jqhd,jkhd->jhqk", heads_grad, back_values, preferred_element_type=jnp.float32
    )
    row_delta = jnp.sum(again_weights * prob_grad, axis=-1, keepdims=True)
    score_grad = again_weights * (prob_grad - row_delta)
    bias_term = jnp.einsum(
        "hqk,qkb->bh",
        jnp.sum(score_grad, axis=0),
        bucket_hot.astype(jnp.float32),
        precision=lax.Precision.HIGHEST,
    )
    score_low = score_grad.astype(jnp.bfloat16)
    value_grad = jnp.einsum(
        "jhqk,jqhd->jkhd",
        again_weights.astype(jnp.bfloat16),
        heads_grad,
        preferred_element_type=jnp.float32,
    )
    key_grad = jnp.einsum("jhqk,jqhd->jkhd", score_low, queries, preferred_element_type=jnp.float32)
    query_grad = jnp.einsum(
        "jhqk,jkhd->jqhd", score_low, back_keys, preferred_element_type=jnp.float32
    )
    query_grad = query_grad.astype(jnp.bfloat16).reshape(row_count, local_width)
    key_own, value_own = (
        lax.psum_scatter(key_grad, "seq", scatter_dimension=1, tiled=True),
        lax.psum_scatter(value_grad, "seq", scatter_dimension=1, tiled=True),
    )
    key_low = key_own.astype(jnp.bfloat16).reshape(row_count, local_width)
    value_low = value_own.astype(jnp.bfloat16).reshape(row_count, local_width)
    query_w_grad = jnp.einsum(
        "td,tk->dk", attn_input, query_grad, preferred_element_type=jnp.float32
    )
    key_w_grad = jnp.einsum("td,tk->dk", attn_input, key_low, preferred_element_type=jnp.float32)
    value_w_grad = jnp.einsum(
        "td,tk->dk", attn_input, value_low, preferred_element_type=jnp.float32
    )
    input_part_one = jnp.einsum(
        "tk,dk->td", query_grad, query_full, preferred_element_type=jnp.float32
    )
    input_part_one = input_part_one + jnp.einsum(
        "tk,dk->td", key_low, key_full, preferred_element_type=jnp.float32
    )
    input_part_one = input_part_one + jnp.einsum(
        "tk,dk->td", value_low, value_full, preferred_element_type=jnp.float32
    )
    attn_input_grad = lax.psum(input_part_one, "head")
    first_value, first_pull = jax.vjp(normalize, inputs, gain_one)
    input_norm_grad, gain_one_grad = first_pull(attn_input_grad)
    tokens_grad = (hidden_grad + input_norm_grad).astype(jnp.bfloat16).reshape(tokens.shape)
    query_share, key_share, value_share, router_share, gain_one_share, gain_two_share = (
        lax.psum_scatter(query_w_grad, ("seq", "dp"), scatter_dimension=0, tiled=True),
        lax.psum_scatter(key_w_grad, ("seq", "dp"), scatter_dimension=0, tiled=True),
        lax.psum_scatter(value_w_grad, ("seq", "dp"), scatter_dimension=0, tiled=True),
        lax.psum_scatter(router_grad, ("seq", "dp"), scatter_dimension=0, tiled=True),
        lax.psum_scatter(gain_one_grad, ("seq", "dp"), scatter_dimension=0, tiled=True),
        lax.psum_scatter(gain_two_grad, ("seq", "dp"), scatter_dimension=0, tiled=True),
    )
    output_share = lax.psum_scatter(
        output_grad_part, ("seq", "dp"), scatter_dimension=1, tiled=True
    )
    bias_total = lax.psum(bias_term, ("seq", "dp"))
    return (
        output,
        tokens_grad,
        gain_one_share,
        query_share,
        key_share,
        value_share,
        output_share,
        bias_total,
        gain_two_share,
        router_share,
        up_grad,
        down_grad,
    )


def solution(mesh):
    placed = (
        P("dp", "seq", None),
        P("dp"),
        P("dp", "seq", None),
        P(("seq", "dp")),
        P(("seq", "dp"), "head"),
        P(("seq", "dp"), "head"),
        P(("seq", "dp"), "head"),
        P("head", ("seq", "dp")),
        P(None, "head"),
        P(("seq", "dp")),
        P(("seq", "dp"), None),
        P(("seq", "dp"), None, "head"),
        P(("seq", "dp"), "head", None),
        P("dp", "seq", None),
    )
    return jax.shard_map(
        body,
        mesh=mesh,
        in_specs=placed,
        out_specs=(
            P("dp", "seq", None),
            P("dp", "seq", None),
            P(("seq", "dp")),
            P(("seq", "dp"), "head"),
            P(("seq", "dp"), "head"),
            P(("seq", "dp"), "head"),
            P("head", ("seq", "dp")),
            P(None, "head"),
            P(("seq", "dp")),
            P(("seq", "dp"), None),
            P(("seq", "dp"), None, "head"),
            P(("seq", "dp"), "head", None),
        ),
        check_vma=False,
    )
```

profile of v0, /device:TPU:0, one launch (start us, length us, event | category | flops | bytes accessed | tf_op | source)
XLA Modules:
  0.0 1501.6 jit_solution(2024270781747800338)
XLA Ops:
  11.0 23.1 %all-reduce.5 = (bf16[768]{0:T(1024)(128)(2,1)S(1)}, bf16[768]{0:T(1024)(128)(2,1)S(1)}) all-reduce(bf16[768]{0:T(1024)(128)(2,1)S(1)} %dynamic-update-slice, bf16[768]{0:T(1024)(128)(2,1)S(1)} %dynamic-update-slice.1), channel_id=1, replica_groups=mesh['head'=4,'seq'=4,'dp'=2] {'seq','dp'}, use_global_device_ids=true, to_apply=%add | all-reduce | flops 1536 | bytes 6144
  37.9 31.2 %all_gather.43 = bf16[768,192]{1,0:T(8,128)(2,1)S(1)} all-gather(bf16[96,192]{1,0:T(8,128)(2,1)} %param.20), channel_id=1, replica_groups=mesh['head'=4,'seq'=4,'dp'=2] {'seq','dp'}, dimensions={0}, use_global_device_ids=true | all-gather | bytes 331776 | tf_op jit(solution)/shard_map/all_gather | solution.py:69
  76.2 34.7 %all_gather.40 = bf16[768,192]{1,0:T(8,128)(2,1)S(1)} all-gather(bf16[96,192]{1,0:T(8,128)(2,1)S(1)} %copy-done.27), channel_id=1, replica_groups=mesh['head'=4,'seq'=4,'dp'=2] {'seq','dp'}, dimensions={0}, use_global_device_ids=true | all-gather | bytes 331776 | tf_op jit(solution)/shard_map/all_gather | solution.py:70
  116.2 32.1 %all_gather.46 = bf16[192,768]{0,1:T(8,128)(2,1)S(1)} all-gather(bf16[192,96]{0,1:T(8,128)(2,1)S(1)} %copy.139), channel_id=1, replica_groups=mesh['head'=4,'seq'=4,'dp'=2] {'seq','dp'}, dimensions={1}, use_global_device_ids=true | all-gather | bytes 331776 | tf_op jit(solution)/shard_map/all_gather | solution.py:75
  149.4 34.5 %all_gather.42 = bf16[768,192]{1,0:T(8,128)(2,1)} all-gather(bf16[96,192]{1,0:T(8,128)(2,1)S(1)} %copy-done.28), channel_id=1, replica_groups=mesh['head'=4,'seq'=4,'dp'=2] {'seq','dp'}, dimensions={0}, use_global_device_ids=true | all-gather | bytes 331776 | tf_op jit(solution)/shard_map/all_gather | solution.py:68
  190.6 9.0 iota_compare_fusion
  199.7 46.2 %copy.136 = pred[256,1024,32]{1,2,0:T(32,128)(4,1)} copy(pred[256,1024,32]{0,2,1:T(32,128)(4,1)} %iota_compare_fusion) | data formatting | bytes 16777216 | tf_op jit(solution)/shard_map/eq | solution.py:99
  245.9 9.3 convolution_bitcast_fusion.1
  255.2 5.7 copy.137
  260.9 13.3 fusion.89
  274.1 10.9 fusion
  285.1 11.7 fusion.65
  303.7 25.0 %all-gather.14.cloned.1.call-done = bf16[2048,768]{0,1:T(8,128)(2,1)} async-done(((bf16[2048,192]{0,1:T(8,128)(2,1)}), bf16[2048,768]{0,1:T(8,128)(2,1)}) %all-gather.14.cloned.1.call-update) | async-done | bytes 3145744 | tf_op jit(solution)/shard_map/all_gather | solution.py:126
  328.6 8.8 multiply_reduce_fusion.3
  337.4 13.9 scatter_custom_fusion
  351.3 5.6 all-to-all-start
  356.9 107.9 %all-gather.2 = bf16[8,96,16]{1,2,0:T(8,128)(2,1)S(1)} all-gather(bf16[1,96,16]{1,2,0:T(8,128)(2,1)S(1)} %bitcast.277), channel_id=1, replica_groups=mesh['head'=4,'seq'=4,'dp'=2] {'seq','dp'}, dimensions={0}, use_global_device_ids=true | all-gather | bytes 27648 | tf_op jit(solution)/shard_map/all_gather | solution.py:71
  471.0 13.3 scatter_custom_fusion.1
  489.4 6.1 fusion.33
  502.7 6.8 copy.147
  509.6 62.0 %all-to-all-done.2 = bf16[8,320,768]{2,1,0:T(8,128)(2,1)} async-done(((bf16[8,320,768]{2,1,0:T(8,128)(2,1)}), bf16[8,320,768]{2,1,0:T(8,128)(2,1)}, u32[]{:S(2)}, u32[]{:S(2)}) %all-to-all-start.2) | async-done | bytes 3932192 | tf_op jit(solution)/shard_map/all_to_all | solution.py:31
  571.6 11.2 fusion.12
  588.4 6.8 copy.154
  601.8 53.8 %all-to-all-done.1 = f32[8,320,192]{1,2,0:T(8,128)S(1)} async-done(((f32[8,320,192]{1,2,0:T(8,128)}), f32[8,320,192]{1,2,0:T(8,128)S(1)}, u32[]{:S(2)}, u32[]{:S(2)}) %all-to-all-start.1) | async-done | bytes 1966112 | tf_op jit(solution)/shard_map/all_to_all | solution.py:41
  657.7 8.4 gather_fusion
  669.3 57.7 %all_to_all.20 = f32[8,320,192]{1,2,0:T(8,128)} all-to-all(f32[8,320,192]{1,2,0:T(8,128)S(1)} %copy.155), channel_id=1, replica_groups=mesh['head'=4,'seq'=4,'dp'=2] {'seq','dp'}, dimensions={0} | all-to-all | bytes 3932160 | tf_op jit(solution)/shard_map/all_to_all | solution.py:41
  730.3 8.4 gather_fusion.1
  740.5 6.8 copy.151
  752.7 32.4 %all-gather.20.cloned.1.call-done = f32[2048,768]{0,1:T(8,128)} async-done(((f32[2048,192]{0,1:T(8,128)}), f32[2048,768]{0,1:T(8,128)}) %all-gather.20.cloned.1.call-update) | async-done | bytes 6291472 | tf_op jit(solution)/shard_map/all_gather | solution.py:43
  785.0 6.6 copy.159
  791.7 6.0 multiply_reduce_fusion.1
  797.7 7.0 convert_add_fusion
  808.8 13.0 fusion.41
  821.9 19.5 %multiply_reduce_fusion = (f32[8,3,256]{2,1,0:T(4,128)S(1)}, f32[8,3,256,1024]{3,2,1,0:T(8,128)}) fusion(f32[8,3,256,1024]{3,2,1,0:T(8,128)} %get-tuple-element.30, f32[8,3,256]{2,1,0:T(4,128)S(1)} %log_add_fusion, bf16[8,1024,3,64]{1,3,2,0:T(8,128)(2,1)} %all-gather.10.cloned.1.call-done, bf16[8,256,3,64]{1,0,3,2:T(8,128)(2,1)S(1)} %bitcast.236), kind=kOutput, calls=%fused_computation.6 | convolution fusion | flops 824174592 | bytes 54312960 | tf_op jit(solution)/shard_map/jqhd,jkhd->jhqk/dot_general | solution.py:202
  841.4 18.7 %fusion.17 = (f32[3,256,1024]{2,1,0:T(8,128)}, bf16[8,3,256,1024]{3,2,1,0:T(8,128)(2,1)S(1)}) fusion(f32[8,3,256,1024]{3,2,1,0:T(8,128)} %get-tuple-element.37, f32[8,3,256]{2,1,0:T(4,128)S(1)} %get-tuple-element.36, f32[8,3,256,1024]{3,2,1,0:T(8,128)} %get-tuple-element.30, f32[8,3,256]{2,1,0:T(4,128)S(1)} %log_add_fusion), kind=kLoop, calls=%fused_computation.38 | loop fusion | flops 30670848 | bytes 66109440 | tf_op jit(solution)/shard_map/reduce_sum | solution.py:209
  874.1 9.5 fusion.61
  893.1 39.7 %reduce-scatter.20.cloned.1.call-done = f32[8,256,3,64]{1,3,2,0:T(8,128)} async-done(((f32[8,1024,3,64]{1,3,2,0:T(8,128)}), f32[8,256,3,64]{1,3,2,0:T(8,128)}) %reduce-scatter.20.cloned.1.call-update) | async-done | bytes 1572880 | tf_op jit(solution)/shard_map/reduce_scatter | solution.py:227
  934.9 111.3 %reduce-scatter.18.cloned.1.call-done = f32[8,256,3,64]{1,3,2,0:T(8,128)} async-done(((f32[8,1024,3,64]{1,3,2,0:T(8,128)}), f32[8,256,3,64]{1,3,2,0:T(8,128)}) %reduce-scatter.18.cloned.1.call-update) | async-done | bytes 1572880 | tf_op jit(solution)/shard_map/reduce_scatter | solution.py:226
  1062.5 11.6 fusion.48
  1076.2 8.8 fusion.51
  1090.4 17.6 %convolution_bitcast_fusion.2 = f32[32,3]{0,1:T(4,128)S(1)} fusion(f32[3,256,1024]{1,0,2:T(4,128)} %copy.166, s32[256,1024]{0,1:T(8,128)S(1)} %copy-done.10), kind=kOutput, calls=%fused_computation.100 | convolution fusion | flops 310378496 | bytes 4194688 | tf_op jit(solution)/shard_map/hqk,qkb->bh/dot_general | solution.py:207
  1112.9 63.3 %reduce-scatter.28.cloned.1.call-done = f32[96,192]{1,0:T(8,128)} async-done(((f32[768,192]{1,0:T(8,128)}), f32[96,192]{1,0:T(8,128)}) %reduce-scatter.28.cloned.1.call-update) | async-done | bytes 73744
  1181.7 115.5 %all-reduce.8.cloned.1.call-done = f32[2048,768]{1,0:T(8,128)} async-done(((f32[2048,768]{1,0:T(8,128)}), f32[2048,768]{1,0:T(8,128)}) %all-reduce.8.cloned.1.call-update) | async-done | bytes 6291472 | tf_op jit(solution)/shard_map/psum | solution.py:247
  1302.1 37.1 %all-reduce.4 = (f32[768]{0:T(1024)S(1)}, f32[32,3]{0,1:T(4,128)}, f32[768]{0:T(1024)S(1)}) all-reduce(f32[768]{0:T(1024)S(1)} %get-tuple-element.14, f32[32,3]{0,1:T(4,128)S(1)} %convolution_bitcast_fusion.2, f32[768]{0:T(1024)S(1)} %get-tuple-element.12), channel_id=8, replica_groups=mesh['head'=4,'seq'=4,'dp'=2] {'seq','dp'}, use_global_device_ids=true, to_apply=%region_23.24.clone | all-reduce | flops 1632 | bytes 13056
  1340.4 8.3 fusion.20
  1348.6 15.4 %reduce-scatter.22.cloned.1.call-done = f32[96,192]{1,0:T(8,128)} async-done(((f32[768,192]{1,0:T(8,128)}), f32[96,192]{1,0:T(8,128)}) %reduce-scatter.22.cloned.1.call-update) | async-done | bytes 73744 | tf_op jit(solution)/shard_map/reduce_scatter | solution.py:252
  1364.0 65.1 %reduce-scatter.26.cloned.1.call-done = f32[96,192]{1,0:T(8,128)} async-done(((f32[768,192]{1,0:T(8,128)}), f32[96,192]{1,0:T(8,128)}) %reduce-scatter.26.cloned.1.call-update) | async-done | bytes 73744 | tf_op jit(solution)/shard_map/reduce_scatter | solution.py:254
  1429.1 65.7 %reduce-scatter.24.cloned.1.call-done = f32[96,192]{1,0:T(8,128)} async-done(((f32[768,192]{1,0:T(8,128)}), f32[96,192]{1,0:T(8,128)}) %reduce-scatter.24.cloned.1.call-update) | async-done | bytes 73744 | tf_op jit(solution)/shard_map/reduce_scatter | solution.py:253
  (217 shorter events, 149.0 us)
Async XLA Ops:
  7.2 488.3 %copy-start = (bf16[2,768,768]{2,1,0:T(8,128)(2,1)S(1)}, bf16[2,768,768]{2,1,0:T(8,128)(2,1)}, u32[]{:S(2)}) copy-start(bf16[2,768,768]{2,1,0:T(8,128)(2,1)} %param.27) | copy-start | bytes 7077892
  7.2 253.7 %all-gather.12.cloned.1.call-start = ((), (), s32[]{:S(2)}) async-start(), calls=%async_computation.14 | async-start | bytes 3932160 | tf_op jit(solution)/shard_map/all_gather | solution.py:92
  34.1 40.7 %copy-start.23 = (f32[768]{0:T(1024)}, f32[768]{0:T(1024)S(1)}, u32[]{:S(2)}) copy-start(f32[768]{0:T(1024)S(1)} %convert_element_type.141) | copy-start | bytes 9220
  37.9 37.1 %copy-start.21 = (f32[2048]{0:T(1024)}, f32[2048]{0:T(1024)S(1)}, u32[]{:S(2)}) copy-start(f32[2048]{0:T(1024)S(1)} %rsqrt.25) | copy-start | bytes 24580
  69.1 5.7 copy-start.11
  69.1 7.1 copy-start.27
  74.8 41.2 %copy-start.29 = (bf16[192,96]{1,0:T(8,128)(2,1)S(1)}, bf16[192,96]{1,0:T(8,128)(2,1)}, u32[]{:S(2)}) copy-start(bf16[192,96]{1,0:T(8,128)(2,1)} %param.22) | copy-start | bytes 110596
  75.0 74.2 %copy-start.34 = (s32[8]{0:T(128)S(1)}, s32[8]{0:T(128)}, u32[]{:S(2)}) copy-start(s32[8]{0:T(128)} %param.16) | copy-start | bytes 100
  75.0 74.3 %copy-start.28 = (bf16[96,192]{1,0:T(8,128)(2,1)S(1)}, bf16[96,192]{1,0:T(8,128)(2,1)}, u32[]{:S(2)}) copy-start(bf16[96,192]{1,0:T(8,128)(2,1)} %param.19) | copy-start | bytes 110596
  76.1 108.0 %copy-start.33 = (s32[15]{0:T(128)S(1)}, s32[15]{0:T(128)}, u32[]{:S(2)}) copy-start(s32[15]{0:T(128)} %constant.58.clone) | copy-start | bytes 184
  76.1 208.9 %all-gather.10.cloned.1.call-start = ((), (), s32[]{:S(2)}) async-start(), calls=%async_computation.13 | async-start | bytes 3932160 | tf_op jit(solution)/shard_map/all_gather | solution.py:93
  116.0 187.6 %all-gather.16.cloned.1.call-start = ((), (), s32[]{:S(2)}) async-start(), calls=%async_computation.16 | async-start | bytes 1474560 | tf_op jit(solution)/shard_map/all_gather | solution.py:127
  148.3 35.8 %copy-start.14 = (bf16[192,768]{0,1:T(8,128)(2,1)}, bf16[192,768]{0,1:T(8,128)(2,1)S(1)}, u32[]{:S(2)}) copy-start(bf16[192,768]{0,1:T(8,128)(2,1)S(1)} %all_gather.46) | copy-start | bytes 884740
  149.2 179.4 %all-gather.14.cloned.1.call-start = ((), (), s32[]{:S(2)}) async-start(), calls=%async_computation.15 | async-start | bytes 3932160 | tf_op jit(solution)/shard_map/all_gather | solution.py:126
  190.6 70.3 %copy-start.7 = (bf16[24,8,8,256]{3,2,1,0:T(8,128)(2,1)}, bf16[24,8,8,256]{3,2,1,0:T(8,128)(2,1)S(1)}, u32[]{:S(2)}) copy-start(bf16[24,8,8,256]{3,2,1,0:T(8,128)(2,1)S(1)} %copy.180) | copy-start | bytes 2359300
  199.7 46.2 %copy-start.32 = (bf16[32,3]{0,1:T(4,128)(2,1)S(1)}, bf16[32,3]{0,1:T(4,128)(2,1)}, u32[]{:S(2)}) copy-start(bf16[32,3]{0,1:T(4,128)(2,1)} %param.23) | copy-start | bytes 580
  285.1 13.4 copy-start.20
  351.3 5.7 copy-start.31
  351.3 133.1 %all-to-all-start = ((bf16[8,320,768]{2,1,0:T(8,128)(2,1)}), bf16[8,320,768]{2,1,0:T(8,128)(2,1)}, u32[]{:S(2)}, u32[]{:S(2)}) async-start(bf16[8,320,768]{2,1,0:T(8,128)(2,1)} %bitcast.232), calls=%async_computation | async-start | bytes 7864320 | tf_op jit(solution)/shard_map/all_to_all | solution.py:31
  484.4 87.2 %all-to-all-start.2 = ((bf16[8,320,768]{2,1,0:T(8,128)(2,1)}), bf16[8,320,768]{2,1,0:T(8,128)(2,1)}, u32[]{:S(2)}, u32[]{:S(2)}) async-start(bf16[8,320,768]{2,1,0:T(8,128)(2,1)} %bitcast.231), calls=%async_computation.3 | async-start | bytes 7864320 | tf_op jit(solution)/shard_map/all_to_all | solution.py:31
  488.9 106.4 %reduce-scatter.14.cloned.1.call-start = ((), (), s32[]{:S(2)}) async-start(), calls=%async_computation.17 | async-start | bytes 5898240 | tf_op jit(solution)/shard_map/reduce_scatter | solution.py:35
  495.5 5.0 copy-start.36
  509.5 158.4 %reduce-scatter.16.cloned.1.call-start = ((), (), s32[]{:S(2)}) async-start(), calls=%async_computation.18 | async-start | bytes 5898240 | tf_op jit(solution)/shard_map/reduce_scatter | solution.py:35
  571.6 11.2 copy-start.35
  582.8 3.5 copy-start.37
  598.1 57.5 %all-to-all-start.1 = ((f32[8,320,192]{1,2,0:T(8,128)}), f32[8,320,192]{1,2,0:T(8,128)S(1)}, u32[]{:S(2)}, u32[]{:S(2)}) async-start(f32[8,320,192]{1,2,0:T(8,128)} %copy.148), calls=%async_computation.2 | async-start | bytes 4718592 | tf_op jit(solution)/shard_map/all_to_all | solution.py:41
  601.7 138.7 %all-gather.18.cloned.1.call-start = ((), (), s32[]{:S(2)}) async-start(), calls=%async_computation.25 | async-start | bytes 7864320 | tf_op jit(solution)/shard_map/all_gather | solution.py:43
  667.8 117.2 %all-gather.20.cloned.1.call-start = ((), (), s32[]{:S(2)}) async-start(), calls=%async_computation.26 | async-start | bytes 7864320 | tf_op jit(solution)/shard_map/all_gather | solution.py:43
  740.4 192.4 %reduce-scatter.20.cloned.1.call-start = ((), (), s32[]{:S(2)}) async-start(), calls=%async_computation.20 | async-start | bytes 7864320 | tf_op jit(solution)/shard_map/reduce_scatter | solution.py:227
  791.7 6.0 copy-start.6
  797.7 9.7 copy-start.15
  821.9 224.4 %reduce-scatter.18.cloned.1.call-start = ((), (), s32[]{:S(2)}) async-start(), calls=%async_computation.19 | async-start | bytes 7864320 | tf_op jit(solution)/shard_map/reduce_scatter | solution.py:226
  841.4 23.2 %copy-start.8 = (bf16[24,8,8,256]{3,2,1,0:T(8,128)(2,1)S(1)}, bf16[24,8,8,256]{3,2,1,0:T(8,128)(2,1)}, u32[]{:S(2)}) copy-start(bf16[24,8,8,256]{3,2,1,0:T(8,128)(2,1)} %copy-done.7) | copy-start | bytes 2359300
  860.1 4.5 copy-start.2
  869.6 241.9 %reduce-scatter.30.cloned.1.call-start = ((), (), s32[]{:S(2)}) async-start(), calls=%async_computation.28 | async-start | bytes 442368
  873.7 9.9 copy-start.9
  873.7 302.5 %reduce-scatter.28.cloned.1.call-start = ((), (), s32[]{:S(2)}) async-start(), calls=%async_computation.27 | async-start | bytes 884736
  883.6 5.8 copy-start.13
  889.3 407.9 %all-reduce.8.cloned.1.call-start = ((), (), s32[]{:S(2)}) async-start(), calls=%async_computation.21 | async-start | bytes 12582912 | tf_op jit(solution)/shard_map/psum | solution.py:247
  893.1 155.4 %copy-start.12 = (bf16[768,192]{1,0:T(8,128)(2,1)S(1)}, bf16[768,192]{1,0:T(8,128)(2,1)}, u32[]{:S(2)}) copy-start(bf16[768,192]{1,0:T(8,128)(2,1)} %copy-done.11) | copy-start | bytes 884740
  1055.3 308.8 %reduce-scatter.22.cloned.1.call-start = ((), (), s32[]{:S(2)}) async-start(), calls=%async_computation.22 | async-start | bytes 884736 | tf_op jit(solution)/shard_map/reduce_scatter | solution.py:252
  1062.3 366.8 %reduce-scatter.26.cloned.1.call-start = ((), (), s32[]{:S(2)}) async-start(), calls=%async_computation.24 | async-start | bytes 884736 | tf_op jit(solution)/shard_map/reduce_scatter | solution.py:254
  1062.5 11.7 copy-start.19
  1076.1 418.7 %reduce-scatter.24.cloned.1.call-start = ((), (), s32[]{:S(2)}) async-start(), calls=%async_computation.23 | async-start | bytes 884736 | tf_op jit(solution)/shard_map/reduce_scatter | solution.py:253
  1085.0 5.3 copy-start.10
  1090.3 206.9 %copy-start.22 = (f32[2048]{0:T(1024)S(1)}, f32[2048]{0:T(1024)}, u32[]{:S(2)}) copy-start(f32[2048]{0:T(1024)} %copy-done.21) | copy-start | bytes 24580
  1181.7 158.7 %copy-start.26 = (f32[1,2,8,128]{3,1,2,0:T(2,128)S(1)}, f32[1,2,8,128]{3,1,2,0:T(2,128)}, u32[]{:S(2)}) copy-start(f32[1,2,8,128]{3,1,2,0:T(2,128)} %copy-done.25) | copy-start | bytes 24580
  1340.4 154.4 %copy-start.1 = (bf16[2,768,768]{2,1,0:T(8,128)(2,1)S(1)}, bf16[2,768,768]{2,1,0:T(8,128)(2,1)}, u32[]{:S(2)}) copy-start(bf16[2,768,768]{2,1,0:T(8,128)(2,1)} %param.27) | copy-start | bytes 7077892
  (11 other events, 17.9 us)
Sparse Core Ops, SparseCore 0:
  76.3 65.5 all-gather.11
  144.0 66.0 all-gather.9
  211.7 15.7 all-gather.15
  298.5 30.0 all-gather.13
  509.6 48.1 reduce-scatter.13
  595.4 45.7 reduce-scatter.15
  667.9 44.4 all-gather.17
  740.5 44.5 all-gather.19
  822.0 110.7 reduce-scatter.19
  934.9 111.2 reduce-scatter.17
  1049.5 61.8 reduce-scatter.29
  1114.6 61.5 reduce-scatter.27
  1178.7 118.5 all-reduce.7
  1301.3 62.6 reduce-scatter.21
  1367.7 61.3 reduce-scatter.25
  1433.2 61.5 reduce-scatter.23
where the time goes:
time: 1510 us; the launch traced here: 1500 us
  waiting for transfers between devices  653 us (43%)
  blocking collectives  358 us (24%)
  matrix products  195 us (13%)
  local copies, waits for them, and re-layouts  150 us (10%)
  other arithmetic  113 us (7%)
  between operations  16.3 us (1%)
  starting transfers between devices  15.5 us (1%)
    psum x1, waiting for transfers between devices, body(): attn_input_grad = lax.psum(input_part_one, 'head')  116 us
    reduce_scatter x1, waiting for transfers between devices, body(): lax.psum_scatter(key_grad, 'seq', scatter_dimension=1, tiled=True)  111 us
    all_gather x1, blocking collectives, body(): lax.all_gather(router_weight, ('seq', 'dp'), axis=0, tiled=True)  108 us
    unnamed x18, waiting for transfers between devices  67 us
    reduce_scatter x1, waiting for transfers between devices, body(): lax.psum_scatter(key_w_grad, ('seq', 'dp'), scatter_dimension=0, tiled=True)  65.7 us
    reduce_scatter x1, waiting for transfers between devices, body(): lax.psum_scatter(value_w_grad, ('seq', 'dp'), scatter_dimension=0, tiled=...  65.1 us
    all_to_all x2, waiting for transfers between devices, to_experts(): lax.all_to_all(outgoing, ('seq', 'dp'), split_axis=0, concat_axis=0, tile...  62 us
    unnamed x2, blocking collectives  60.2 us
  transfers between devices with their start and end apart: 19, of which 12 were waited for; matrix products, arithmetic and copies ran while one was open for 25% of the time, Pallas kernels for 0%

commit v1 on v0

v1 whole, which is shorter than its diff:
```python
import functools

import jax
import jax.numpy as jnp
import numpy as np
from jax import lax
from jax.experimental import pallas as pl
from jax.experimental.pallas import tpu as pltpu
from jax.sharding import PartitionSpec as P

HEAD_DIM = 64
EPS = 1e-06
bucket_edges = np.array([1, 2, 3, 4, 5, 6, 7, 8, 12, 16, 23, 32, 46, 64, 91], np.int32)
ANY = pl.BlockSpec(memory_space=pl.ANY)
VMEM = pl.BlockSpec(memory_space=pltpu.VMEM)
MESH = pl.DeviceIdType.MESH
DMA = pltpu.SemaphoreType.DMA
F32 = jnp.float32
BF16 = jnp.bfloat16


def normalize(vector, scales):
    return vector * lax.rsqrt(jnp.mean(vector * vector, axis=-1, keepdims=True) + EPS) * scales


def gelu_tanh(vector):
    return jax.nn.gelu(vector)


def bucket_of(offset, bucket_count):
    distance = jnp.abs(offset)
    magnitude = jnp.zeros_like(offset)
    for edge in bucket_edges:
        magnitude = magnitude + (distance >= int(edge)).astype(jnp.int32)
    return magnitude + bucket_count // 2 * (offset > 0).astype(jnp.int32)


def send(src, dst, send_sem, recv_sem, **device):
    copy = pltpu.make_async_remote_copy(
        src_ref=src,
        dst_ref=dst,
        send_sem=send_sem,
        recv_sem=recv_sem,
        device_id=device,
        device_id_type=MESH,
    )
    copy.start()
    return copy


def arrived(ref, recv_sem):
    pltpu.make_async_copy(ref, ref, recv_sem).wait()


def greet(devices):
    barrier = pltpu.get_barrier_semaphore()
    for device in devices:
        pl.semaphore_signal(barrier, inc=1, device_id=device, device_id_type=MESH)
    pl.semaphore_wait(barrier, len(devices))


def mod(value, size):
    return lax.rem(value + 2 * size, size)


class Place:
    def __init__(self, seqs, dps):
        self.h, self.s, self.d = lax.axis_index("head"), lax.axis_index("seq"), lax.axis_index("dp")
        self.seqs, self.dps = seqs, dps
        self.near = lax.rem(self.h, 2) * -2 + self.h + 1
        self.across = mod(self.h + 2, 4)
        self.near_across = lax.rem(self.across, 2) * -2 + self.across + 1

    def seq_peers(self):
        return [{"seq": mod(self.s + i, self.seqs)} for i in range(1, self.seqs)]

    def dp_peers(self):
        return [{"dp": mod(self.d + i, self.dps)} for i in range(1, self.dps)]

    def head_pair(self):
        return [{"head": self.near}, {"head": self.across}]

    def group_peers(self):
        return [
            {"seq": mod(self.s + i, self.seqs), "dp": mod(self.d + j, self.dps)}
            for i in range(self.seqs)
            for j in range(self.dps)
            if i or j
        ]

    def block(self, j, h=None):
        return mod((self.h if h is None else h) + 2 * j, 4)


def params(**more):
    return pltpu.CompilerParams(has_side_effects=True, vmem_limit_bytes=56 * 2**20, **more)


def line_gather(me, own, whole, sems, slot):
    (hop_send, hop_recv, dp_send, dp_recv) = sems
    s, d, count = me.s, me.d, me.seqs

    def spread(src, source):
        for i in range(1, me.dps):
            send(
                src,
                whole.at[source, d],
                dp_send.at[i - 1, source],
                dp_recv.at[i - 1, source],
                dp=mod(d + i, me.dps),
            )

    def spread_wait(source):
        for i in range(1, me.dps):
            here = whole.at[source, mod(d - i, me.dps)]
            arrived(here, dp_recv.at[i - 1, source])
            pltpu.make_async_copy(here, here, dp_send.at[i - 1, source]).wait()

    def start():
        @pl.when(s < count - 1)
        def _():
            send(own, whole.at[s, d], hop_send.at[0, s], hop_recv.at[s], seq=s + 1)

        @pl.when(s > 0)
        def _():
            send(own, whole.at[s, d], hop_send.at[1, s], hop_recv.at[s], seq=s - 1)

        spread(own, s)

    def step(t):
        @pl.when(s - t >= 0)
        def _():
            source = s - t
            here = whole.at[source, d]
            arrived(here, hop_recv.at[source])

            @pl.when(s < count - 1)
            def _():
                send(here, here, hop_send.at[0, source], hop_recv.at[source], seq=s + 1)

            spread(here, source)

        @pl.when(s + t < count)
        def _():
            source = s + t
            here = whole.at[source, d]
            arrived(here, hop_recv.at[source])

            @pl.when(s > 0)
            def _():
                send(here, here, hop_send.at[1, source], hop_recv.at[source], seq=s - 1)

            spread(here, source)

    def finish():
        for source in range(count):
            spread_wait(source)
            here = whole.at[source, d]

            @pl.when((s < count - 1) & (source <= s))
            def _():
                pltpu.make_async_copy(here, here, hop_send.at[0, source]).wait()

            @pl.when((s > 0) & (source >= s))
            def _():
                pltpu.make_async_copy(here, here, hop_send.at[1, source]).wait()

    return start, step, finish


def line_sems(seqs, dps):
    return [
        DMA((2, seqs)),
        DMA((seqs,)),
        DMA((max(1, dps - 1), seqs)),
        DMA((max(1, dps - 1), seqs)),
    ]


CHUNKS = 2


def gather_kernel(
    seqs, dps, tok, pack, ids, tok_all, pack_all, ids_all, ls, z_send, z_recv, h_send, h_recv, i_send, i_recv, *sems
):
    me = Place(seqs, dps)
    h, s, d = me.h, me.s, me.d
    per = tok.shape[0] // seqs
    rows = tok.shape[1] // CHUNKS
    own_copies = [pltpu.make_async_copy(tok.at[per * s + j], tok_all.at[j, s], ls.at[j]) for j in range(per)]
    own_copies.append(pltpu.make_async_copy(pack, pack_all.at[s, d], ls.at[per]))
    own_copies.append(pltpu.make_async_copy(ids, ids_all.at[s], ls.at[per + 1]))
    for copy in own_copies:
        copy.start()
    greet(me.seq_peers() + me.dp_peers() + me.head_pair())
    start, step, finish = line_gather(me, pack, pack_all, sems, 0)
    start()
    turn = mod(h - s, 4)
    mine = lax.rem(turn, 2) == 0
    which = lax.div(turn, 2)
    for i in range(1, seqs):
        to = mod(s + i, seqs)
        send(ids, ids_all.at[s], i_send.at[i - 1], i_recv.at[i - 1], seq=to)

    @pl.when(mine)
    def _():
        for c in range(CHUNKS):
            for i in range(1, seqs):
                to = mod(s + i, seqs)
                part = pl.ds(c * rows, rows)
                send(
                    tok.at[per * to + which, part],
                    tok_all.at[which, s, part],
                    z_send.at[i - 1, c],
                    z_recv.at[which, c],
                    seq=to,
                )

    def at(j, c, head):
        return tok_all.at[j, me.block(j, head), pl.ds(c * rows, rows)]

    for t in range(1, seqs):
        step(t)
    for c in range(CHUNKS):
        for j in range(per):
            here = at(j, c, h)

            @pl.when(me.block(j) != s)
            def _():
                arrived(here, z_recv.at[j, c])
                send(here, here, h_send.at[0, j, c], h_recv.at[0, j, c], head=me.across)
                send(here, here, h_send.at[1, j, c], h_recv.at[1, j, c], head=me.near)

    for c in range(CHUNKS):
        for j in range(per):
            there = at(j, c, me.across)

            @pl.when(me.block(j, me.across) != s)
            def _():
                arrived(there, h_recv.at[0, j, c])
                send(there, there, h_send.at[2, j, c], h_recv.at[2, j, c], head=me.near)

    for c in range(CHUNKS):
        for j in range(per):
            here = at(j, c, h)

            @pl.when(me.block(j) != s)
            def _():
                for k in range(2):
                    pltpu.make_async_copy(here, here, h_send.at[k, j, c]).wait()

            @pl.when(me.block(j, me.across) != s)
            def _():
                pltpu.make_async_copy(here, here, h_send.at[2, j, c]).wait()

            @pl.when(me.block(j, me.near) != s)
            def _():
                arrived(at(j, c, me.near), h_recv.at[1, j, c])

            @pl.when(me.block(j, me.near_across) != s)
            def _():
                arrived(at(j, c, me.near_across), h_recv.at[2, j, c])

    for i in range(1, seqs):
        arrived(ids_all.at[mod(s - i, seqs)], i_recv.at[i - 1])
        pltpu.make_async_copy(ids, ids, i_send.at[i - 1]).wait()

    @pl.when(mine)
    def _():
        for c in range(CHUNKS):
            for i in range(1, seqs):
                part = tok.at[0, pl.ds(c * rows, rows)]
                pltpu.make_async_copy(part, part, z_send.at[i - 1, c]).wait()

    finish()
    for copy in own_copies:
        copy.wait()


def gather_inputs(tokens, pack, ids, seqs, dps):
    seq_local, span, width = tokens.shape
    per = seq_local // seqs
    return pl.pallas_call(
        functools.partial(gather_kernel, seqs, dps),
        out_shape=(
            jax.ShapeDtypeStruct((per, seqs, span, width), BF16),
            jax.ShapeDtypeStruct((seqs, dps) + pack.shape, BF16),
            jax.ShapeDtypeStruct((seqs,) + ids.shape, jnp.int32),
        ),
        in_specs=[ANY] * 3,
        out_specs=[ANY] * 3,
        scratch_shapes=[
            DMA((per + 2,)),
            DMA((seqs - 1, CHUNKS)),
            DMA((per, CHUNKS)),
            DMA((3, per, CHUNKS)),
            DMA((3, per, CHUNKS)),
            DMA((seqs - 1,)),
            DMA((seqs - 1,)),
        ]
        + line_sems(seqs, dps),
        compiler_params=params(collective_id=0),
        name="gather_inputs",
    )(tokens, pack, ids)


def heads_kernel(
    seqs, dps, out, cot, pack, out_all, cot_own, pack_all, weight_all, ls, z_send, z_recv, a_send, a_recv, w_send, w_recv, *sems
):
    me = Place(seqs, dps)
    h, s, d = me.h, me.s, me.d
    per = cot_own.shape[0]
    greet(me.seq_peers() + me.dp_peers() + [{"head": mod(h + i, 4)} for i in range(1, 4)])
    start, step, finish = line_gather(me, pack, pack_all, sems, 0)
    copies = []
    for i in range(1, 4):
        to = mod(h + i, 4)
        for j in range(per):
            copies.append(
                send(
                    out.at[j, me.block(j, to)],
                    out_all.at[h, j],
                    a_send.at[i - 1, j],
                    a_recv.at[i - 1, j],
                    head=to,
                )
            )
    own_copies = [pltpu.make_async_copy(out.at[j, me.block(j)], out_all.at[h, j], ls.at[j]) for j in range(per)]
    own_copies.append(pltpu.make_async_copy(pack, pack_all.at[s, d], ls.at[per]))
    for copy in own_copies:
        copy.start()
    start()
    turn = mod(h - s, 4)
    mine = lax.rem(turn, 2) == 0
    which = lax.div(turn, 2)

    @pl.when(mine)
    def _():
        for i in range(1, seqs):
            to = mod(s + i, seqs)
            send(cot.at[per * to + which], cot_own.at[which], z_send.at[i - 1], z_recv.at[which], seq=to)
        own = pltpu.make_async_copy(cot.at[per * s + which], cot_own.at[which], ls.at[per + 1])
        own.start()
        own.wait()

    for t in range(1, seqs):
        step(t)
    for copy in own_copies:
        copy.wait()
    finish()
    lanes = weight_all.shape[-1]
    gone = []
    for i in range(1, 4):
        gone.append(
            send(
                pack_all.at[:, :, :, pl.ds(0, lanes)],
                weight_all.at[h],
                w_send.at[i - 1],
                w_recv.at[i - 1],
                head=mod(h + i, 4),
            )
        )
    own = pltpu.make_async_copy(pack_all.at[:, :, :, pl.ds(0, lanes)], weight_all.at[h], ls.at[0])
    own.start()
    own.wait()
    for j in range(per):

        @pl.when(me.block(j) != s)
        def _():
            arrived(cot_own.at[j], z_recv.at[j])

    @pl.when(mine)
    def _():
        for i in range(1, seqs):
            pltpu.make_async_copy(cot.at[0], cot.at[0], z_send.at[i - 1]).wait()

    for copy in copies + gone:
        copy.wait_send()
    for i in range(1, 4):
        source = mod(h - i, 4)
        for j in range(per):
            arrived(out_all.at[source, j], a_recv.at[i - 1, j])
        arrived(weight_all.at[source], w_recv.at[i - 1])


def gather_heads(out, cot, pack, seqs, dps, lanes):
    per, _, span, width = out.shape
    return pl.pallas_call(
        functools.partial(heads_kernel, seqs, dps),
        out_shape=(
            jax.ShapeDtypeStruct((4, per, span, width), BF16),
            jax.ShapeDtypeStruct((per,) + cot.shape[1:], BF16),
            jax.ShapeDtypeStruct((seqs, dps) + pack.shape, BF16),
            jax.ShapeDtypeStruct((4, seqs, dps, pack.shape[0], lanes), BF16),
        ),
        in_specs=[ANY] * 3,
        out_specs=[ANY] * 4,
        scratch_shapes=[
            DMA((per + 2,)),
            DMA((seqs - 1,)),
            DMA((per,)),
            DMA((3, per)),
            DMA((3, per)),
            DMA((3,)),
            DMA((3,)),
        ]
        + line_sems(seqs, dps),
        compiler_params=params(collective_id=1),
        name="gather_heads",
    )(out, cot, pack)


def dispatch_kernel(seqs, dps, rows, taken, ls, g_send, g_recv, h_send, h_recv):
    me = Place(seqs, dps)
    h, s, d = me.h, me.s, me.d
    groups, parts = seqs * dps, rows.shape[0]
    me_group = s * dps + d
    greet(me.group_peers() + me.head_pair())
    others = [(i, j) for i in range(seqs) for j in range(dps) if i or j]
    for part in range(parts):
        pltpu.make_async_copy(rows.at[part, me_group], taken.at[h, part, me_group], ls.at[part]).start()
        for n, (i, j) in enumerate(others):
            to_s, to_d = mod(s + i, seqs), mod(d + j, dps)
            send(
                rows.at[part, to_s * dps + to_d],
                taken.at[h, part, me_group],
                g_send.at[part, n],
                g_recv.at[part, n],
                seq=to_s,
                dp=to_d,
            )

    def from_of(n):
        i, j = others[n]
        return mod(s - i, seqs) * dps + mod(d - j, dps)

    for part in range(parts):
        for n in range(-1, len(others)):
            source = me_group if n < 0 else from_of(n)
            here = taken.at[h, part, source]
            if n < 0:
                pltpu.make_async_copy(here, here, ls.at[part]).wait()
            else:
                arrived(here, g_recv.at[part, n])
            send(here, here, h_send.at[0, part, n + 1], h_recv.at[0, part, n + 1], head=me.across)
            send(here, here, h_send.at[1, part, n + 1], h_recv.at[1, part, n + 1], head=me.near)
    for part in range(parts):
        for n in range(-1, len(others)):
            source = me_group if n < 0 else from_of(n)
            there = taken.at[me.across, part, source]
            arrived(there, h_recv.at[0, part, n + 1])
            send(there, there, h_send.at[2, part, n + 1], h_recv.at[2, part, n + 1], head=me.near)
    for part in range(parts):
        for n in range(-1, len(others)):
            source = me_group if n < 0 else from_of(n)
            here = taken.at[h, part, source]
            for k in range(3):
                pltpu.make_async_copy(here, here, h_send.at[k, part, n + 1]).wait()
            if n >= 0:
                pltpu.make_async_copy(here, here, g_send.at[part, n]).wait()
            arrived(taken.at[me.near, part, source], h_recv.at[1, part, n + 1])
            arrived(taken.at[me.near_across, part, source], h_recv.at[2, part, n + 1])


def dispatch(rows, seqs, dps):
    parts, groups = rows.shape[:2]
    return pl.pallas_call(
        functools.partial(dispatch_kernel, seqs, dps),
        out_shape=jax.ShapeDtypeStruct((4,) + rows.shape, BF16),
        in_specs=[ANY],
        out_specs=ANY,
        scratch_shapes=[
            DMA((parts,)),
            DMA((parts, groups)),
            DMA((parts, groups)),
            DMA((3, parts, groups)),
            DMA((3, parts, groups)),
        ],
        compiler_params=params(collective_id=2),
        name="dispatch",
    )(rows)


def combine_kernel(
    seqs, dps, partial, summed, own, near, far_out, far_in, total, ls, n_send, n_recv, x_send, x_recv, g_send, g_recv
):
    me = Place(seqs, dps)
    h, s, d = me.h, me.s, me.d
    groups, parts = seqs * dps, summed.shape[0]
    me_group = s * dps + d
    greet(me.group_peers() + me.head_pair())
    others = [(i, j) for i in range(seqs) for j in range(dps) if i or j] + [(0, 0)]
    order = [(part, n) for part in range(parts) for n in range(groups)]

    def group_of(n):
        i, j = others[n]
        return mod(s + i, seqs), mod(d + j, dps)

    for part, n in order:
        to_s, to_d = group_of(n)
        group = to_s * dps + to_d
        for k, head in enumerate((me.near_across, me.near)):
            send(
                partial.at[head, part, group],
                near.at[k, part, n],
                n_send.at[k, part, n],
                n_recv.at[k, part, n],
                head=me.near,
            )
        for k, head in enumerate((me.across, h)):
            pltpu.make_async_copy(partial.at[head, part, group], own.at[k, part, n], ls.at[k, part, n]).start()
    for part, n in order:
        arrived(near.at[0, part, n], n_recv.at[0, part, n])
        pltpu.make_async_copy(own.at[0, part, n], own.at[0, part, n], ls.at[0, part, n]).wait()
        both = own[0, part, n].astype(F32) + near[0, part, n].astype(F32)
        far_out[part, n] = both.astype(BF16)
        send(far_out.at[part, n], far_in.at[part, n], x_send.at[part, n], x_recv.at[part, n], head=me.across)
    for part, n in order:
        to_s, to_d = group_of(n)
        arrived(near.at[1, part, n], n_recv.at[1, part, n])
        pltpu.make_async_copy(own.at[1, part, n], own.at[1, part, n], ls.at[1, part, n]).wait()
        arrived(far_in.at[part, n], x_recv.at[part, n])
        both = own[1, part, n].astype(F32) + near[1, part, n].astype(F32) + far_in[part, n].astype(F32)
        total[part, n] = both.astype(BF16)
        if n < groups - 1:
            send(
                total.at[part, n],
                summed.at[part, me_group],
                g_send.at[part, n],
                g_recv.at[part, n],
                seq=to_s,
                dp=to_d,
            )
        else:
            pltpu.make_async_copy(total.at[part, n], summed.at[part, me_group], g_send.at[part, n]).start()
    for part, n in order:
        i, j = others[n]
        for k in range(2):
            pltpu.make_async_copy(near.at[k, part, n], near.at[k, part, n], n_send.at[k, part, n]).wait()
        pltpu.make_async_copy(far_out.at[part, n], far_out.at[part, n], x_send.at[part, n]).wait()
        pltpu.make_async_copy(total.at[part, n], total.at[part, n], g_send.at[part, n]).wait()
        if n < groups - 1:
            source = mod(s - i, seqs) * dps + mod(d - j, dps)
            arrived(summed.at[part, source], g_recv.at[part, n])


def combine(partial, seqs, dps):
    _, parts, groups, rows, width = partial.shape
    block = (parts, groups, rows, width)
    return pl.pallas_call(
        functools.partial(combine_kernel, seqs, dps),
        out_shape=jax.ShapeDtypeStruct(block, BF16),
        in_specs=[ANY],
        out_specs=ANY,
        scratch_shapes=[
            pltpu.VMEM((2,) + block, BF16),
            pltpu.VMEM((2,) + block, BF16),
            pltpu.VMEM(block, BF16),
            pltpu.VMEM(block, BF16),
            pltpu.VMEM(block, BF16),
        ]
        + [DMA((2, parts, groups))] * 3
        + [DMA((parts, groups))] * 4,
        compiler_params=params(collective_id=3),
        name="combine",
    )(partial)


def send_home(me, own, home, ls, z_send, z_recv, h_send, h_recv):
    h, s, seqs = me.h, me.s, me.seqs
    per = own.shape[0]
    turn = mod(s - h, 4)
    mine = lax.rem(turn, 2) == 0
    which = lax.div(turn, 2)

    def start():
        for j in range(per):
            to = me.block(j)

            @pl.when(to != s)
            def _():
                send(own.at[j], home.at[per * s + j], z_send.at[j], z_recv.at[s], seq=to)

            @pl.when(to == s)
            def _():
                pltpu.make_async_copy(own.at[j], home.at[per * s + j], ls).start()

    def forward():
        @pl.when(mine)
        def _():
            for i in range(seqs):
                source = mod(s + i, seqs)
                here = home.at[per * source + which]
                if i == 0:
                    pltpu.make_async_copy(here, here, ls).wait()
                else:
                    arrived(here, z_recv.at[source])
                send(here, here, h_send.at[0, source], h_recv.at[0, source], head=me.across)
                send(here, here, h_send.at[1, source], h_recv.at[1, source], head=me.near)
            for i in range(seqs):
                source = mod(s + i, seqs)
                there = home.at[per * source + 1 - which]
                arrived(there, h_recv.at[0, source])
                send(there, there, h_send.at[2, source], h_recv.at[2, source], head=me.near)

    def finish():
        for j in range(per):

            @pl.when(me.block(j) != s)
            def _():
                pltpu.make_async_copy(own.at[j], own.at[j], z_send.at[j]).wait()

        @pl.when(mine)
        def _():
            for source in range(seqs):
                for k in range(3):
                    here = home.at[per * source]
                    pltpu.make_async_copy(here, here, h_send.at[k, source]).wait()

        @pl.when(jnp.logical_not(mine))
        def _():
            for source in range(seqs):
                arrived(home.at[per * source], h_recv.at[1, source])
                arrived(home.at[per * source + 1], h_recv.at[2, source])

    return start, forward, finish


def home_sems(per, seqs):
    return [DMA(()), DMA((per,)), DMA((seqs,)), DMA((3, seqs)), DMA((3, seqs))]


def grads_kernel(seqs, dps, grad, result, grad_all, home, ls, a_send, a_recv, *sems):
    me = Place(seqs, dps)
    h = me.h
    per = result.shape[0]
    start, forward, finish = send_home(me, result, home, *sems)
    greet(me.seq_peers() + [{"head": mod(h + i, 4)} for i in range(1, 4)])
    copies = []
    for i in range(1, 4):
        to = mod(h + i, 4)
        for j in range(per):
            copies.append(
                send(
                    grad.at[to, j],
                    grad_all.at[j, me.block(j)],
                    a_send.at[i - 1, j],
                    a_recv.at[i - 1, j],
                    head=to,
                )
            )
    own_copies = [pltpu.make_async_copy(grad.at[h, j], grad_all.at[j, me.block(j)], ls.at[j]) for j in range(per)]
    for copy in own_copies:
        copy.start()
    start()
    forward()
    finish()
    for copy in own_copies:
        copy.wait()
    for copy in copies:
        copy.wait_send()
    for i in range(1, 4):
        source = mod(h - i, 4)
        for j in range(per):
            arrived(grad_all.at[j, me.block(j, source)], a_recv.at[i - 1, j])


def gather_grads(grad, result, seqs, dps):
    _, per, span, width = grad.shape
    return pl.pallas_call(
        functools.partial(grads_kernel, seqs, dps),
        out_shape=(
            jax.ShapeDtypeStruct((per, seqs, span, width), BF16),
            jax.ShapeDtypeStruct((per * seqs,) + result.shape[1:], BF16),
        ),
        in_specs=[ANY] * 2,
        out_specs=[ANY] * 2,
        scratch_shapes=[DMA((per,)), DMA((3, per)), DMA((3, per))] + home_sems(per, seqs),
        compiler_params=params(collective_id=4),
        name="gather_grads",
    )(grad, result)


def input_kernel(
    seqs, dps, partial, weight, total, weight_out, own, near, far_out, far_in, wown, wnear, wfar_out, wfar_in,
    ls, n_send, n_recv, x_send, x_recv, wls, wn_send, wn_recv, wx_send, wx_recv
):
    me = Place(seqs, dps)
    h = me.h
    per = total.shape[0]
    greet(me.head_pair())
    for j in range(per):
        for k, head in enumerate((me.near_across, me.near)):
            send(partial.at[j, me.block(j, head)], near.at[k, j], n_send.at[k, j], n_recv.at[k, j], head=me.near)
        for k, head in enumerate((me.across, h)):
            pltpu.make_async_copy(partial.at[j, me.block(j, head)], own.at[k, j], ls.at[k, j]).start()
    for k, head in enumerate((me.near_across, me.near)):
        send(weight.at[head], wnear.at[k], wn_send.at[k], wn_recv.at[k], head=me.near)
    for k, head in enumerate((me.across, h)):
        pltpu.make_async_copy(weight.at[head], wown.at[k], wls.at[k]).start()
    for j in range(per):
        arrived(near.at[0, j], n_recv.at[0, j])
        pltpu.make_async_copy(own.at[0, j], own.at[0, j], ls.at[0, j]).wait()
        far_out[j] = (own[0, j].astype(F32) + near[0, j].astype(F32)).astype(BF16)
        send(far_out.at[j], far_in.at[j], x_send.at[j], x_recv.at[j], head=me.across)
    arrived(wnear.at[0], wn_recv.at[0])
    pltpu.make_async_copy(wown.at[0], wown.at[0], wls.at[0]).wait()
    wfar_out[...] = (wown[0].astype(F32) + wnear[0].astype(F32)).astype(BF16)
    send(wfar_out, wfar_in, wx_send, wx_recv, head=me.across)
    for j in range(per):
        arrived(near.at[1, j], n_recv.at[1, j])
        pltpu.make_async_copy(own.at[1, j], own.at[1, j], ls.at[1, j]).wait()
        arrived(far_in.at[j], x_recv.at[j])
        total[j] = own[1, j].astype(F32) + near[1, j].astype(F32) + far_in[j].astype(F32)
    arrived(wnear.at[1], wn_recv.at[1])
    pltpu.make_async_copy(wown.at[1], wown.at[1], wls.at[1]).wait()
    arrived(wfar_in, wx_recv)
    weight_out[...] = wown[1].astype(F32) + wnear[1].astype(F32) + wfar_in[...].astype(F32)
    for j in range(per):
        for k in range(2):
            pltpu.make_async_copy(near.at[k, j], near.at[k, j], n_send.at[k, j]).wait()
        pltpu.make_async_copy(far_out.at[j], far_out.at[j], x_send.at[j]).wait()
    for k in range(2):
        pltpu.make_async_copy(wnear.at[k], wnear.at[k], wn_send.at[k]).wait()
    pltpu.make_async_copy(wfar_out, wfar_out, wx_send).wait()


def add_heads(partial, weight, seqs, dps):
    per, _, span, width = partial.shape
    block = (per, span, width)
    wblock = weight.shape[1:]
    return pl.pallas_call(
        functools.partial(input_kernel, seqs, dps),
        out_shape=(jax.ShapeDtypeStruct(block, F32), jax.ShapeDtypeStruct(wblock, F32)),
        in_specs=[ANY] * 2,
        out_specs=[VMEM] * 2,
        scratch_shapes=[
            pltpu.VMEM((2,) + block, BF16),
            pltpu.VMEM((2,) + block, BF16),
            pltpu.VMEM(block, BF16),
            pltpu.VMEM(block, BF16),
            pltpu.VMEM((2,) + wblock, BF16),
            pltpu.VMEM((2,) + wblock, BF16),
            pltpu.VMEM(wblock, BF16),
            pltpu.VMEM(wblock, BF16),
        ]
        + [DMA((2, per))] * 3
        + [DMA((per,))] * 2
        + [DMA((2,))] * 3
        + [DMA(())] * 2,
        compiler_params=params(collective_id=5),
        name="add_heads",
    )(partial, weight)


def last_kernel(
    seqs, dps, grad, weights, bias, home, weights_sum, bias_sum, wsum, wtake, ytake, btake, small,
    ls, y_send, y_recv, w_send, w_recv, b_send, b_recv, s_send, s_recv, *sems
):
    me = Place(seqs, dps)
    h, s, d = me.h, me.s, me.d
    start, forward, finish = send_home(me, grad, home, *sems)
    others = [(i, j) for i in range(seqs) for j in range(dps) if i or j]
    greet(me.group_peers() + [{"head": mod(h + i, 4)} for i in range(1, 4)])
    for i in range(1, dps):
        to = mod(d + i, dps)
        send(weights.at[to], ytake.at[i - 1], y_send.at[i - 1], y_recv.at[i - 1], dp=to)
    mine_y = pltpu.make_async_copy(weights.at[d], wsum, ls)
    mine_y.start()
    for n, (i, j) in enumerate(others):
        send(bias, btake.at[n], b_send.at[n], b_recv.at[n], seq=mod(s + i, seqs), dp=mod(d + j, dps))
    start()
    mine_y.wait()
    for i in range(1, dps):
        arrived(ytake.at[i - 1], y_recv.at[i - 1])
    for t in range(seqs):
        acc = wsum[t].astype(F32)
        for i in range(1, dps):
            acc = acc + ytake[i - 1, t].astype(F32)
        wsum[t] = acc.astype(BF16)
    for i in range(1, seqs):
        to = mod(s + i, seqs)
        send(wsum.at[to], wtake.at[i - 1], w_send.at[i - 1], w_recv.at[i - 1], seq=to)
    forward()
    acc = wsum[s].astype(F32)
    for i in range(1, seqs):
        arrived(wtake.at[i - 1], w_recv.at[i - 1])
        acc = acc + wtake[i - 1].astype(F32)
    weights_sum[...] = acc
    lanes = small.shape[-1]
    small[0] = acc[:, acc.shape[-1] - lanes :]
    for i in range(1, 4):
        send(small.at[0], small.at[i], s_send.at[i - 1], s_recv.at[i - 1], head=mod(h + i, 4))
    total = bias[...]
    for n in range(len(others)):
        arrived(btake.at[n], b_recv.at[n])
        total = total + btake[n]
    bias_sum[...] = total
    tail = small[0]
    for i in range(1, 4):
        arrived(small.at[i], s_recv.at[i - 1])
        tail = tail + small[i]
    weights_sum[:, acc.shape[-1] - lanes :] = tail
    for i in range(1, 4):
        pltpu.make_async_copy(small.at[0], small.at[0], s_send.at[i - 1]).wait()
    for i in range(1, dps):
        pltpu.make_async_copy(ytake.at[0], ytake.at[0], y_send.at[i - 1]).wait()
    for i in range(1, seqs):
        pltpu.make_async_copy(wsum.at[0], wsum.at[0], w_send.at[i - 1]).wait()
    for n in range(len(others)):
        pltpu.make_async_copy(btake.at[0], btake.at[0], b_send.at[n]).wait()
    finish()


def finish_grads(grad, weights, bias, seqs, dps, small):
    per, span, width = grad.shape
    _, _, rows, lanes = weights.shape
    groups = seqs * dps
    return pl.pallas_call(
        functools.partial(last_kernel, seqs, dps),
        out_shape=(
            jax.ShapeDtypeStruct((per * seqs, span, width), BF16),
            jax.ShapeDtypeStruct((rows, lanes), F32),
            jax.ShapeDtypeStruct(bias.shape, F32),
        ),
        in_specs=[ANY, ANY, VMEM],
        out_specs=[ANY, VMEM, VMEM],
        scratch_shapes=[
            pltpu.VMEM((seqs, rows, lanes), BF16),
            pltpu.VMEM((seqs - 1, rows, lanes), BF16),
            pltpu.VMEM((max(1, dps - 1), seqs, rows, lanes), BF16),
            pltpu.VMEM((groups - 1,) + bias.shape, F32),
            pltpu.VMEM((4, rows, small), F32),
            DMA(()),
            DMA((max(1, dps - 1),)),
            DMA((max(1, dps - 1),)),
            DMA((seqs - 1,)),
            DMA((seqs - 1,)),
            DMA((groups - 1,)),
            DMA((groups - 1,)),
            DMA((3,)),
            DMA((3,)),
        ]
        + home_sems(per, seqs),
        compiler_params=params(collective_id=6),
        name="finish_grads",
    )(grad, weights, bias)


def bias_block(band, far, head, q_block, k_block, span):
    step = k_block - q_block
    if abs(step) <= 1:
        return band[head, :, (step + 1) * span : (step + 2) * span]
    return far[head, 0 if step < 0 else 1]


def attend_kernel(heads, blocks, span, q_ref, k_ref, v_ref, band, far, mask, out_ref, prob_ref):
    for head in range(heads):
        cols = slice(head * HEAD_DIM, (head + 1) * HEAD_DIM)
        key = k_ref[0, :, cols]
        value = v_ref[0, :, cols]
        for q_block in range(blocks):
            rows = slice(q_block * span, (q_block + 1) * span)
            query = q_ref[0, rows, cols]
            scores = lax.dot_general(query, key, (((1,), (1,)), ((), ())), preferred_element_type=F32)
            parts = []
            for k_block in range(blocks):
                part = scores[:, k_block * span : (k_block + 1) * span]
                valid = mask[0, :, k_block * span : (k_block + 1) * span]
                term = bias_block(band, far, head, q_block, k_block, span)
                parts.append(jnp.where(valid > 0, part + term, -1e30))
            scores = jnp.concatenate(parts, axis=1)
            top = jnp.max(scores, axis=-1, keepdims=True)
            grown = jnp.exp(scores - top)
            total = jnp.sum(grown, axis=-1, keepdims=True)
            weights = (grown * (1.0 / total)).astype(BF16)
            prob_ref[0, head, rows, :] = weights
            mixed = jnp.dot(weights, value, preferred_element_type=F32)
            out_ref[0, rows, cols] = mixed.astype(BF16)


def attend(queries, keys, values, band, far, mask, heads, blocks, span):
    per, length, width = queries.shape
    whole = pl.BlockSpec((1, length, width), lambda j: (j, 0, 0))
    return pl.pallas_call(
        functools.partial(attend_kernel, heads, blocks, span),
        grid=(per,),
        out_shape=(
            jax.ShapeDtypeStruct((per, length, width), BF16),
            jax.ShapeDtypeStruct((per, heads, length, length), BF16),
        ),
        in_specs=[
            whole,
            whole,
            whole,
            pl.BlockSpec(band.shape, lambda j: (0, 0, 0)),
            pl.BlockSpec(memory_space=pltpu.SMEM),
            pl.BlockSpec((1, 1, length), lambda j: (j, 0, 0)),
        ],
        out_specs=[whole, pl.BlockSpec((1, heads, length, length), lambda j: (j, 0, 0, 0))],
        compiler_params=pltpu.CompilerParams(vmem_limit_bytes=56 * 2**20),
        name="attend",
    )(queries, keys, values, band, far, mask)


def attend_back_kernel(
    heads, blocks, span, q_ref, k_ref, v_ref, g_ref, p_ref, dq_ref, dk_ref, dv_ref, band_ref, far_ref, dk_sum, dv_sum
):
    first = pl.program_id(0) == 0
    for head in range(heads):
        cols = slice(head * HEAD_DIM, (head + 1) * HEAD_DIM)
        key = k_ref[0, :, cols]
        value = v_ref[0, :, cols]
        for q_block in range(blocks):
            rows = slice(q_block * span, (q_block + 1) * span)
            query = q_ref[0, rows, cols]
            grad = g_ref[0, rows, cols]
            weights = p_ref[0, head, rows, :]
            prob_grad = lax.dot_general(grad, value, (((1,), (1,)), ((), ())), preferred_element_type=F32)
            wide = weights.astype(F32)
            delta = jnp.sum(wide * prob_grad, axis=-1, keepdims=True)
            score_grad = wide * (prob_grad - delta)
            for k_block in range(blocks):
                part = score_grad[:, k_block * span : (k_block + 1) * span]
                step = k_block - q_block
                if abs(step) <= 1:
                    where = (head, slice(None), slice((step + 1) * span, (step + 2) * span))
                    begin = first & (q_block == (1 if step < 0 else 0))
                    old = band_ref[where]
                    band_ref[where] = jnp.where(begin, 0.0, old) + part
                else:
                    side = 0 if step < 0 else 1
                    begin = first & ((q_block, k_block) == ((2, 0) if side == 0 else (0, 2)))
                    flat = jnp.sum(part.reshape(span // 8, 8, span), axis=0)
                    old = far_ref[head, side]
                    far_ref[head, side] = jnp.where(begin, 0.0, old) + flat
            low = score_grad.astype(BF16)
            dq_ref[0, rows, cols] = jnp.dot(low, key, preferred_element_type=F32).astype(BF16)
            dk = lax.dot_general(low, query, (((0,), (0,)), ((), ())), preferred_element_type=F32)
            dv = lax.dot_general(weights, grad, (((0,), (0,)), ((), ())), preferred_element_type=F32)
            if q_block == 0:
                dk_sum[...] = dk
                dv_sum[...] = dv
            else:
                dk_sum[...] += dk
                dv_sum[...] += dv
        dk_ref[0, :, cols] = dk_sum[...].astype(BF16)
        dv_ref[0, :, cols] = dv_sum[...].astype(BF16)


def attend_back(queries, keys, values, grads, probs, heads, blocks, span):
    per, length, width = queries.shape
    whole = pl.BlockSpec((1, length, width), lambda j: (j, 0, 0))
    return pl.pallas_call(
        functools.partial(attend_back_kernel, heads, blocks, span),
        grid=(per,),
        out_shape=(
            jax.ShapeDtypeStruct((per, length, width), BF16),
            jax.ShapeDtypeStruct((per, length, width), BF16),
            jax.ShapeDtypeStruct((per, length, width), BF16),
            jax.ShapeDtypeStruct((heads, span, 3 * span), F32),
            jax.ShapeDtypeStruct((heads, 2, 8, span), F32),
        ),
        in_specs=[whole] * 4 + [pl.BlockSpec((1, heads, length, length), lambda j: (j, 0, 0, 0))],
        out_specs=[whole] * 3
        + [
            pl.BlockSpec((heads, span, 3 * span), lambda j: (0, 0, 0)),
            pl.BlockSpec((heads, 2, 8, span), lambda j: (0, 0, 0, 0)),
        ],
        scratch_shapes=[pltpu.VMEM((length, HEAD_DIM), F32)] * 2,
        compiler_params=pltpu.CompilerParams(vmem_limit_bytes=56 * 2**20),
        name="attend_back",
    )(queries, keys, values, grads, probs)


def up_to(value, unit):
    return -(-value // unit) * unit


def body(
    tokens,
    lengths,
    expert_ids,
    attention_gain,
    query_weight,
    key_weight,
    value_weight,
    output_weight,
    position_bias,
    feedforward_gain,
    router_weight,
    expert_up,
    expert_down,
    cotangent,
):
    seqs, dps = lax.axis_size("seq"), lax.axis_size("dp")
    groups = seqs * dps
    seq_local, span, width = tokens.shape
    per = seq_local // seqs
    length = seqs * span
    count = per * length
    own_rows = per * span
    local_width = query_weight.shape[1]
    bucket_count, heads = position_bias.shape
    experts = router_weight.shape[1]
    exp_local = expert_up.shape[0]
    shard = query_weight.shape[0]
    head_at, seq_at = lax.axis_index("head"), lax.axis_index("seq")

    first_width = up_to(3 * local_width + 1, 128)
    first_pack = jnp.concatenate(
        [
            query_weight,
            key_weight,
            value_weight,
            attention_gain[:, None],
            jnp.zeros((shard, first_width - 3 * local_width - 1), BF16),
        ],
        axis=1,
    )
    lanes = up_to(local_width, 128)
    small = up_to(experts + 1, 128)
    second_pack = jnp.concatenate(
        [
            output_weight.T,
            jnp.zeros((shard, lanes - local_width), BF16),
            router_weight,
            feedforward_gain[:, None],
            jnp.zeros((shard, small - experts - 1), BF16),
        ],
        axis=1,
    )
    ids = expert_ids.reshape(seq_local, span)
    tok_all, first_all, ids_all = gather_inputs(tokens, first_pack, ids, seqs, dps)
    first_all = first_all.reshape(width, first_width)
    project_weight = first_all[:, : 3 * local_width]
    gain_one = first_all[:, 3 * local_width].astype(F32)

    inputs = tok_all.reshape(count, width).astype(F32)
    attn_input = normalize(inputs, gain_one).astype(BF16)
    made = jnp.dot(attn_input, project_weight, preferred_element_type=F32).astype(BF16)
    queries, keys, values = (
        made[:, i * local_width : (i + 1) * local_width].reshape(per, length, local_width) for i in range(3)
    )
    offset = jnp.arange(3 * span, dtype=jnp.int32)[None, :] - span - jnp.arange(span, dtype=jnp.int32)[:, None]
    bucket = bucket_of(offset, bucket_count)
    table = position_bias.astype(F32)
    band = jnp.zeros((heads, span, 3 * span), F32)
    for b in range(bucket_count):
        band = jnp.where((bucket == b)[None], table[b][:, None, None], band)
    far = jnp.stack([table[bucket_count // 2 - 1], table[bucket_count - 1]], axis=1)
    own_lengths = lax.dynamic_slice_in_dim(lengths, per * seq_at, per)
    mask = (jnp.arange(length, dtype=jnp.int32)[None, None, :] < own_lengths[:, None, None]).astype(F32)
    heads_out, probs = attend(queries, keys, values, band, far, mask, heads, seqs, span)

    heads_all, cot_own, second_all, out_weight = gather_heads(
        heads_out.reshape(per, seqs, span, local_width), cotangent, second_pack, seqs, dps, lanes
    )
    second_all = second_all.reshape(width, lanes + small)
    router_full = second_all[:, lanes : lanes + experts]
    gain_two = second_all[:, lanes + experts].astype(F32)
    out_weight = out_weight.reshape(4, width, lanes)[:, :, :local_width]
    heads_all = heads_all.reshape(4, own_rows, local_width)
    own_blocks = [lax.rem(head_at + 2 * j, 4) for j in range(per)]
    own_inputs = jnp.stack([lax.dynamic_index_in_dim(tok_all[j], own_blocks[j], 0, False) for j in range(per)])
    own_inputs = own_inputs.reshape(own_rows, width).astype(F32)
    attention = jnp.einsum("htk,hdk->td", heads_all, out_weight, preferred_element_type=F32)
    hidden = own_inputs + attention
    ffn_input = normalize(hidden, gain_two).astype(BF16)
    logits = jnp.dot(ffn_input, router_full, preferred_element_type=F32)
    router_probs = jax.nn.softmax(logits, axis=-1)

    capacity = max(2, (5 * span + 4 * experts - 1) // (4 * experts))
    own_ids = jnp.stack(
        [
            lax.dynamic_index_in_dim(lax.dynamic_index_in_dim(ids_all, own_blocks[j], 0, False), per * seq_at + j, 0, False)
            for j in range(per)
        ]
    )
    earlier = jnp.arange(span)[None, :] < jnp.arange(span)[:, None]
    same = (own_ids[:, :, None] == own_ids[:, None, :]) & earlier[None]
    slot = jnp.sum(same.astype(jnp.int32), axis=-1)
    rows_used = exp_local * per * capacity
    rows_pad = up_to(rows_used, 16)
    place = (
        own_ids // exp_local * rows_pad
        + (own_ids % exp_local * per + jnp.arange(per, dtype=jnp.int32)[:, None]) * capacity
        + slot
    ).reshape(own_rows)
    spots = groups * rows_pad
    place_hot = (jnp.arange(spots, dtype=jnp.int32)[:, None] == place[None, :]).astype(BF16)
    hot = (own_ids.reshape(own_rows, 1) == jnp.arange(experts, dtype=jnp.int32)).astype(F32)
    gate = jnp.sum(router_probs * hot, axis=-1)
    grad_out = cot_own.reshape(own_rows, width).astype(F32)
    sent_grad = (gate[:, None] * grad_out).astype(BF16)
    to_send = jnp.stack([ffn_input, sent_grad])
    rows = jnp.einsum("rt,ptd->prd", place_hot, to_send, preferred_element_type=F32).astype(BF16)
    taken = dispatch(rows.reshape(2, groups, rows_pad, width), seqs, dps)

    def by_expert(part):
        part = taken[:, part, :, :rows_used].reshape(4 * groups, exp_local, per * capacity, width)
        return jnp.swapaxes(part, 0, 1).reshape(exp_local, 4 * groups * per * capacity, width)

    def by_group(part):
        part = jnp.swapaxes(part.reshape(exp_local, 4 * groups, per * capacity, width), 0, 1)
        part = part.reshape(4, groups, rows_used, width)
        return jnp.pad(part, ((0, 0), (0, 0), (0, rows_pad - rows_used), (0, 0)))

    received, grad_rows = by_expert(0), by_expert(1)
    hidden_pre = jnp.einsum("xrd,xdf->xrf", received, expert_up, preferred_element_type=F32)
    activated = gelu_tanh(hidden_pre).astype(BF16)
    partial_out = jnp.einsum("xrf,xfd->xrd", activated, expert_down, preferred_element_type=F32).astype(BF16)
    act_grad = jnp.einsum("xrd,xfd->xrf", grad_rows, expert_down, preferred_element_type=F32)
    _, gelu_pull = jax.vjp(gelu_tanh, hidden_pre)
    pre_grad = gelu_pull(act_grad)[0].astype(BF16)
    input_part = jnp.einsum("xrf,xdf->xrd", pre_grad, expert_up, preferred_element_type=F32).astype(BF16)
    summed = combine(jnp.stack([by_group(partial_out), by_group(input_part)], axis=1), seqs, dps)
    down_grad = jnp.einsum("xrf,xrd->xfd", activated, grad_rows, preferred_element_type=F32)
    up_grad = jnp.einsum("xrd,xrf->xdf", received, pre_grad, preferred_element_type=F32)

    back = jnp.einsum("rt,prd->ptd", place_hot, summed.reshape(2, spots, width), preferred_element_type=F32)
    token_out, expert_input_grad = back[0], back[1]
    result = (hidden + gate[:, None] * token_out).astype(BF16)
    gate_grad = jnp.sum(grad_out * token_out, axis=-1)
    logit_grad = router_probs * (gate_grad[:, None] * hot - (gate_grad * gate)[:, None])
    logit_low = logit_grad.astype(BF16)
    router_grad = jnp.einsum("td,te->de", ffn_input, logit_low, preferred_element_type=F32)
    ffn_input_grad = expert_input_grad + jnp.einsum("te,de->td", logit_low, router_full, preferred_element_type=F32)
    _, norm_pull = jax.vjp(normalize, hidden, gain_two)
    hidden_norm_grad, gain_two_grad = norm_pull(ffn_input_grad)
    hidden_grad = grad_out + hidden_norm_grad
    attn_grad = hidden_grad.astype(BF16)
    heads_grad = jnp.einsum("td,hdk->htk", attn_grad, out_weight, preferred_element_type=F32).astype(BF16)
    grad_all, output = gather_grads(
        heads_grad.reshape(4, per, span, local_width), result.reshape(per, span, width), seqs, dps
    )
    out_w_part = jnp.einsum("td,htk->hdk", attn_grad, heads_all, preferred_element_type=F32).astype(BF16)

    query_grad, key_grad, value_grad, band_grad, far_grad = attend_back(
        queries, keys, values, grad_all.reshape(per, length, local_width), probs, heads, seqs, span
    )
    bias_grad = jnp.stack(
        [jnp.sum(jnp.where((bucket == b)[None], band_grad, 0.0), axis=(1, 2)) for b in range(bucket_count)]
    )
    far_sum = jnp.sum(far_grad, axis=(2, 3))
    bias_grad = bias_grad.at[bucket_count // 2 - 1].add(far_sum[:, 0]).at[bucket_count - 1].add(far_sum[:, 1])
    made_grad = jnp.concatenate([query_grad, key_grad, value_grad], axis=-1).reshape(count, 3 * local_width)
    project_grad = jnp.einsum("td,tk->dk", attn_input, made_grad, preferred_element_type=F32).astype(BF16)
    input_part = jnp.einsum("tk,dk->td", made_grad, project_weight, preferred_element_type=F32).astype(BF16)
    attn_input_grad, out_w_sum = add_heads(input_part.reshape(per, seqs, span, width), out_w_part, seqs, dps)
    _, first_pull = jax.vjp(normalize, own_inputs, gain_one)
    input_norm_grad, gain_one_grad = first_pull(attn_input_grad.reshape(own_rows, width))
    tokens_grad = (hidden_grad + input_norm_grad).astype(BF16).reshape(per, span, width)

    tail = jnp.concatenate(
        [
            router_grad,
            gain_one_grad[:, None],
            gain_two_grad[:, None],
            jnp.zeros((width, up_to(experts + 2, 128) - experts - 2), F32),
        ],
        axis=1,
    ).astype(BF16)
    weights = jnp.concatenate([project_grad, out_w_sum.astype(BF16), tail], axis=1)
    weights = jnp.swapaxes(weights.reshape(seqs, dps, shard, weights.shape[-1]), 0, 1)
    bias_pad = jnp.pad(bias_grad, ((0, 0), (0, 128 - heads)))
    tokens_grad, weights_sum, bias_sum = finish_grads(tokens_grad, weights, bias_pad, seqs, dps, tail.shape[1])
    at = 4 * local_width
    return (
        output,
        tokens_grad,
        weights_sum[:, at + experts],
        weights_sum[:, :local_width],
        weights_sum[:, local_width : 2 * local_width],
        weights_sum[:, 2 * local_width : 3 * local_width],
        weights_sum[:, 3 * local_width : at].T,
        bias_sum[:, :heads],
        weights_sum[:, at + experts + 1],
        weights_sum[:, at : at + experts],
        up_grad,
        down_grad,
    )


def solution(mesh):
    placed = (
        P("dp", "seq", None),
        P("dp"),
        P("dp", "seq", None),
        P(("seq", "dp")),
        P(("seq", "dp"), "head"),
        P(("seq", "dp"), "head"),
        P(("seq", "dp"), "head"),
        P("head", ("seq", "dp")),
        P(None, "head"),
        P(("seq", "dp")),
        P(("seq", "dp"), None),
        P(("seq", "dp"), None, "head"),
        P(("seq", "dp"), "head", None),
        P("dp", "seq", None),
    )
    return jax.shard_map(
        body,
        mesh=mesh,
        in_specs=placed,
        out_specs=(
            P("dp", "seq", None),
            P("dp", "seq", None),
            P(("seq", "dp")),
            P(("seq", "dp"), "head"),
            P(("seq", "dp"), "head"),
            P(("seq", "dp"), "head"),
            P("head", ("seq", "dp")),
            P(None, "head"),
            P(("seq", "dp")),
            P(("seq", "dp"), None),
            P(("seq", "dp"), None, "head"),
            P(("seq", "dp"), "head", None),
        ),
        check_vma=False,
    )
```

time: 1510 us -> 603 us (0.40)
  waiting for transfers between devices: 653 us -> 0 us
  Pallas kernels: 0 us -> 392 us
  blocking collectives: 358 us -> 0 us
  matrix products: 195 us -> 68.5 us
  local copies, waits for them, and re-layouts: 150 us -> 69.7 us
  other arithmetic: 113 us -> 61.7 us
  starting transfers between devices: 15.5 us -> 0 us
    pallas_call x0 -> x9, Pallas kernels: none -> 392 us  [the longest x1 65 us: combine(): pl.pallas_call(functools.partial(combine_kernel, seqs, dps), out_shape=ja...]
    reduce_scatter x7 -> x0, waiting for transfers between devices: 297 us -> none  [the longest x1 111 us: body(): lax.psum_scatter(key_grad, 'seq', scatter_dimension=1, tiled=True)]
    all_gather x5 -> x0, blocking collectives: 240 us -> none  [the longest x1 108 us: body(): lax.all_gather(router_weight, ('seq', 'dp'), axis=0, tiled=True)]
    dot_general x27 -> x17, matrix products: 186 us -> 68.5 us  [the longest x1 10.6 us: body(): jnp.einsum('xrf,xrd->xfd', activated, grad_rows, preferred_element_type=F32)]
    all_to_all x3 -> x0, waiting for transfers between devices: 116 us -> none  [the longest x2 62 us: to_experts(): lax.all_to_all(outgoing, ('seq', 'dp'), split_axis=0, concat_axis=0, tile...]
    psum x1 -> x0, waiting for transfers between devices: 116 us -> none  [body(): attn_input_grad = lax.psum(input_part_one, 'head')]
    unnamed x18 -> x0, waiting for transfers between devices: 67 us -> none
    unnamed x2 -> x0, blocking collectives: 60.2 us -> none
  transfers between devices with their start and end apart: 19 -> 0, of which waited for: 12 -> 0; matrix products, arithmetic and copies ran while one was open for 25% -> 0% of each run, Pallas kernels for 0% -> 0%
where the time goes in v1:
time: 603 us; the launch traced here: 594 us
  Pallas kernels  392 us (65%)
  local copies, waits for them, and re-layouts  69.7 us (12%)
  matrix products  68.5 us (11%)
  other arithmetic  61.7 us (10%)
    pallas_call x1, Pallas kernels, combine(): pl.pallas_call(functools.partial(combine_kernel, seqs, dps), out_shape=ja...  65 us
    pallas_call x1, Pallas kernels, dispatch(): pl.pallas_call(functools.partial(dispatch_kernel, seqs, dps), out_shape=j...  56.7 us
    pallas_call x1, Pallas kernels, gather_heads(): pl.pallas_call(functools.partial(heads_kernel, seqs, dps), out_shape=(jax...  54.2 us
    pallas_call x1, Pallas kernels, finish_grads(): pl.pallas_call(functools.partial(last_kernel, seqs, dps), out_shape=(jax....  49.9 us
    pallas_call x1, Pallas kernels, gather_grads(): pl.pallas_call(functools.partial(grads_kernel, seqs, dps), out_shape=(jax...  44.9 us
    pallas_call x1, Pallas kernels, gather_inputs(): pl.pallas_call(functools.partial(gather_kernel, seqs, dps), out_shape=(ja...  43.4 us
    pallas_call x1, Pallas kernels, add_heads(): pl.pallas_call(functools.partial(input_kernel, seqs, dps), out_shape=(jax...  31.9 us
    pallas_call x1, Pallas kernels, attend_back(): pl.pallas_call(functools.partial(attend_back_kernel, heads, blocks, span)...  25.1 us

profile of v1, /device:TPU:0, one launch (start us, length us, event | category | flops | bytes accessed | tf_op | source)
XLA Modules:
  0.0 594.1 jit_solution(2774098823641419454)
XLA Ops:
  0.7 6.2 %broadcast_compare_fusion.19 = (pred[256,768]{1,0:T(8,128)(4,1)S(1)}, pred[256,768]{1,0:T(8,128)(4,1)S(1)}, pred[256,768]{1,0:T(8,128)(4,1)S(1)}, pred[256,768]{...) fusion(s32[768]{0:T(1024)S(1)} %iota_add_fusion), kind=kLoop, calls=%fused_computation.147 | loop fusion | flops 15925248 | bytes 6294528 | tf_op jit(solution)/shard_map/eq | solution.py:1050
  8.2 8.5 %select_select_fusion.band = f32[3,256,768]{2,1,0:T(8,128)} fusion(f32[3]{0:T(128)S(1)} %get-tuple-element.191, f32[3]{0:T(128)S(1)} %get-tuple-element.192, f32[3]{0:T(128)S(1)} %get-tuple-element.193, f32[3]{0:T(128)S(1)} %get-tuple-element.194, f32[3]{0:T(128)S(1)} %get-tuple-element.195, f32[3]{0:T(128)S(1)} %get-tuple-element.196, ...), kind=kLoop, calls=%fused_computation.55 | loop fusion | flops 18874368 | bytes 8651136 | tf_op jit(solution)/shard_map/jit(_where)/select_n | solution.py:1050
  19.1 43.4 %gather_inputs.1 = (bf16[2,4,256,768]{3,2,1,0:T(8,128)(2,1)}, bf16[4,2,96,640]{3,2,1,0:T(8,128)(2,1)}, s32[4,8,256]{2,1,0:T(8,128)}) custom-call(bf16[8,256,768]{2,1,0:T(8,128)(2,1)} %tok.1, bf16[96,640]{1,0:T(8,128)(2,1)} %concatenate.19.pack, s32[8,256]{1,0:T(8,128)} %bitcast.234), custom_call_target="tpu_custom_call" | custom-call | tf_op jit(solution)/shard_map/gather_inputs/pallas_call | solution.py:283
  63.7 2.7 multiply_reduce_fusion
  68.3 2.1 convolution_convert_fusion.3
  71.7 2.2 copy.235
  73.9 2.2 copy.236
  78.2 20.6 %attend.1 = (bf16[2,1024,192]{2,1,0:T(8,128)(2,1)}, bf16[2,3,1024,1024]{3,2,1,0:T(8,128)(2,1)}) custom-call(bf16[2,1024,192]{2,1,0:T(8,128)(2,1)} %bitcast.192, bf16[2,1024,192]{2,1,0:T(8,128)(2,1)} %bitcast.194, bf16[2,1024,192]{2,1,0:T(8,128)(2,1)} %bitcast.196, f32[3,256,768]{2,1,0:T(8,128)} %select_select_fusion.band, f32[3,2]{1,0:T(4,128)} %pad_maximum_fusion.3.far, ...), custom_call_target="tpu_custom_call" | custom-call | tf_op jit(solution)/shard_map/attend/pallas_call | solution.py:885
  100.0 54.2 %gather_heads.1 = (bf16[4,2,256,192]{3,2,1,0:T(8,128)(2,1)}, bf16[2,256,768]{2,1,0:T(8,128)(2,1)}, bf16[4,2,96,384]{3,2,1,0:T(8,128)(2,1)}, bf16[4,4,2,96,256]{4,3,2,1,0:T(8,128)(2,1)}) custom-call(bf16[2,4,256,192]{3,2,1,0:T(8,128)(2,1)} %bitcast.222, bf16[8,256,768]{2,1,0:T(8,128)(2,1)} %cot.1, bf16[96,384]{1,0:T(8,128)(2,1)} %concatenate.20.pack), custom_call_target="tpu_custom_call" | custom-call | tf_op jit(solution)/shard_map/gather_heads/pallas_call | solution.py:388
  154.2 2.1 fusion.77
  158.0 2.2 multiply_reduce_fusion.3
  163.1 2.6 fusion.102
  172.7 2.6 convolution_convert_fusion.4
  175.2 56.7 %dispatch.1 = bf16[4,2,8,80,768]{4,3,2,1,0:T(8,128)(2,1)} custom-call(bf16[2,8,80,768]{3,2,1,0:T(8,128)(2,1)} %bitcast.215), custom_call_target="tpu_custom_call" | custom-call | tf_op jit(solution)/shard_map/dispatch/pallas_call | solution.py:467
  231.9 3.7 fusion.76
  237.3 3.3 fusion.81
  240.8 10.2 %fusion.6 = (bf16[2,1280,768]{2,1,0:T(8,128)(2,1)}, f32[2,1280,768]{2,1,0:T(8,128)}) fusion(f32[2,1280,768]{2,1,0:T(8,128)S(1)} %fusion.81, bf16[2,1280,768]{2,1,0:T(8,128)(2,1)S(1)} %bitcast.205, bf16[2,768,768]{2,1,0:T(8,128)(2,1)S(1)} %copy-done), kind=kOutput, calls=%fused_computation.8 | convolution fusion | flops 3059220480 | bytes 25952256 | tf_op jit(solution)/shard_map/xrd,xdf->xrf/dot_general | solution.py:1110
  251.0 10.6 %fusion.75 = f32[2,768,768]{2,1,0:T(8,128)} fusion(bf16[2,1280,768]{2,1,0:T(8,128)(2,1)S(1)} %bitcast.204, f32[2,1280,768]{2,1,0:T(8,128)} %get-tuple-element.297), kind=kOutput, calls=%fused_computation.246 | convolution fusion | flops 3037593600 | bytes 16515072 | tf_op jit(solution)/shard_map/xrf,xrd->xfd/dot_general | solution.py:1118
  261.5 5.0 fusion.82
  266.6 7.1 %convolution_convert_fusion.1 = bf16[2,1280,768]{2,1,0:T(8,128)(2,1)S(1)} fusion(bf16[2,768,768]{2,1,0:T(8,128)(2,1)S(1)} %copy-done.89, f32[2,1280,768]{2,1,0:T(8,128)} %get-tuple-element.297), kind=kOutput, calls=%fused_computation.17 | convolution fusion | flops 3039559680 | bytes 14155776 | tf_op jit(solution)/shard_map/xrf,xfd->xrd/dot_general | solution.py:1112
  273.9 3.7 convolution_convert_fusion
  277.7 2.2 copy.250
  279.9 5.9 pad_maximum_fusion.partial
  285.8 65.0 %combine.1 = bf16[2,8,80,768]{3,2,1,0:T(8,128)(2,1)} custom-call(bf16[4,2,8,80,768]{4,3,2,1,0:T(8,128)(2,1)} %pad_maximum_fusion.partial), custom_call_target="tpu_custom_call" | custom-call | tf_op jit(solution)/shard_map/combine/pallas_call | solution.py:550
  350.8 3.1 convolution_bitcast_fusion
  355.2 2.3 multiply_reduce_fusion.1
  359.1 2.0 fusion.28
  361.1 2.2 copy.251
  363.4 44.9 %gather_grads.1 = (bf16[2,4,256,192]{3,2,1,0:T(8,128)(2,1)}, bf16[8,256,768]{2,1,0:T(8,128)(2,1)}) custom-call(bf16[4,2,256,192]{3,2,1,0:T(8,128)(2,1)} %bitcast.202, bf16[2,256,768]{2,1,0:T(8,128)(2,1)} %bitcast.212), custom_call_target="tpu_custom_call" | custom-call | tf_op jit(solution)/shard_map/gather_grads/pallas_call | solution.py:670
  408.5 25.1 %attend_back.1 = (bf16[2,1024,192]{2,1,0:T(8,128)(2,1)}, bf16[2,1024,192]{2,1,0:T(8,128)(2,1)}, bf16[2,1024,192]{2,1,0:T(8,128)(2,1)}, f32[3,256,768]{2,1,0:T(8,128)}, f32[3,2,8,256]{3,2,1,0:T(8,128)}) custom-call(bf16[2,1024,192]{2,1,0:T(8,128)(2,1)} %bitcast.193, bf16[2,1024,192]{2,1,0:T(8,128)(2,1)} %bitcast.195, bf16[2,1024,192]{2,1,0:T(8,128)(2,1)} %bitcast.197, ...), custom_call_target="tpu_custom_call" | custom-call | tf_op jit(solution)/shard_map/attend_back/pallas_call | solution.py:954
  433.7 8.1 %select_reduce_fusion = (f32[3]{0:T(128)}, f32[3]{0:T(128)}, f32[3]{0:T(128)}, f32[3]{0:T(128)}, f32[3]{0:T(128)}, /*index=5*/f32[3]{0:T(128)}, f32[3]{0:T(128)}...) fusion(f32[3,256,768]{2,1,0:T(8,128)} %get-tuple-element.73, ...), kind=kLoop, calls=%fused_computation.23 | loop fusion | flops 21233608 | bytes 5898456 | tf_op jit(solution)/shard_map/reduce_sum | solution.py:1143
  444.6 7.2 %select_reduce_fusion.18 = (f32[3]{0:T(128)}, f32[3]{0:T(128)}, f32[3]{0:T(128)}, f32[3]{0:T(128)}, f32[3]{0:T(128)}, /*index=5*/f32[3]{0:T(128)}, f32[3]{0:T(12...) fusion(f32[3,256,768]{2,1,0:T(8,128)} %get-tuple-element.73, ...), kind=kLoop, calls=%fused_computation.41 | loop fusion | flops 16515030 | bytes 5111976 | tf_op jit(solution)/shard_map/reduce_sum | solution.py:1143
  451.8 2.9 stack.168
  456.7 2.0 convolution_convert_fusion.8
  458.7 3.0 pad_maximum_fusion.1
  463.2 3.1 convolution_convert_fusion.6
  466.3 1.8 convolution_convert_fusion.5
  468.1 2.7 copy.253
  470.8 6.3 %convolution_convert_fusion.2 = bf16[2048,768]{1,0:T(8,128)(2,1)} fusion(bf16[2048,576]{1,0:T(8,128)(2,1)} %bitcast.214, bf16[768,640]{1,0:T(8,128)(2,1)} %bitcast.232), kind=kOutput, calls=%fused_computation.18 | convolution fusion | flops 1813512192 | bytes 6488064 | tf_op jit(solution)/shard_map/tk,dk->td/dot_general | solution.py:1149
  477.1 31.9 %add_heads.1 = (f32[2,256,768]{2,1,0:T(8,128)}, f32[768,192]{1,0:T(8,128)}) custom-call(bf16[2,4,256,768]{3,2,1,0:T(8,128)(2,1)} %bitcast.210, bf16[4,768,192]{2,1,0:T(8,128)(2,1)} %bitcast.199), custom_call_target="tpu_custom_call" | custom-call | tf_op jit(solution)/shard_map/add_heads/pallas_call | solution.py:732
  511.3 2.0 fusion.21
  514.1 9.3 %concatenate.22 = bf16[768,896]{0,1:T(8,128)(2,1)} concatenate(bf16[768,576]{0,1:T(8,128)(2,1)} %convolution_convert_fusion.6, bf16[768,192]{0,1:T(8,128)(2,1)S(1)} %copy-done.62, bf16[768,16]{0,1:T(8,128)(2,1)S(1)} %copy-done.68, bf16[768,1]{0,1:T(2,128)(2,1)S(1)} %broadcast_in_dim.815, bf16[768,1]{0,1:T(2,128)(2,1)S(1)} %broadcast_in_dim.816, bf16[768,110]{0,1:T(8,128)(2,1)} %broadcast_in_dim.817), dimensions={1} | concatenate | bytes 2752512 | tf_op jit(solution)/shard_map/concatenate | solution.py:1164
  523.4 2.5 copy.255
  525.9 2.6 copy.280
  528.6 2.8 fusion.11
  531.3 49.9 %finish_grads.1 = (bf16[8,256,768]{2,1,0:T(8,128)(2,1)}, f32[96,896]{1,0:T(8,128)}, f32[32,128]{1,0:T(8,128)}) custom-call(bf16[2,256,768]{2,1,0:T(8,128)(2,1)} %bitcast.209, bf16[2,4,96,896]{3,2,1,0:T(8,128)(2,1)} %bitcast.200, f32[32,128]{1,0:T(8,128)} %pad.8.bias), custom_call_target="tpu_custom_call" | custom-call | tf_op jit(solution)/shard_map/finish_grads/pallas_call | solution.py:819
  581.3 1.9 slice_bitcast_fusion.2
  588.3 3.9 copy.286
  (261 shorter events, 43.3 us)
Async XLA Ops:
  0.6 240.2 %copy-start = (bf16[2,768,768]{2,1,0:T(8,128)(2,1)S(1)}, bf16[2,768,768]{2,1,0:T(8,128)(2,1)}, u32[]{:S(2)}) copy-start(bf16[2,768,768]{2,1,0:T(8,128)(2,1)} %param.29) | copy-start | bytes 7077892
  6.9 9.8 %copy-start.12 = (pred[256,768]{1,0:T(8,128)(4,1)}, pred[256,768]{1,0:T(8,128)(4,1)S(1)}, u32[]{:S(2)}) copy-start(pred[256,768]{1,0:T(8,128)(4,1)S(1)} %get-tuple-element.259) | copy-start | bytes 589828
  6.9 9.8 %copy-start.13 = (pred[256,768]{1,0:T(8,128)(4,1)}, pred[256,768]{1,0:T(8,128)(4,1)S(1)}, u32[]{:S(2)}) copy-start(pred[256,768]{1,0:T(8,128)(4,1)S(1)} %get-tuple-element.260) | copy-start | bytes 589828
  6.9 9.8 %copy-start.14 = (pred[256,768]{1,0:T(8,128)(4,1)}, pred[256,768]{1,0:T(8,128)(4,1)S(1)}, u32[]{:S(2)}) copy-start(pred[256,768]{1,0:T(8,128)(4,1)S(1)} %get-tuple-element.261) | copy-start | bytes 589828
  6.9 9.8 %copy-start.15 = (pred[256,768]{1,0:T(8,128)(4,1)}, pred[256,768]{1,0:T(8,128)(4,1)S(1)}, u32[]{:S(2)}) copy-start(pred[256,768]{1,0:T(8,128)(4,1)S(1)} %get-tuple-element.262) | copy-start | bytes 589828
  6.9 9.8 %copy-start.16 = (pred[256,768]{1,0:T(8,128)(4,1)}, pred[256,768]{1,0:T(8,128)(4,1)S(1)}, u32[]{:S(2)}) copy-start(pred[256,768]{1,0:T(8,128)(4,1)S(1)} %get-tuple-element.263) | copy-start | bytes 589828
  6.9 9.8 %copy-start.17 = (pred[256,768]{1,0:T(8,128)(4,1)}, pred[256,768]{1,0:T(8,128)(4,1)S(1)}, u32[]{:S(2)}) copy-start(pred[256,768]{1,0:T(8,128)(4,1)S(1)} %get-tuple-element.264) | copy-start | bytes 589828
  6.9 9.8 %copy-start.18 = (pred[256,768]{1,0:T(8,128)(4,1)}, pred[256,768]{1,0:T(8,128)(4,1)S(1)}, u32[]{:S(2)}) copy-start(pred[256,768]{1,0:T(8,128)(4,1)S(1)} %get-tuple-element.265) | copy-start | bytes 589828
  6.9 9.8 %copy-start.19 = (pred[256,768]{1,0:T(8,128)(4,1)}, pred[256,768]{1,0:T(8,128)(4,1)S(1)}, u32[]{:S(2)}) copy-start(pred[256,768]{1,0:T(8,128)(4,1)S(1)} %get-tuple-element.266) | copy-start | bytes 589828
  6.9 9.8 %copy-start.20 = (pred[256,768]{1,0:T(8,128)(4,1)}, pred[256,768]{1,0:T(8,128)(4,1)S(1)}, u32[]{:S(2)}) copy-start(pred[256,768]{1,0:T(8,128)(4,1)S(1)} %get-tuple-element.267) | copy-start | bytes 589828
  7.0 9.8 %copy-start.21 = (pred[256,768]{1,0:T(8,128)(4,1)}, pred[256,768]{1,0:T(8,128)(4,1)S(1)}, u32[]{:S(2)}) copy-start(pred[256,768]{1,0:T(8,128)(4,1)S(1)} %get-tuple-element.268) | copy-start | bytes 589828
  7.0 9.8 %copy-start.22 = (pred[256,768]{1,0:T(8,128)(4,1)}, pred[256,768]{1,0:T(8,128)(4,1)S(1)}, u32[]{:S(2)}) copy-start(pred[256,768]{1,0:T(8,128)(4,1)S(1)} %get-tuple-element.269) | copy-start | bytes 589828
  7.0 9.8 %copy-start.23 = (pred[256,768]{1,0:T(8,128)(4,1)}, pred[256,768]{1,0:T(8,128)(4,1)S(1)}, u32[]{:S(2)}) copy-start(pred[256,768]{1,0:T(8,128)(4,1)S(1)} %get-tuple-element.270) | copy-start | bytes 589828
  7.0 9.8 %copy-start.24 = (pred[256,768]{1,0:T(8,128)(4,1)}, pred[256,768]{1,0:T(8,128)(4,1)S(1)}, u32[]{:S(2)}) copy-start(pred[256,768]{1,0:T(8,128)(4,1)S(1)} %get-tuple-element.239) | copy-start | bytes 589828
  7.0 9.8 %copy-start.26 = (pred[256,768]{1,0:T(8,128)(4,1)}, pred[256,768]{1,0:T(8,128)(4,1)S(1)}, u32[]{:S(2)}) copy-start(pred[256,768]{1,0:T(8,128)(4,1)S(1)} %get-tuple-element.240) | copy-start | bytes 589828
  7.0 9.8 %copy-start.28 = (pred[256,768]{1,0:T(8,128)(4,1)}, pred[256,768]{1,0:T(8,128)(4,1)S(1)}, u32[]{:S(2)}) copy-start(pred[256,768]{1,0:T(8,128)(4,1)S(1)} %get-tuple-element.241) | copy-start | bytes 589828
  7.0 9.8 %copy-start.30 = (pred[256,768]{1,0:T(8,128)(4,1)}, pred[256,768]{1,0:T(8,128)(4,1)S(1)}, u32[]{:S(2)}) copy-start(pred[256,768]{1,0:T(8,128)(4,1)S(1)} %get-tuple-element.242) | copy-start | bytes 589828
  7.0 9.8 %copy-start.32 = (pred[256,768]{1,0:T(8,128)(4,1)}, pred[256,768]{1,0:T(8,128)(4,1)S(1)}, u32[]{:S(2)}) copy-start(pred[256,768]{1,0:T(8,128)(4,1)S(1)} %get-tuple-element.243) | copy-start | bytes 589828
  7.0 9.8 %copy-start.34 = (pred[256,768]{1,0:T(8,128)(4,1)}, pred[256,768]{1,0:T(8,128)(4,1)S(1)}, u32[]{:S(2)}) copy-start(pred[256,768]{1,0:T(8,128)(4,1)S(1)} %get-tuple-element.244) | copy-start | bytes 589828
  7.0 9.8 %copy-start.36 = (pred[256,768]{1,0:T(8,128)(4,1)}, pred[256,768]{1,0:T(8,128)(4,1)S(1)}, u32[]{:S(2)}) copy-start(pred[256,768]{1,0:T(8,128)(4,1)S(1)} %get-tuple-element.245) | copy-start | bytes 589828
  7.1 9.8 %copy-start.38 = (pred[256,768]{1,0:T(8,128)(4,1)}, pred[256,768]{1,0:T(8,128)(4,1)S(1)}, u32[]{:S(2)}) copy-start(pred[256,768]{1,0:T(8,128)(4,1)S(1)} %get-tuple-element.246) | copy-start | bytes 589828
  7.1 9.8 %copy-start.40 = (pred[256,768]{1,0:T(8,128)(4,1)}, pred[256,768]{1,0:T(8,128)(4,1)S(1)}, u32[]{:S(2)}) copy-start(pred[256,768]{1,0:T(8,128)(4,1)S(1)} %get-tuple-element.247) | copy-start | bytes 589828
  7.1 9.8 %copy-start.42 = (pred[256,768]{1,0:T(8,128)(4,1)}, pred[256,768]{1,0:T(8,128)(4,1)S(1)}, u32[]{:S(2)}) copy-start(pred[256,768]{1,0:T(8,128)(4,1)S(1)} %get-tuple-element.248) | copy-start | bytes 589828
  7.1 9.8 %copy-start.44 = (pred[256,768]{1,0:T(8,128)(4,1)}, pred[256,768]{1,0:T(8,128)(4,1)S(1)}, u32[]{:S(2)}) copy-start(pred[256,768]{1,0:T(8,128)(4,1)S(1)} %get-tuple-element.249) | copy-start | bytes 589828
  8.2 10.4 %copy-start.84 = (s32[8,256,1]{1,2,0:T(1,128)S(1)}, s32[8,256,1]{1,2,0:T(1,128)}, u32[]{:S(2)}) copy-start(s32[8,256,1]{1,2,0:T(1,128)} %param.20) | copy-start | bytes 24580
  78.2 20.7 %copy-start.74 = (bf16[192,96]{1,0:T(8,128)(2,1)S(1)}, bf16[192,96]{1,0:T(8,128)(2,1)}, u32[]{:S(2)}) copy-start(bf16[192,96]{1,0:T(8,128)(2,1)} %param.25) | copy-start | bytes 110596
  78.2 20.8 %copy-start.85 = (bf16[96,16]{0,1:T(8,128)(2,1)S(1)}, bf16[96,16]{0,1:T(8,128)(2,1)}, u32[]{:S(2)}) copy-start(bf16[96,16]{0,1:T(8,128)(2,1)} %param.28) | copy-start | bytes 9220
  78.2 20.9 %copy-start.88 = (bf16[96]{0:T(256)(128)(2,1)S(1)}, bf16[96]{0:T(256)(128)(2,1)}, u32[]{:S(2)}) copy-start(bf16[96]{0:T(256)(128)(2,1)} %param.27) | copy-start | bytes 580
  251.0 10.6 %copy-start.91 = (bf16[2,1280,768]{2,1,0:T(8,128)(2,1)S(1)}, bf16[2,1280,768]{2,1,0:T(8,128)(2,1)}, u32[]{:S(2)}) copy-start(bf16[2,1280,768]{2,1,0:T(8,128)(2,1)} %get-tuple-element.296) | copy-start | bytes 11796484
  408.3 25.3 %copy-start.25 = (pred[256,768]{1,0:T(8,128)(4,1)S(1)}, pred[256,768]{1,0:T(8,128)(4,1)}, u32[]{:S(2)}) copy-start(pred[256,768]{1,0:T(8,128)(4,1)} %copy-done.24) | copy-start | bytes 589828
  408.3 25.3 %copy-start.27 = (pred[256,768]{1,0:T(8,128)(4,1)S(1)}, pred[256,768]{1,0:T(8,128)(4,1)}, u32[]{:S(2)}) copy-start(pred[256,768]{1,0:T(8,128)(4,1)} %copy-done.26) | copy-start | bytes 589828
  408.3 25.3 %copy-start.29 = (pred[256,768]{1,0:T(8,128)(4,1)S(1)}, pred[256,768]{1,0:T(8,128)(4,1)}, u32[]{:S(2)}) copy-start(pred[256,768]{1,0:T(8,128)(4,1)} %copy-done.28) | copy-start | bytes 589828
  408.3 25.3 %copy-start.31 = (pred[256,768]{1,0:T(8,128)(4,1)S(1)}, pred[256,768]{1,0:T(8,128)(4,1)}, u32[]{:S(2)}) copy-start(pred[256,768]{1,0:T(8,128)(4,1)} %copy-done.30) | copy-start | bytes 589828
  408.3 25.3 %copy-start.33 = (pred[256,768]{1,0:T(8,128)(4,1)S(1)}, pred[256,768]{1,0:T(8,128)(4,1)}, u32[]{:S(2)}) copy-start(pred[256,768]{1,0:T(8,128)(4,1)} %copy-done.32) | copy-start | bytes 589828
  408.3 25.3 %copy-start.35 = (pred[256,768]{1,0:T(8,128)(4,1)S(1)}, pred[256,768]{1,0:T(8,128)(4,1)}, u32[]{:S(2)}) copy-start(pred[256,768]{1,0:T(8,128)(4,1)} %copy-done.34) | copy-start | bytes 589828
  408.3 25.3 %copy-start.37 = (pred[256,768]{1,0:T(8,128)(4,1)S(1)}, pred[256,768]{1,0:T(8,128)(4,1)}, u32[]{:S(2)}) copy-start(pred[256,768]{1,0:T(8,128)(4,1)} %copy-done.36) | copy-start | bytes 589828
  408.3 25.3 %copy-start.39 = (pred[256,768]{1,0:T(8,128)(4,1)S(1)}, pred[256,768]{1,0:T(8,128)(4,1)}, u32[]{:S(2)}) copy-start(pred[256,768]{1,0:T(8,128)(4,1)} %copy-done.38) | copy-start | bytes 589828
  408.4 25.3 %copy-start.41 = (pred[256,768]{1,0:T(8,128)(4,1)S(1)}, pred[256,768]{1,0:T(8,128)(4,1)}, u32[]{:S(2)}) copy-start(pred[256,768]{1,0:T(8,128)(4,1)} %copy-done.40) | copy-start | bytes 589828
  408.4 25.3 %copy-start.43 = (pred[256,768]{1,0:T(8,128)(4,1)S(1)}, pred[256,768]{1,0:T(8,128)(4,1)}, u32[]{:S(2)}) copy-start(pred[256,768]{1,0:T(8,128)(4,1)} %copy-done.42) | copy-start | bytes 589828
  408.4 25.3 %copy-start.45 = (pred[256,768]{1,0:T(8,128)(4,1)S(1)}, pred[256,768]{1,0:T(8,128)(4,1)}, u32[]{:S(2)}) copy-start(pred[256,768]{1,0:T(8,128)(4,1)} %copy-done.44) | copy-start | bytes 589828
  408.4 25.3 %copy-start.47 = (pred[256,768]{1,0:T(8,128)(4,1)S(1)}, pred[256,768]{1,0:T(8,128)(4,1)}, u32[]{:S(2)}) copy-start(pred[256,768]{1,0:T(8,128)(4,1)} %copy-done.46) | copy-start | bytes 589828
  408.4 25.3 %copy-start.49 = (pred[256,768]{1,0:T(8,128)(4,1)S(1)}, pred[256,768]{1,0:T(8,128)(4,1)}, u32[]{:S(2)}) copy-start(pred[256,768]{1,0:T(8,128)(4,1)} %copy-done.48) | copy-start | bytes 589828
  408.4 25.3 %copy-start.51 = (pred[256,768]{1,0:T(8,128)(4,1)S(1)}, pred[256,768]{1,0:T(8,128)(4,1)}, u32[]{:S(2)}) copy-start(pred[256,768]{1,0:T(8,128)(4,1)} %copy-done.50) | copy-start | bytes 589828
  408.4 25.3 %copy-start.53 = (pred[256,768]{1,0:T(8,128)(4,1)S(1)}, pred[256,768]{1,0:T(8,128)(4,1)}, u32[]{:S(2)}) copy-start(pred[256,768]{1,0:T(8,128)(4,1)} %copy-done.52) | copy-start | bytes 589828
  408.4 25.3 %copy-start.55 = (pred[256,768]{1,0:T(8,128)(4,1)S(1)}, pred[256,768]{1,0:T(8,128)(4,1)}, u32[]{:S(2)}) copy-start(pred[256,768]{1,0:T(8,128)(4,1)} %copy-done.54) | copy-start | bytes 589828
  408.4 25.3 %copy-start.57 = (pred[256,768]{1,0:T(8,128)(4,1)S(1)}, pred[256,768]{1,0:T(8,128)(4,1)}, u32[]{:S(2)}) copy-start(pred[256,768]{1,0:T(8,128)(4,1)} %copy-done.56) | copy-start | bytes 589828
  408.4 25.3 %copy-start.59 = (pred[256,768]{1,0:T(8,128)(4,1)S(1)}, pred[256,768]{1,0:T(8,128)(4,1)}, u32[]{:S(2)}) copy-start(pred[256,768]{1,0:T(8,128)(4,1)} %copy-done.58) | copy-start | bytes 589828
  444.6 12.1 %copy-start.77 = (f32[512]{0:T(512)S(1)}, f32[512]{0:T(512)}, u32[]{:S(2)}) copy-start(f32[512]{0:T(512)} %copy-done.76) | copy-start | bytes 6148
  (44 other events, 191.8 us)

commit v2 on v1

--- a/solution.py
+++ b/solution.py
@@ -177,393 +177,540 @@
     ]
 
 
-CHUNKS = 2
-
-
-def gather_kernel(
-    seqs, dps, tok, pack, ids, tok_all, pack_all, ids_all, ls, z_send, z_recv, h_send, h_recv, i_send, i_recv, *sems
+def spread_hot(at, shard, width):
+    row = lax.broadcasted_iota(jnp.int32, (128, width), 0)
+    column = lax.broadcasted_iota(jnp.int32, (128, width), 1)
+    return ((column == row + at) & (row < shard)).astype(BF16)
+
+
+def squeeze_hot(shard, padded, rows, count):
+    row = lax.broadcasted_iota(jnp.int32, (rows, count * padded), 0)
+    column = lax.broadcasted_iota(jnp.int32, (rows, count * padded), 1)
+    inside = lax.rem(column, padded)
+    return ((lax.div(column, padded) * shard + inside == row) & (inside < shard)).astype(BF16)
+
+
+CHUNKS = 4
+
+
+def front_kernel(
+    seqs, dps, heads,
+    tok, cot, wq, wk, wv, wo, router, gain_a, gain_f, ids, table, lengths,
+    attn_input, weights, split_out, probs, heads_all, own_tok, cot_own, wo_all, gains, ids_all,
+    tok_all, pack, pack_all, wo_pad, wo_parts, tile, tile_all, split, ext, slot, out,
+    p_sem, ls, z_send, z_recv, h_send, h_recv, c_send, c_recv, a_send, a_recv, w_send, w_recv, i_send, i_recv, *line
 ):
     me = Place(seqs, dps)
     h, s, d = me.h, me.s, me.d
-    per = tok.shape[0] // seqs
-    rows = tok.shape[1] // CHUNKS
-    own_copies = [pltpu.make_async_copy(tok.at[per * s + j], tok_all.at[j, s], ls.at[j]) for j in range(per)]
-    own_copies.append(pltpu.make_async_copy(pack, pack_all.at[s, d], ls.at[per]))
-    own_copies.append(pltpu.make_async_copy(ids, ids_all.at[s], ls.at[per + 1]))
+    per, blocks, span, width = tok_all.shape
+    length = blocks * span
+    shard, local = wq.shape
+    groups = seqs * dps
+    experts = router.shape[1]
+    part_rows = span // CHUNKS
+    half = CHUNKS // 2
+    pack[...] = jnp.zeros_like(pack)
+    for n, ref in enumerate((wq, wk, wv)):
+        pack[:shard, n * local : (n + 1) * local] = ref[...]
+    pack[:shard, 3 * local : 3 * local + experts] = router[...]
+    wo_pad[...] = jnp.zeros_like(wo_pad)
+    wo_pad[:, :shard] = wo[...]
+    tile[...] = jnp.zeros_like(tile)
+    tile[0:1, :shard] = gain_a[...].astype(F32)
+    tile[1:2, :shard] = gain_f[...].astype(F32)
+    greet(
+        me.seq_peers()
+        + [{"head": me.near} | peer for peer in me.seq_peers()]
+        + me.dp_peers()
+        + [{"head": mod(h + i, 4)} for i in range(1, 4)]
+    )
+    lines = [
+        line_gather(me, pack, pack_all, line[0:4], 0),
+        line_gather(me, tile, tile_all, line[4:8], 0),
+        line_gather(me, wo_pad, wo_parts, line[8:12], 0),
+    ]
+    own_copies = [
+        pltpu.make_async_copy(pack, pack_all.at[s, d], ls.at[0]),
+        pltpu.make_async_copy(tile, tile_all.at[s, d], ls.at[1]),
+        pltpu.make_async_copy(wo_pad, wo_parts.at[s, d], ls.at[2]),
+        pltpu.make_async_copy(ids, ids_all.at[s], ls.at[3]),
+    ]
+    for j in range(per):
+        own_copies.append(pltpu.make_async_copy(tok.at[per * s + j], tok_all.at[j, s], ls.at[4 + j]))
     for copy in own_copies:
         copy.start()
-    greet(me.seq_peers() + me.dp_peers() + me.head_pair())
-    start, step, finish = line_gather(me, pack, pack_all, sems, 0)
-    start()
-    turn = mod(h - s, 4)
-    mine = lax.rem(turn, 2) == 0
-    which = lax.div(turn, 2)
+    for start, _, _ in lines:
+        start()
     for i in range(1, seqs):
-        to = mod(s + i, seqs)
-        send(ids, ids_all.at[s], i_send.at[i - 1], i_recv.at[i - 1], seq=to)
-
-    @pl.when(mine)
-    def _():
-        for c in range(CHUNKS):
-            for i in range(1, seqs):
+        send(ids, ids_all.at[s], i_send.at[i - 1], i_recv.at[i - 1], seq=mod(s + i, seqs))
+
+    owns = lax.rem(mod(h - s, 4), 2) == 0
+    target = jnp.where(owns, h, me.near)
+    which = lax.div(mod(target - s, 4), 2)
+    first = jnp.where(owns, 0, half)
+
+    def chunk(c):
+        return pl.ds(pl.multiple_of(c * part_rows, part_rows), part_rows)
+
+    for c in range(half):
+        for i in range(1, seqs):
+            to = mod(s + i, seqs)
+            rows = chunk(first + c)
+            send(
+                tok.at[per * to + which, rows],
+                tok_all.at[which, s, rows],
+                z_send.at[i - 1, c],
+                z_recv.at[which, first + c],
+                head=target,
+                seq=to,
+            )
+        for _, step, _ in lines:
+            step(c + 1)
+
+    def build_bias(head):
+        turn = lax.broadcasted_iota(jnp.int32, (8, 4 * span), 1)
+        bucket = bucket_of(jnp.where(turn < 3 * span, turn, turn - 4 * span) - span, table.shape[0])
+        row = jnp.zeros((8, 4 * span), F32)
+        for b in range(table.shape[0]):
+            row = jnp.where(bucket == b, table[b, head], row)
+        rolled = pltpu.roll(jnp.broadcast_to(row[0:1], (span, 4 * span)), 0, 1, stride=1, stride_axis=0)
+        ext[head, :, 2 * span : 5 * span] = rolled[:, : 3 * span]
+        ext[head, :, : 2 * span] = jnp.broadcast_to(row[0:1, 0:1], (span, 2 * span))
+        ext[head, :, 5 * span :] = jnp.broadcast_to(row[0:1, 3 * span - 1 : 3 * span], (span, 2 * span))
+
+    build_bias(0)
+    for _, step, _ in lines:
+        for t in range(half + 1, seqs):
+            step(t)
+    for head in range(1, heads):
+        build_bias(head)
+
+    def at(j, c, head):
+        return tok_all.at[j, me.block(j, head), chunk(c)]
+
+    for c in range(half):
+        for part in range(2):
+            for j in range(per):
+                k = part * half + c
+                here = at(j, k, h)
+
+                @pl.when(me.block(j) != s)
+                def _():
+                    arrived(here, z_recv.at[j, k])
+                    send(here, here, h_send.at[0, j, k], h_recv.at[0, j, k], head=me.across)
+                    send(here, here, h_send.at[1, j, k], h_recv.at[1, j, k], head=me.near)
+
+    for copy in own_copies:
+        copy.wait()
+    for _, _, finish in lines:
+        finish()
+    if shard % 16:
+        whole = pack_all[...].reshape(groups * pack.shape[0], pack.shape[1])
+        hot = squeeze_hot(shard, pack.shape[0], width, groups)
+        weights[...] = jnp.dot(hot, whole, preferred_element_type=F32).astype(BF16)
+    else:
+        weights[...] = pack_all[...].reshape(width, pack.shape[1])
+    row = jnp.zeros((8, width), F32)
+    for g in range(groups):
+        piece = tile_all[g // dps, g % dps].astype(BF16)
+        row = row + jnp.dot(piece, spread_hot(g * shard, shard, width), preferred_element_type=F32)
+    gains[...] = row
+
+    def project(j, block):
+        rows = pl.ds(pl.multiple_of(block * span, span), span)
+        x = tok_all[j, block].astype(F32)
+        normed = (x * lax.rsqrt(jnp.mean(x * x, axis=-1, keepdims=True) + EPS) * gains[0:1, :]).astype(BF16)
+        attn_input[j, rows, :] = normed
+        parts = jnp.dot(normed, weights[...], preferred_element_type=F32).astype(BF16)
+        for n in range(3 * heads):
+            split[j, n, rows, :] = parts[:, n * HEAD_DIM : (n + 1) * HEAD_DIM]
+
+    for c in range(half):
+        for part in range(2):
+            for j in range(per):
+                k = part * half + c
+                there = at(j, k, me.across)
+
+                @pl.when(me.block(j, me.across) != s)
+                def _():
+                    arrived(there, h_recv.at[0, j, k])
+                    send(there, there, h_send.at[2, j, k], h_recv.at[2, j, k], head=me.near)
+
+    @pl.loop(0, 4 * per)
+    def _(n):
+        hop, j = lax.div(n, per), lax.rem(n, per)
+        source = jnp.where(hop == 0, h, jnp.where(hop == 1, me.across, jnp.where(hop == 2, me.near, me.near_across)))
+        block = mod(source + 2 * j, 4)
+
+        @pl.when((hop >= 2) & (block != s))
+        def _():
+            for k in range(CHUNKS):
+                arrived(tok_all.at[j, block, chunk(k)], h_recv.at[hop - 1, j, k])
+
+        project(j, block)
+
+    out_split = pltpu.make_async_copy(split, split_out, ls.at[4 + per])
+    out_split.start()
+    own_tokens = [pltpu.make_async_copy(tok_all.at[j, me.block(j)], own_tok.at[j], ls.at[4 + j]) for j in range(per)]
+    for copy in own_tokens:
+        copy.start()
+    total = jnp.zeros((local, width), F32)
+    for g in range(groups):
+        total = total + jnp.dot(
+            wo_parts[g // dps, g % dps], spread_hot(g * shard, shard, width), preferred_element_type=F32
+        )
+    wo_all[h] = total.astype(BF16)
+    send(wo_all.at[h], wo_all.at[h], w_send.at[0], w_recv.at[0], head=me.across)
+    send(wo_all.at[h], wo_all.at[h], w_send.at[1], w_recv.at[1], head=me.near)
+
+    @pl.loop(0, per * blocks)
+    def _(unit):
+        j, block = lax.div(unit, blocks), lax.rem(unit, blocks)
+        rows = pl.ds(pl.multiple_of(block * span, span), span)
+        turn = lax.rem(unit, 2)
+
+        @pl.when(unit >= 2)
+        def _():
+            pltpu.make_async_copy(slot.at[turn], slot.at[turn], p_sem.at[turn]).wait()
+
+        window = pl.ds(pl.multiple_of((blocks - 1 - block) * span, span), length)
+        valid = lax.broadcasted_iota(jnp.int32, (1, length), 1) < lengths[per * s + j]
+        for head in range(heads):
+            query, key, value = split[j, head, rows, :], split[j, heads + head], split[j, 2 * heads + head]
+            scores = lax.dot_general(query, key, (((1,), (1,)), ((), ())), preferred_element_type=F32)
+            scores = jnp.where(valid, scores + ext[head, :, window], -1e30)
+            top = jnp.max(scores, axis=-1, keepdims=True)
+            grown = jnp.exp(scores - top)
+            total = jnp.sum(grown, axis=-1, keepdims=True)
+            part = (grown * (1.0 / total)).astype(BF16)
+            slot[turn, head] = part
+            mixed = jnp.dot(part, value, preferred_element_type=F32)
+            out[unit, :, head * HEAD_DIM : (head + 1) * HEAD_DIM] = mixed.astype(BF16)
+        pltpu.make_async_copy(slot.at[turn], probs.at[j, :, rows, :], p_sem.at[turn]).start()
+        owner = mod(block - 2 * j, 4)
+        away = mod(owner - h, 4)
+
+        @pl.when(away == 0)
+        def _():
+            pltpu.make_async_copy(out.at[unit], heads_all.at[h, j], ls.at[j]).start()
+
+        @pl.when(away > 0)
+        def _():
+            send(out.at[unit], heads_all.at[h, j], a_send.at[away - 1, j], a_recv.at[away - 1, j], head=owner)
+
+        for i in range(1, seqs):
+
+            @pl.when(unit == i - 1)
+            def _():
                 to = mod(s + i, seqs)
-                part = pl.ds(c * rows, rows)
+                half_rows = pl.ds(pl.multiple_of(first * part_rows, part_rows), half * part_rows)
                 send(
-                    tok.at[per * to + which, part],
-                    tok_all.at[which, s, part],
-                    z_send.at[i - 1, c],
-                    z_recv.at[which, c],
+                    cot.at[per * to + which, half_rows],
+                    cot_own.at[which, half_rows],
+                    c_send.at[i - 1],
+                    c_recv.at[which, lax.div(first, half)],
+                    head=target,
                     seq=to,
                 )
 
-    def at(j, c, head):
-        return tok_all.at[j, me.block(j, head), pl.ds(c * rows, rows)]
-
-    for t in range(1, seqs):
-        step(t)
-    for c in range(CHUNKS):
-        for j in range(per):
-            here = at(j, c, h)
+        @pl.when(unit == seqs)
+        def _():
+            there = wo_all.at[me.across]
+            arrived(there, w_recv.at[0])
+            send(there, there, w_send.at[2], w_recv.at[2], head=me.near)
+
+    out_split.wait()
+    for copy in own_tokens:
+        copy.wait()
+    for turn in range(2):
+        pltpu.make_async_copy(slot.at[turn], slot.at[turn], p_sem.at[turn]).wait()
+    for j in range(per):
+        block = me.block(j)
+
+        @pl.when(block == s)
+        def _():
+            own = pltpu.make_async_copy(cot.at[per * s + j], cot_own.at[j], ls.at[2 + j])
+            own.start()
+            own.wait()
+
+        @pl.when(block != s)
+        def _():
+            for part in range(2):
+                arrived(cot_own.at[j, pl.ds(part * half * part_rows, half * part_rows)], c_recv.at[j, part])
+
+        pltpu.make_async_copy(out.at[0], heads_all.at[h, j], ls.at[j]).wait()
+        for i in range(1, 4):
+            pltpu.make_async_copy(out.at[0], out.at[0], a_send.at[i - 1, j]).wait()
+            arrived(heads_all.at[mod(h - i, 4), j], a_recv.at[i - 1, j])
+        for k in range(CHUNKS):
+            here = at(j, k, h)
 
             @pl.when(me.block(j) != s)
             def _():
-                arrived(here, z_recv.at[j, c])
-                send(here, here, h_send.at[0, j, c], h_recv.at[0, j, c], head=me.across)
-                send(here, here, h_send.at[1, j, c], h_recv.at[1, j, c], head=me.near)
-
-    for c in range(CHUNKS):
-        for j in range(per):
-            there = at(j, c, me.across)
+                for n in range(2):
+                    pltpu.make_async_copy(here, here, h_send.at[n, j, k]).wait()
 
             @pl.when(me.block(j, me.across) != s)
             def _():
-                arrived(there, h_recv.at[0, j, c])
-                send(there, there, h_send.at[2, j, c], h_recv.at[2, j, c], head=me.near)
-
-    for c in range(CHUNKS):
-        for j in range(per):
-            here = at(j, c, h)
-
-            @pl.when(me.block(j) != s)
-            def _():
-                for k in range(2):
-                    pltpu.make_async_copy(here, here, h_send.at[k, j, c]).wait()
-
-            @pl.when(me.block(j, me.across) != s)
-            def _():
-                pltpu.make_async_copy(here, here, h_send.at[2, j, c]).wait()
-
-            @pl.when(me.block(j, me.near) != s)
-            def _():
-                arrived(at(j, c, me.near), h_recv.at[1, j, c])
-
-            @pl.when(me.block(j, me.near_across) != s)
-            def _():
-                arrived(at(j, c, me.near_across), h_recv.at[2, j, c])
+                pltpu.make_async_copy(here, here, h_send.at[2, j, k]).wait()
 
     for i in range(1, seqs):
+        for c in range(half):
+            rows = tok.at[0, pl.ds(0, part_rows)]
+            pltpu.make_async_copy(rows, rows, z_send.at[i - 1, c]).wait()
+        rows = cot.at[0, pl.ds(0, half * part_rows)]
+        pltpu.make_async_copy(rows, rows, c_send.at[i - 1]).wait()
+        pltpu.make_async_copy(ids, ids, i_send.at[i - 1]).wait()
         arrived(ids_all.at[mod(s - i, seqs)], i_recv.at[i - 1])
-        pltpu.make_async_copy(ids, ids, i_send.at[i - 1]).wait()
-
-    @pl.when(mine)
-    def _():
-        for c in range(CHUNKS):
-            for i in range(1, seqs):
-                part = tok.at[0, pl.ds(c * rows, rows)]
-                pltpu.make_async_copy(part, part, z_send.at[i - 1, c]).wait()
-
-    finish()
-    for copy in own_copies:
-        copy.wait()
-
-
-def gather_inputs(tokens, pack, ids, seqs, dps):
+    for k in range(3):
+        pltpu.make_async_copy(wo_all.at[h], wo_all.at[h], w_send.at[k]).wait()
+    arrived(wo_all.at[me.near], w_recv.at[1])
+    arrived(wo_all.at[me.near_across], w_recv.at[2])
+
+
+def front(tokens, cot, wq, wk, wv, wo, router, gain_a, gain_f, ids, table, lengths, seqs, dps):
     seq_local, span, width = tokens.shape
     per = seq_local // seqs
+    length = seqs * span
+    shard, local = wq.shape
+    heads = local // HEAD_DIM
+    lanes = up_to(3 * local + router.shape[1], 128)
+    padded = up_to(shard, 16)
+    smem = pl.BlockSpec(memory_space=pltpu.SMEM)
     return pl.pallas_call(
-        functools.partial(gather_kernel, seqs, dps),
+        functools.partial(front_kernel, seqs, dps, heads),
         out_shape=(
-            jax.ShapeDtypeStruct((per, seqs, span, width), BF16),
-            jax.ShapeDtypeStruct((seqs, dps) + pack.shape, BF16),
+            jax.ShapeDtypeStruct((per, length, width), BF16),
+            jax.ShapeDtypeStruct((width, lanes), BF16),
+            jax.ShapeDtypeStruct((per, 3 * heads, length, HEAD_DIM), BF16),
+            jax.ShapeDtypeStruct((per, heads, length, length), BF16),
+            jax.ShapeDtypeStruct((4, per, span, local), BF16),
+            jax.ShapeDtypeStruct((per, span, width), BF16),
+            jax.ShapeDtypeStruct((per, span, width), BF16),
+            jax.ShapeDtypeStruct((4, local, width), BF16),
+            jax.ShapeDtypeStruct((8, width), F32),
             jax.ShapeDtypeStruct((seqs,) + ids.shape, jnp.int32),
         ),
-        in_specs=[ANY] * 3,
-        out_specs=[ANY] * 3,
+        in_specs=[ANY] * 2 + [VMEM] * 7 + [ANY, smem, smem],
+        out_specs=[VMEM] * 2 + [ANY] * 5 + [VMEM] * 2 + [ANY],
         scratch_shapes=[
-            DMA((per + 2,)),
-            DMA((seqs - 1, CHUNKS)),
+            pltpu.VMEM((per, seqs, span, width), BF16),
+            pltpu.VMEM((padded, lanes), BF16),
+            pltpu.VMEM((seqs, dps, padded, lanes), BF16),
+            pltpu.VMEM((local, 128), BF16),
+            pltpu.VMEM((seqs, dps, local, 128), BF16),
+            pltpu.VMEM((8, 128), F32),
+            pltpu.VMEM((seqs, dps, 8, 128), F32),
+            pltpu.VMEM((per, 3 * heads, length, HEAD_DIM), BF16),
+            pltpu.VMEM((heads, span, 7 * span), F32),
+            pltpu.VMEM((2, heads, span, length), BF16),
+            pltpu.VMEM((per * seqs, span, local), BF16),
+            DMA((2,)),
+            DMA((5 + per,)),
+            DMA((seqs - 1, CHUNKS // 2)),
             DMA((per, CHUNKS)),
             DMA((3, per, CHUNKS)),
             DMA((3, per, CHUNKS)),
             DMA((seqs - 1,)),
-            DMA((seqs - 1,)),
-        ]
-        + line_sems(seqs, dps),
-        compiler_params=params(collective_id=0),
-        name="gather_inputs",
-    )(tokens, pack, ids)
-
-
-def heads_kernel(
-    seqs, dps, out, cot, pack, out_all, cot_own, pack_all, weight_all, ls, z_send, z_recv, a_send, a_recv, w_send, w_recv, *sems
-):
-    me = Place(seqs, dps)
-    h, s, d = me.h, me.s, me.d
-    per = cot_own.shape[0]
-    greet(me.seq_peers() + me.dp_peers() + [{"head": mod(h + i, 4)} for i in range(1, 4)])
-    start, step, finish = line_gather(me, pack, pack_all, sems, 0)
-    copies = []
-    for i in range(1, 4):
-        to = mod(h + i, 4)
-        for j in range(per):
-            copies.append(
-                send(
-                    out.at[j, me.block(j, to)],
-                    out_all.at[h, j],
-                    a_send.at[i - 1, j],
-                    a_recv.at[i - 1, j],
-                    head=to,
-                )
-            )
-    own_copies = [pltpu.make_async_copy(out.at[j, me.block(j)], out_all.at[h, j], ls.at[j]) for j in range(per)]
-    own_copies.append(pltpu.make_async_copy(pack, pack_all.at[s, d], ls.at[per]))
-    for copy in own_copies:
-        copy.start()
-    start()
-    turn = mod(h - s, 4)
-    mine = lax.rem(turn, 2) == 0
-    which = lax.div(turn, 2)
-
-    @pl.when(mine)
-    def _():
-        for i in range(1, seqs):
-            to = mod(s + i, seqs)
-            send(cot.at[per * to + which], cot_own.at[which], z_send.at[i - 1], z_recv.at[which], seq=to)
-        own = pltpu.make_async_copy(cot.at[per * s + which], cot_own.at[which], ls.at[per + 1])
-        own.start()
-        own.wait()
-
-    for t in range(1, seqs):
-        step(t)
-    for copy in own_copies:
-        copy.wait()
-    finish()
-    lanes = weight_all.shape[-1]
-    gone = []
-    for i in range(1, 4):
-        gone.append(
-            send(
-                pack_all.at[:, :, :, pl.ds(0, lanes)],
-                weight_all.at[h],
-                w_send.at[i - 1],
-                w_recv.at[i - 1],
-                head=mod(h + i, 4),
-            )
-        )
-    own = pltpu.make_async_copy(pack_all.at[:, :, :, pl.ds(0, lanes)], weight_all.at[h], ls.at[0])
-    own.start()
-    own.wait()
-    for j in range(per):
-
-        @pl.when(me.block(j) != s)
-        def _():
-            arrived(cot_own.at[j], z_recv.at[j])
-
-    @pl.when(mine)
-    def _():
-        for i in range(1, seqs):
-            pltpu.make_async_copy(cot.at[0], cot.at[0], z_send.at[i - 1]).wait()
-
-    for copy in copies + gone:
-        copy.wait_send()
-    for i in range(1, 4):
-        source = mod(h - i, 4)
-        for j in range(per):
-            arrived(out_all.at[source, j], a_recv.at[i - 1, j])
-        arrived(weight_all.at[source], w_recv.at[i - 1])
-
-
-def gather_heads(out, cot, pack, seqs, dps, lanes):
-    per, _, span, width = out.shape
-    return pl.pallas_call(
-        functools.partial(heads_kernel, seqs, dps),
-        out_shape=(
-            jax.ShapeDtypeStruct((4, per, span, width), BF16),
-            jax.ShapeDtypeStruct((per,) + cot.shape[1:], BF16),
-            jax.ShapeDtypeStruct((seqs, dps) + pack.shape, BF16),
-            jax.ShapeDtypeStruct((4, seqs, dps, pack.shape[0], lanes), BF16),
-        ),
-        in_specs=[ANY] * 3,
-        out_specs=[ANY] * 4,
-        scratch_shapes=[
-            DMA((per + 2,)),
-            DMA((seqs - 1,)),
-            DMA((per,)),
+            DMA((per, 2)),
             DMA((3, per)),
             DMA((3, per)),
             DMA((3,)),
             DMA((3,)),
+            DMA((seqs - 1,)),
+            DMA((seqs - 1,)),
         ]
-        + line_sems(seqs, dps),
-        compiler_params=params(collective_id=1),
-        name="gather_heads",
-    )(out, cot, pack)
-
-
-def dispatch_kernel(seqs, dps, rows, taken, ls, g_send, g_recv, h_send, h_recv):
-    me = Place(seqs, dps)
-    h, s, d = me.h, me.s, me.d
-    groups, parts = seqs * dps, rows.shape[0]
-    me_group = s * dps + d
-    greet(me.group_peers() + me.head_pair())
-    others = [(i, j) for i in range(seqs) for j in range(dps) if i or j]
-    for part in range(parts):
-        pltpu.make_async_copy(rows.at[part, me_group], taken.at[h, part, me_group], ls.at[part]).start()
-        for n, (i, j) in enumerate(others):
-            to_s, to_d = mod(s + i, seqs), mod(d + j, dps)
-            send(
-                rows.at[part, to_s * dps + to_d],
-                taken.at[h, part, me_group],
-                g_send.at[part, n],
-                g_recv.at[part, n],
-                seq=to_s,
-                dp=to_d,
-            )
-
-    def from_of(n):
-        i, j = others[n]
-        return mod(s - i, seqs) * dps + mod(d - j, dps)
-
-    for part in range(parts):
-        for n in range(-1, len(others)):
-            source = me_group if n < 0 else from_of(n)
-            here = taken.at[h, part, source]
-            if n < 0:
-                pltpu.make_async_copy(here, here, ls.at[part]).wait()
-            else:
-                arrived(here, g_recv.at[part, n])
-            send(here, here, h_send.at[0, part, n + 1], h_recv.at[0, part, n + 1], head=me.across)
-            send(here, here, h_send.at[1, part, n + 1], h_recv.at[1, part, n + 1], head=me.near)
-    for part in range(parts):
-        for n in range(-1, len(others)):
-            source = me_group if n < 0 else from_of(n)
-            there = taken.at[me.across, part, source]
-            arrived(there, h_recv.at[0, part, n + 1])
-            send(there, there, h_send.at[2, part, n + 1], h_recv.at[2, part, n + 1], head=me.near)
-    for part in range(parts):
-        for n in range(-1, len(others)):
-            source = me_group if n < 0 else from_of(n)
-            here = taken.at[h, part, source]
-            for k in range(3):
-                pltpu.make_async_copy(here, here, h_send.at[k, part, n + 1]).wait()
-            if n >= 0:
-                pltpu.make_async_copy(here, here, g_send.at[part, n]).wait()
-            arrived(taken.at[me.near, part, source], h_recv.at[1, part, n + 1])
-            arrived(taken.at[me.near_across, part, source], h_recv.at[2, part, n + 1])
-
-
-def dispatch(rows, seqs, dps):
-    parts, groups = rows.shape[:2]
-    return pl.pallas_call(
-        functools.partial(dispatch_kernel, seqs, dps),
-        out_shape=jax.ShapeDtypeStruct((4,) + rows.shape, BF16),
-        in_specs=[ANY],
-        out_specs=ANY,
-        scratch_shapes=[
-            DMA((parts,)),
-            DMA((parts, groups)),
-            DMA((parts, groups)),
-            DMA((3, parts, groups)),
-            DMA((3, parts, groups)),
-        ],
-        compiler_params=params(collective_id=2),
-        name="dispatch",
-    )(rows)
-
-
-def combine_kernel(
-    seqs, dps, partial, summed, own, near, far_out, far_in, total, ls, n_send, n_recv, x_send, x_recv, g_send, g_recv
+        + line_sems(seqs, dps) * 3,
+        compiler_params=params(collective_id=0),
+        name="front",
+    )(tokens, cot, wq, wk, wv, wo, router, gain_a, gain_f, ids, table, lengths)
+
+
+def expert_windows(exp_local, per_expert):
+    return [(e * per_expert // 16 * 16, up_to((e + 1) * per_expert, 16)) for e in range(exp_local)]
+
+
+def contract(a, b, over_a, over_b):
+    return lax.dot_general(a, b, (((over_a,), (over_b,)), ((), ())), preferred_element_type=F32)
+
+
+GELU_A, GELU_B = float(np.sqrt(2.0 / np.pi)), 0.044715
+
+
+def experts_kernel(
+    seqs, dps, per_expert, rows, up, down, summed, up_grad, down_grad, taken, near, far,
+    ls, g_send, g_recv, h_send, h_recv, n_send, n_recv, x_send, x_recv, r_send, r_recv
 ):
     me = Place(seqs, dps)
     h, s, d = me.h, me.s, me.d
-    groups, parts = seqs * dps, summed.shape[0]
+    groups, _, height, width = rows.shape
+    exp_local = up.shape[0]
+    windows = expert_windows(exp_local, per_expert)
     me_group = s * dps + d
+
+    def away(n):
+        i, j = lax.div(n, dps), lax.rem(n, dps)
+        return jnp.where(i == 2, 3, jnp.where(i == 3, 2, i)), j
+
+    def ahead(n):
+        i, j = away(n)
+        return mod(s + i, seqs), mod(d + j, dps)
+
+    def behind(n):
+        i, j = away(n)
+        return mod(s - i, seqs), mod(d - j, dps)
+
+    up_grad[...] = jnp.zeros_like(up_grad)
+    down_grad[...] = jnp.zeros_like(down_grad)
     greet(me.group_peers() + me.head_pair())
-    others = [(i, j) for i in range(seqs) for j in range(dps) if i or j] + [(0, 0)]
-    order = [(part, n) for part in range(parts) for n in range(groups)]
-
-    def group_of(n):
-        i, j = others[n]
-        return mod(s + i, seqs), mod(d + j, dps)
-
-    for part, n in order:
-        to_s, to_d = group_of(n)
-        group = to_s * dps + to_d
-        for k, head in enumerate((me.near_across, me.near)):
-            send(
-                partial.at[head, part, group],
-                near.at[k, part, n],
-                n_send.at[k, part, n],
-                n_recv.at[k, part, n],
-                head=me.near,
-            )
-        for k, head in enumerate((me.across, h)):
-            pltpu.make_async_copy(partial.at[head, part, group], own.at[k, part, n], ls.at[k, part, n]).start()
-    for part, n in order:
-        arrived(near.at[0, part, n], n_recv.at[0, part, n])
-        pltpu.make_async_copy(own.at[0, part, n], own.at[0, part, n], ls.at[0, part, n]).wait()
-        both = own[0, part, n].astype(F32) + near[0, part, n].astype(F32)
-        far_out[part, n] = both.astype(BF16)
-        send(far_out.at[part, n], far_in.at[part, n], x_send.at[part, n], x_recv.at[part, n], head=me.across)
-    for part, n in order:
-        to_s, to_d = group_of(n)
-        arrived(near.at[1, part, n], n_recv.at[1, part, n])
-        pltpu.make_async_copy(own.at[1, part, n], own.at[1, part, n], ls.at[1, part, n]).wait()
-        arrived(far_in.at[part, n], x_recv.at[part, n])
-        both = own[1, part, n].astype(F32) + near[1, part, n].astype(F32) + far_in[part, n].astype(F32)
-        total[part, n] = both.astype(BF16)
-        if n < groups - 1:
-            send(
-                total.at[part, n],
-                summed.at[part, me_group],
-                g_send.at[part, n],
-                g_recv.at[part, n],
-                seq=to_s,
-                dp=to_d,
-            )
-        else:
-            pltpu.make_async_copy(total.at[part, n], summed.at[part, me_group], g_send.at[part, n]).start()
-    for part, n in order:
-        i, j = others[n]
+    pltpu.make_async_copy(rows.at[me_group], taken.at[h, 0], ls.at[0]).start()
+
+    @pl.loop(1, groups)
+    def _(n):
+        to_s, to_d = ahead(n)
+        send(rows.at[to_s * dps + to_d], taken.at[h, n], g_send.at[n], g_recv.at[n], seq=to_s, dp=to_d)
+
+    def gather_own(n):
+        here = taken.at[h, n]
+
+        @pl.when(n == 0)
+        def _():
+            pltpu.make_async_copy(here, here, ls.at[0]).wait()
+
+        @pl.when(n > 0)
+        def _():
+            arrived(here, g_recv.at[n])
+
+        send(here, here, h_send.at[0, n], h_recv.at[0, n], head=me.across)
+        send(here, here, h_send.at[1, n], h_recv.at[1, n], head=me.near)
+
+    def gather_across(n):
+        there = taken.at[me.across, n]
+        arrived(there, h_recv.at[0, n])
+        send(there, there, h_send.at[2, n], h_recv.at[2, n], head=me.near)
+
+    def compute(n):
+        arrived(taken.at[me.near, n], h_recv.at[1, n])
+        arrived(taken.at[me.near_across, n], h_recv.at[2, n])
+        for k in range(3):
+            pltpu.make_async_copy(taken.at[h, n], taken.at[h, n], h_send.at[k, n]).wait()
+        kept = []
+        for e, (low, high) in enumerate(windows):
+            size = high - low
+            at = lax.broadcasted_iota(jnp.int32, (4 * size, width), 0)
+            slot = lax.rem(at, size) + low
+            inside = (slot >= e * per_expert) & (slot < (e + 1) * per_expert)
+
+            def mine(part):
+                block = jnp.concatenate([taken[q, n, part, low:high, :] for q in range(4)], axis=0)
+                return jnp.where(inside, block.astype(F32), 0.0).astype(BF16)
+
+            x, g = mine(0), mine(1)
+            pre = jnp.dot(x, up[e], preferred_element_type=F32)
+            square = pre * pre
+            bent = jnp.tanh(GELU_A * pre * (1.0 + GELU_B * square))
+            act = (0.5 * pre * (1.0 + bent)).astype(BF16)
+            slope = 0.5 * (1.0 + bent) + 0.5 * pre * (1.0 - bent * bent) * (GELU_A * (1.0 + 3.0 * GELU_B * square))
+            out = jnp.dot(act, down[e], preferred_element_type=F32).astype(BF16)
+            act_grad = contract(g, down[e], 1, 1)
+            pre_grad = (act_grad * slope).astype(BF16)
+            back = contract(pre_grad, up[e], 1, 1).astype(BF16)
+            kept.append((x, g, act, pre_grad, out, back))
+        for q in range(4):
+            for part in range(2):
+                for tile in range(0, height, 16):
+                    total = None
+                    for (low, high), made in zip(windows, kept):
+                        if low <= tile < high:
+                            begin = q * (high - low) + tile - low
+                            piece = made[4 + part][begin : begin + 16, :]
+                            total = piece if total is None else total + piece
+                    if total is not None:
+                        taken[q, n, part, tile : tile + 16, :] = total
+        send(taken.at[me.near_across, n], near.at[0, n], n_send.at[0, n], n_recv.at[0, n], head=me.near)
+        send(taken.at[me.near, n], near.at[1, n], n_send.at[1, n], n_recv.at[1, n], head=me.near)
+        for e in range(exp_local):
+            x, g, act, pre_grad, _, _ = kept[e]
+            up_grad[e] += contract(x, pre_grad, 0, 0)
+            down_grad[e] += contract(act, g, 0, 0)
+
+    def add_near(n):
+        arrived(near.at[0, n], n_recv.at[0, n])
+        both = taken[me.across, n].astype(F32) + near[0, n].astype(F32)
+        taken[me.across, n] = both.astype(BF16)
+        send(taken.at[me.across, n], far.at[n], x_send.at[n], x_recv.at[n], head=me.across)
+
+    def send_back(n):
+        arrived(near.at[1, n], n_recv.at[1, n])
+        arrived(far.at[n], x_recv.at[n])
+        total = taken[h, n].astype(F32) + near[1, n].astype(F32) + far[n].astype(F32)
+        taken[h, n] = total.astype(BF16)
+        to_s, to_d = behind(n)
+
+        @pl.when(n == 0)
+        def _():
+            pltpu.make_async_copy(taken.at[h, n], summed.at[me_group], r_send.at[n]).start()
+
+        @pl.when(n > 0)
+        def _():
+            send(taken.at[h, n], summed.at[me_group], r_send.at[n], r_recv.at[n], seq=to_s, dp=to_d)
+
+    stages = (send_back, add_near, compute, gather_across, gather_own)
+
+    @pl.loop(0, groups + len(stages) - 1)
+    def _(step):
+        for k, stage in enumerate(stages):
+            n = step - (len(stages) - 1 - k)
+
+            @pl.when((n >= 0) & (n < groups))
+            def _():
+                stage(n)
+
+    @pl.loop(0, groups)
+    def _(n):
+        here = taken.at[h, n]
         for k in range(2):
-            pltpu.make_async_copy(near.at[k, part, n], near.at[k, part, n], n_send.at[k, part, n]).wait()
-        pltpu.make_async_copy(far_out.at[part, n], far_out.at[part, n], x_send.at[part, n]).wait()
-        pltpu.make_async_copy(total.at[part, n], total.at[part, n], g_send.at[part, n]).wait()
-        if n < groups - 1:
-            source = mod(s - i, seqs) * dps + mod(d - j, dps)
-            arrived(summed.at[part, source], g_recv.at[part, n])
-
-
-def combine(partial, seqs, dps):
-    _, parts, groups, rows, width = partial.shape
-    block = (parts, groups, rows, width)
+            pltpu.make_async_copy(here, here, n_send.at[k, n]).wait()
+        pltpu.make_async_copy(here, here, x_send.at[n]).wait()
+        pltpu.make_async_copy(here, here, r_send.at[n]).wait()
+
+        @pl.when(n > 0)
+        def _():
+            pltpu.make_async_copy(here, here, g_send.at[n]).wait()
+            from_s, from_d = ahead(n)
+            arrived(summed.at[from_s * dps + from_d], r_recv.at[n])
+
+
+def run_experts(rows, up, down, seqs, dps, per_expert):
+    groups, parts, height, width = rows.shape
     return pl.pallas_call(
-        functools.partial(combine_kernel, seqs, dps),
-        out_shape=jax.ShapeDtypeStruct(block, BF16),
-        in_specs=[ANY],
-        out_specs=ANY,
+        functools.partial(experts_kernel, seqs, dps, per_expert),
+        out_shape=(
+            jax.ShapeDtypeStruct(rows.shape, BF16),
+            jax.ShapeDtypeStruct(up.shape, F32),
+            jax.ShapeDtypeStruct(down.shape, F32),
+        ),
+        in_specs=[ANY, VMEM, VMEM],
+        out_specs=[ANY, VMEM, VMEM],
         scratch_shapes=[
-            pltpu.VMEM((2,) + block, BF16),
-            pltpu.VMEM((2,) + block, BF16),
-            pltpu.VMEM(block, BF16),
-            pltpu.VMEM(block, BF16),
-            pltpu.VMEM(block, BF16),
-        ]
-        + [DMA((2, parts, groups))] * 3
-        + [DMA((parts, groups))] * 4,
-        compiler_params=params(collective_id=3),
-        name="combine",
-    )(partial)
+            pltpu.VMEM((4,) + rows.shape, BF16),
+            pltpu.VMEM((2,) + rows.shape, BF16),
+            pltpu.VMEM(rows.shape, BF16),
+            DMA((1,)),
+            DMA((groups,)),
+            DMA((groups,)),
+            DMA((3, groups)),
+            DMA((3, groups)),
+            DMA((2, groups)),
+            DMA((2, groups)),
+            DMA((groups,)),
+            DMA((groups,)),
+            DMA((groups,)),
+            DMA((groups,)),
+        ],
+        compiler_params=params(collective_id=2),
+        name="experts",
+    )(rows, up, down)
 
 
 def send_home(me, own, home, ls, z_send, z_recv, h_send, h_recv):
@@ -847,73 +994,17 @@
     )(grad, weights, bias)
 
 
-def bias_block(band, far, head, q_block, k_block, span):
-    step = k_block - q_block
-    if abs(step) <= 1:
-        return band[head, :, (step + 1) * span : (step + 2) * span]
-    return far[head, 0 if step < 0 else 1]
-
-
-def attend_kernel(heads, blocks, span, q_ref, k_ref, v_ref, band, far, mask, out_ref, prob_ref):
-    for head in range(heads):
-        cols = slice(head * HEAD_DIM, (head + 1) * HEAD_DIM)
-        key = k_ref[0, :, cols]
-        value = v_ref[0, :, cols]
-        for q_block in range(blocks):
-            rows = slice(q_block * span, (q_block + 1) * span)
-            query = q_ref[0, rows, cols]
-            scores = lax.dot_general(query, key, (((1,), (1,)), ((), ())), preferred_element_type=F32)
-            parts = []
-            for k_block in range(blocks):
-                part = scores[:, k_block * span : (k_block + 1) * span]
-                valid = mask[0, :, k_block * span : (k_block + 1) * span]
-                term = bias_block(band, far, head, q_block, k_block, span)
-                parts.append(jnp.where(valid > 0, part + term, -1e30))
-            scores = jnp.concatenate(parts, axis=1)
-            top = jnp.max(scores, axis=-1, keepdims=True)
-            grown = jnp.exp(scores - top)
-            total = jnp.sum(grown, axis=-1, keepdims=True)
-            weights = (grown * (1.0 / total)).astype(BF16)
-            prob_ref[0, head, rows, :] = weights
-            mixed = jnp.dot(weights, value, preferred_element_type=F32)
-            out_ref[0, rows, cols] = mixed.astype(BF16)
-
-
-def attend(queries, keys, values, band, far, mask, heads, blocks, span):
-    per, length, width = queries.shape
-    whole = pl.BlockSpec((1, length, width), lambda j: (j, 0, 0))
-    return pl.pallas_call(
-        functools.partial(attend_kernel, heads, blocks, span),
-        grid=(per,),
-        out_shape=(
-            jax.ShapeDtypeStruct((per, length, width), BF16),
-            jax.ShapeDtypeStruct((per, heads, length, length), BF16),
-        ),
-        in_specs=[
-            whole,
-            whole,
-            whole,
-            pl.BlockSpec(band.shape, lambda j: (0, 0, 0)),
-            pl.BlockSpec(memory_space=pltpu.SMEM),
-            pl.BlockSpec((1, 1, length), lambda j: (j, 0, 0)),
-        ],
-        out_specs=[whole, pl.BlockSpec((1, heads, length, length), lambda j: (j, 0, 0, 0))],
-        compiler_params=pltpu.CompilerParams(vmem_limit_bytes=56 * 2**20),
-        name="attend",
-    )(queries, keys, values, band, far, mask)
-
-
 def attend_back_kernel(
-    heads, blocks, span, q_ref, k_ref, v_ref, g_ref, p_ref, dq_ref, dk_ref, dv_ref, band_ref, far_ref, dk_sum, dv_sum
+    heads, blocks, span, s_ref, g_ref, p_ref, dq_ref, dk_ref, dv_ref, band_ref, far_ref, dk_sum, dv_sum
 ):
     first = pl.program_id(0) == 0
     for head in range(heads):
         cols = slice(head * HEAD_DIM, (head + 1) * HEAD_DIM)
-        key = k_ref[0, :, cols]
-        value = v_ref[0, :, cols]
+        key = s_ref[0, heads + head]
+        value = s_ref[0, 2 * heads + head]
         for q_block in range(blocks):
             rows = slice(q_block * span, (q_block + 1) * span)
-            query = q_ref[0, rows, cols]
+            query = s_ref[0, head, rows, :]
             grad = g_ref[0, rows, cols]
             weights = p_ref[0, head, rows, :]
             prob_grad = lax.dot_general(grad, value, (((1,), (1,)), ((), ())), preferred_element_type=F32)
@@ -948,8 +1039,8 @@
         dv_ref[0, :, cols] = dv_sum[...].astype(BF16)
 
 
-def attend_back(queries, keys, values, grads, probs, heads, blocks, span):
-    per, length, width = queries.shape
+def attend_back(split, grads, probs, heads, blocks, span):
+    per, length, width = grads.shape
     whole = pl.BlockSpec((1, length, width), lambda j: (j, 0, 0))
     return pl.pallas_call(
         functools.partial(attend_back_kernel, heads, blocks, span),
@@ -961,7 +1052,8 @@
             jax.ShapeDtypeStruct((heads, span, 3 * span), F32),
             jax.ShapeDtypeStruct((heads, 2, 8, span), F32),
         ),
-        in_specs=[whole] * 4 + [pl.BlockSpec((1, heads, length, length), lambda j: (j, 0, 0, 0))],
+        in_specs=[pl.BlockSpec((1,) + split.shape[1:], lambda j: (j, 0, 0, 0)), whole]
+        + [pl.BlockSpec((1, heads, length, length), lambda j: (j, 0, 0, 0))],
         out_specs=[whole] * 3
         + [
             pl.BlockSpec((heads, span, 3 * span), lambda j: (0, 0, 0)),
@@ -970,7 +1062,7 @@
         scratch_shapes=[pltpu.VMEM((length, HEAD_DIM), F32)] * 2,
         compiler_params=pltpu.CompilerParams(vmem_limit_bytes=56 * 2**20),
         name="attend_back",
-    )(queries, keys, values, grads, probs)
+    )(split, grads, probs)
 
 
 def up_to(value, unit):
@@ -1007,64 +1099,33 @@
     shard = query_weight.shape[0]
     head_at, seq_at = lax.axis_index("head"), lax.axis_index("seq")
 
-    first_width = up_to(3 * local_width + 1, 128)
-    first_pack = jnp.concatenate(
-        [
-            query_weight,
-            key_weight,
-            value_weight,
-            attention_gain[:, None],
-            jnp.zeros((shard, first_width - 3 * local_width - 1), BF16),
-        ],
-        axis=1,
+    ids = expert_ids.reshape(seq_local, span)
+    attn_input, weights, split, probs, heads_all, own_tok, cot_own, out_weight, gains, ids_all = front(
+        tokens,
+        cotangent,
+        query_weight,
+        key_weight,
+        value_weight,
+        output_weight,
+        router_weight,
+        attention_gain[None, :],
+        feedforward_gain[None, :],
+        ids,
+        position_bias.astype(F32),
+        lengths,
+        seqs,
+        dps,
     )
-    lanes = up_to(local_width, 128)
-    small = up_to(experts + 1, 128)
-    second_pack = jnp.concatenate(
-        [
-            output_weight.T,
-            jnp.zeros((shard, lanes - local_width), BF16),
-            router_weight,
-            feedforward_gain[:, None],
-            jnp.zeros((shard, small - experts - 1), BF16),
-        ],
-        axis=1,
-    )
-    ids = expert_ids.reshape(seq_local, span)
-    tok_all, first_all, ids_all = gather_inputs(tokens, first_pack, ids, seqs, dps)
-    first_all = first_all.reshape(width, first_width)
-    project_weight = first_all[:, : 3 * local_width]
-    gain_one = first_all[:, 3 * local_width].astype(F32)
-
-    inputs = tok_all.reshape(count, width).astype(F32)
-    attn_input = normalize(inputs, gain_one).astype(BF16)
-    made = jnp.dot(attn_input, project_weight, preferred_element_type=F32).astype(BF16)
-    queries, keys, values = (
-        made[:, i * local_width : (i + 1) * local_width].reshape(per, length, local_width) for i in range(3)
-    )
+    project_weight = weights[:, : 3 * local_width]
+    router_full = weights[:, 3 * local_width : 3 * local_width + experts]
+    gain_one, gain_two = gains[0], gains[1]
+    attn_input = attn_input.reshape(count, width)
     offset = jnp.arange(3 * span, dtype=jnp.int32)[None, :] - span - jnp.arange(span, dtype=jnp.int32)[:, None]
     bucket = bucket_of(offset, bucket_count)
-    table = position_bias.astype(F32)
-    band = jnp.zeros((heads, span, 3 * span), F32)
-    for b in range(bucket_count):
-        band = jnp.where((bucket == b)[None], table[b][:, None, None], band)
-    far = jnp.stack([table[bucket_count // 2 - 1], table[bucket_count - 1]], axis=1)
-    own_lengths = lax.dynamic_slice_in_dim(lengths, per * seq_at, per)
-    mask = (jnp.arange(length, dtype=jnp.int32)[None, None, :] < own_lengths[:, None, None]).astype(F32)
-    heads_out, probs = attend(queries, keys, values, band, far, mask, heads, seqs, span)
-
-    heads_all, cot_own, second_all, out_weight = gather_heads(
-        heads_out.reshape(per, seqs, span, local_width), cotangent, second_pack, seqs, dps, lanes
-    )
-    second_all = second_all.reshape(width, lanes + small)
-    router_full = second_all[:, lanes : lanes + experts]
-    gain_two = second_all[:, lanes + experts].astype(F32)
-    out_weight = out_weight.reshape(4, width, lanes)[:, :, :local_width]
     heads_all = heads_all.reshape(4, own_rows, local_width)
     own_blocks = [lax.rem(head_at + 2 * j, 4) for j in range(per)]
-    own_inputs = jnp.stack([lax.dynamic_index_in_dim(tok_all[j], own_blocks[j], 0, False) for j in range(per)])
-    own_inputs = own_inputs.reshape(own_rows, width).astype(F32)
-    attention = jnp.einsum("htk,hdk->td", heads_all, out_weight, preferred_element_type=F32)
+    own_inputs = own_tok.reshape(own_rows, width).astype(F32)
+    attention = jnp.einsum("htk,hkd->td", heads_all, out_weight, preferred_element_type=F32)
     hidden = own_inputs + attention
     ffn_input = normalize(hidden, gain_two).astype(BF16)
     logits = jnp.dot(ffn_input, router_full, preferred_element_type=F32)
@@ -1093,32 +1154,13 @@
     gate = jnp.sum(router_probs * hot, axis=-1)
     grad_out = cot_own.reshape(own_rows, width).astype(F32)
     sent_grad = (gate[:, None] * grad_out).astype(BF16)
-    to_send = jnp.stack([ffn_input, sent_grad])
-    rows = jnp.einsum("rt,ptd->prd", place_hot, to_send, preferred_element_type=F32).astype(BF16)
-    taken = dispatch(rows.reshape(2, groups, rows_pad, width), seqs, dps)
-
-    def by_expert(part):
-        part = taken[:, part, :, :rows_used].reshape(4 * groups, exp_local, per * capacity, width)
-        return jnp.swapaxes(part, 0, 1).reshape(exp_local, 4 * groups * per * capacity, width)
-
-    def by_group(part):
-        part = jnp.swapaxes(part.reshape(exp_local, 4 * groups, per * capacity, width), 0, 1)
-        part = part.reshape(4, groups, rows_used, width)
-        return jnp.pad(part, ((0, 0), (0, 0), (0, rows_pad - rows_used), (0, 0)))
-
-    received, grad_rows = by_expert(0), by_expert(1)
-    hidden_pre = jnp.einsum("xrd,xdf->xrf", received, expert_up, preferred_element_type=F32)
-    activated = gelu_tanh(hidden_pre).astype(BF16)
-    partial_out = jnp.einsum("xrf,xfd->xrd", activated, expert_down, preferred_element_type=F32).astype(BF16)
-    act_grad = jnp.einsum("xrd,xfd->xrf", grad_rows, expert_down, preferred_element_type=F32)
-    _, gelu_pull = jax.vjp(gelu_tanh, hidden_pre)
-    pre_grad = gelu_pull(act_grad)[0].astype(BF16)
-    input_part = jnp.einsum("xrf,xdf->xrd", pre_grad, expert_up, preferred_element_type=F32).astype(BF16)
-    summed = combine(jnp.stack([by_group(partial_out), by_group(input_part)], axis=1), seqs, dps)
-    down_grad = jnp.einsum("xrf,xrd->xfd", activated, grad_rows, preferred_element_type=F32)
-    up_grad = jnp.einsum("xrd,xrf->xdf", received, pre_grad, preferred_element_type=F32)
-
-    back = jnp.einsum("rt,prd->ptd", place_hot, summed.reshape(2, spots, width), preferred_element_type=F32)
+    to_send = jnp.concatenate([ffn_input, sent_grad], axis=1)
+    rows = jnp.dot(place_hot, to_send, preferred_element_type=F32).astype(BF16)
+    rows = jnp.swapaxes(rows.reshape(groups, rows_pad, 2, width), 1, 2)
+    summed, up_grad, down_grad = run_experts(rows, expert_up, expert_down, seqs, dps, per * capacity)
+    summed = jnp.swapaxes(summed, 1, 2).reshape(spots, 2 * width)
+    back = jnp.einsum("rt,rd->td", place_hot, summed, preferred_element_type=F32)
+    back = (back[:, :width], back[:, width:])
     token_out, expert_input_grad = back[0], back[1]
     result = (hidden + gate[:, None] * token_out).astype(BF16)
     gate_grad = jnp.sum(grad_out * token_out, axis=-1)
@@ -1130,14 +1172,14 @@
     hidden_norm_grad, gain_two_grad = norm_pull(ffn_input_grad)
     hidden_grad = grad_out + hidden_norm_grad
     attn_grad = hidden_grad.astype(BF16)
-    heads_grad = jnp.einsum("td,hdk->htk", attn_grad, out_weight, preferred_element_type=F32).astype(BF16)
+    heads_grad = jnp.einsum("td,hkd->htk", attn_grad, out_weight, preferred_element_type=F32).astype(BF16)
     grad_all, output = gather_grads(
         heads_grad.reshape(4, per, span, local_width), result.reshape(per, span, width), seqs, dps
     )
     out_w_part = jnp.einsum("td,htk->hdk", attn_grad, heads_all, preferred_element_type=F32).astype(BF16)
 
     query_grad, key_grad, value_grad, band_grad, far_grad = attend_back(
-        queries, keys, values, grad_all.reshape(per, length, local_width), probs, heads, seqs, span
+        split, grad_all.reshape(per, length, local_width), probs, heads, seqs, span
     )
     bias_grad = jnp.stack(
         [jnp.sum(jnp.where((bucket == b)[None], band_grad, 0.0), axis=(1, 2)) for b in range(bucket_count)]

time: 603 us -> 460 us (0.76)
  matrix products: 68.5 us -> 19.1 us
  Pallas kernels: 392 us -> 356 us
  other arithmetic: 61.7 us -> 27.3 us
  local copies, waits for them, and re-layouts: 69.7 us -> 47.8 us
    dot_general x11 -> x4, matrix products: 51.8 us -> 7.44 us  [the longest x1 2.73 us: body(): jnp.einsum('htk,hkd->td', heads_all, out_weight, preferred_element_type=F32)]
    pallas_call x5 -> x2, Pallas kernels: 240 us -> 204 us  [the longest x1 118 us: run_experts(): pl.pallas_call(functools.partial(experts_kernel, seqs, dps, per_expert),...]
    slice x9 -> x1, local copies, waits for them, and re-layouts: 16.2 us -> 0.84 us  [body(): gain_one, gain_two = (gains[0], gains[1])]
    another operation x4 -> x0, other arithmetic: 9.21 us -> none  [the longest x1 5.88 us: body(): jnp.stack([by_group(partial_out), by_group(input_part)], axis=1)]
    select_n x1 -> x0, other arithmetic: 8.5 us -> none  [body(): band = jnp.where((bucket == b)[None], table[b][:, None, None], band)]
    concatenate x2, local copies, waits for them, and re-layouts: 11.8 us -> 5.03 us  [body(): jnp.concatenate([project_grad, out_w_sum.astype(BF16), tail], axis=1)]
    unnamed x201 -> x80, local copies, waits for them, and re-layouts: 17.4 us -> 21.4 us
where the time goes in v2:
time: 460 us; the launch traced here: 452 us
  Pallas kernels  356 us (77%)
  local copies, waits for them, and re-layouts  47.8 us (10%)
  other arithmetic  27.3 us (6%)
  matrix products  19.1 us (4%)
    pallas_call x1, Pallas kernels, run_experts(): pl.pallas_call(functools.partial(experts_kernel, seqs, dps, per_expert),...  118 us
    pallas_call x1, Pallas kernels, front(): pl.pallas_call(functools.partial(front_kernel, seqs, dps, heads), out_sha...  86.6 us
    pallas_call x1, Pallas kernels, finish_grads(): pl.pallas_call(functools.partial(last_kernel, seqs, dps), out_shape=(jax....  50.6 us
    pallas_call x1, Pallas kernels, gather_grads(): pl.pallas_call(functools.partial(grads_kernel, seqs, dps), out_shape=(jax...  43.9 us
    pallas_call x1, Pallas kernels, add_heads(): pl.pallas_call(functools.partial(input_kernel, seqs, dps), out_shape=(jax...  32.3 us
    pallas_call x1, Pallas kernels, attend_back(): pl.pallas_call(functools.partial(attend_back_kernel, heads, blocks, span)...  25 us
    unnamed x80, local copies, waits for them, and re-layouts  21.4 us
    reduce_sum x2, other arithmetic, body(): jnp.sum(jnp.where((bucket == b)[None], band_grad, 0.0), axis=(1, 2))  11.8 us

profile of v2, /device:TPU:0, one launch (start us, length us, event | category | flops | bytes accessed | tf_op | source)
XLA Modules:
  0.0 452.1 jit_solution(6345466947655295720)
XLA Ops:
  0.6 1.4 copy.163.router
  2.0 1.3 copy.193
  3.3 1.4 copy.164.table
  4.7 86.6 %front.1 = (bf16[2,1024,768]{2,1,0:T(8,128)(2,1)}, bf16[768,640]{1,0:T(8,128)(2,1)}, bf16[2,9,1024,64]{3,2,1,0:T(8,128)(2,1)}, bf16[2,3,1024,1024]{3,2,1,0:T(8,1...) custom-call(bf16[8,256,768]{2,1,0:T(8,128)(2,1)} %tok.1, ...), custom_call_target="tpu_custom_call" | custom-call | tf_op jit(solution)/shard_map/front/pallas_call | solution.py:480
  91.3 2.7 multiply_reduce_fusion.2
  94.0 0.8 slice_reduce_fusion.2
  94.9 0.8 dynamic-slice_bitcast_fusion.1
  96.0 1.6 fusion.57
  99.4 2.5 convolution_convert_fusion.1
  101.8 4.2 reshape.941
  106.1 1.5 copy.191
  107.6 117.9 %experts.1 = (bf16[8,2,80,768]{3,2,1,0:T(8,128)(2,1)}, f32[2,768,768]{2,1,0:T(8,128)}, f32[2,768,768]{2,1,0:T(8,128)}) custom-call(bf16[8,2,80,768]{3,2,1,0:T(8,128)(2,1)} %bitcast.118, bf16[2,768,768]{2,1,0:T(8,128)(2,1)} %up.1, bf16[2,768,768]{2,1,0:T(8,128)(2,1)} %down.1), custom_call_target="tpu_custom_call" | custom-call | tf_op jit(solution)/shard_map/experts/pallas_call | solution.py:686
  225.6 3.2 copy.167
  229.4 1.4 fusion.12
  230.9 1.3 add_convert_fusion
  232.3 1.7 multiply_reduce_fusion
  234.5 0.8 copy-done.27
  235.3 0.8 fusion.13
  236.1 1.3 copy.168
  237.4 43.9 %gather_grads.1 = (bf16[2,4,256,192]{3,2,1,0:T(8,128)(2,1)}, bf16[8,256,768]{2,1,0:T(8,128)(2,1)}) custom-call(bf16[4,2,256,192]{3,2,1,0:T(8,128)(2,1)} %bitcast.127, bf16[2,256,768]{2,1,0:T(8,128)(2,1)} %bitcast.130), custom_call_target="tpu_custom_call" | custom-call | tf_op jit(solution)/shard_map/gather_grads/pallas_call | solution.py:817
  281.3 25.0 %attend_back.1 = (bf16[2,1024,192]{2,1,0:T(8,128)(2,1)}, bf16[2,1024,192]{2,1,0:T(8,128)(2,1)}, bf16[2,1024,192]{2,1,0:T(8,128)(2,1)}, f32[3,256,768]{2,1,0:T(8,128)}, f32[3,2,8,256]{3,2,1,0:T(8,128)}) custom-call(bf16[2,9,1024,64]{3,2,1,0:T(8,128)(2,1)} %get-tuple-element.70.s_ref, bf16[2,1024,192]{2,1,0:T(8,128)(2,1)} %bitcast.134, ...), custom_call_target="tpu_custom_call" | custom-call | tf_op jit(solution)/shard_map/attend_back/pallas_call | solution.py:1045
  306.3 2.9 pad_maximum_fusion
  309.2 4.3 convolution_convert_fusion
  313.6 0.8 convolution_convert_fusion.2
  314.4 1.5 copy.170
  315.9 32.3 %add_heads.1 = (f32[2,256,768]{2,1,0:T(8,128)}, f32[768,192]{1,0:T(8,128)}) custom-call(bf16[2,4,256,768]{3,2,1,0:T(8,128)(2,1)} %bitcast.129, bf16[4,768,192]{2,1,0:T(8,128)(2,1)} %bitcast.120), custom_call_target="tpu_custom_call" | custom-call | tf_op jit(solution)/shard_map/add_heads/pallas_call | solution.py:879
  348.5 2.2 fusion.11
  350.8 1.3 fusion.1
  352.1 0.8 copy-done.9
  352.9 3.0 bitcast_convert_fusion
  356.1 0.9 copy-done.3
  357.3 4.2 concatenate.18
  361.5 0.9 copy.173
  362.3 1.2 copy.192
  363.5 6.1 %broadcast_compare_fusion.15 = (pred[256,768]{1,0:T(8,128)(4,1)S(1)}, pred[256,768]{1,0:T(8,128)(4,1)S(1)}, pred[256,768]{1,0:T(8,128)(4,1)S(1)}, pred[256,768]{...) fusion(s32[768]{0:T(1024)S(1)} %iota_add_fusion), kind=kLoop, calls=%fused_computation.113 | loop fusion | flops 15925248 | bytes 6294528 | tf_op jit(solution)/shard_map/eq | solution.py:1185
  369.6 5.2 %select_reduce_fusion.18 = (f32[3]{0:T(128)S(1)}, f32[3]{0:T(128)S(1)}, f32[3]{0:T(128)S(1)}, f32[3]{0:T(128)S(1)}, f32[3]{0:T(128)S(1)}, /*index=5*/f32[3]{0:T(...) fusion(f32[3,256,768]{2,1,0:T(8,128)S(1)} %copy-done, ...), kind=kLoop, calls=%fused_computation.26 | loop fusion | flops 16515030 | bytes 5111976 | tf_op jit(solution)/shard_map/reduce_sum | solution.py:1185
  374.9 6.5 %select_reduce_fusion = (f32[3]{0:T(128)S(1)}, f32[3]{0:T(128)S(1)}, f32[3]{0:T(128)S(1)}, f32[3]{0:T(128)S(1)}, f32[3]{0:T(128)S(1)}, /*index=5*/f32[3]{0:T(128...) fusion(f32[3,256,768]{2,1,0:T(8,128)S(1)} %copy-done, ...), kind=kLoop, calls=%fused_computation.8 | loop fusion | flops 21233608 | bytes 5898456 | tf_op jit(solution)/shard_map/reduce_sum | solution.py:1185
  382.5 50.6 %finish_grads.1 = (bf16[8,256,768]{2,1,0:T(8,128)(2,1)}, f32[96,896]{1,0:T(8,128)}, f32[32,128]{1,0:T(8,128)}) custom-call(bf16[2,256,768]{2,1,0:T(8,128)(2,1)} %bitcast.128, bf16[2,4,96,896]{3,2,1,0:T(8,128)(2,1)} %bitcast.121, f32[32,128]{1,0:T(8,128)} %pad.8.bias), custom_call_target="tpu_custom_call" | custom-call | tf_op jit(solution)/shard_map/finish_grads/pallas_call | solution.py:966
  433.1 1.6 slice_reduce_fusion
  434.7 1.9 slice_bitcast_fusion
  436.6 0.7 copy.175
  437.3 1.4 copy.176
  438.7 0.8 slice.96
  439.5 0.7 copy.177
  440.2 3.9 copy.200
  444.1 1.7 copy.201
  446.3 2.4 copy.202
  449.5 2.2 copy.203
  (100 shorter events, 6.4 us)
Async XLA Ops:
  94.0 0.9 copy-start.22
  94.0 1.7 copy-start.20
  94.9 3.3 copy-start.4
  95.9 2.8 copy-start.2
  97.5 0.6 copy-start.11
  98.1 0.6 copy-start.16
  98.2 0.6 copy-start.18
  98.8 0.6 copy-start.24
  228.7 0.7 copy-start.25
  229.4 1.5 copy-start.5
  229.4 1.5 copy-start.19
  230.9 1.3 copy-start.12
  230.9 1.3 copy-start.17
  230.9 1.3 copy-start.21
  232.3 1.7 copy-start.23
  234.0 1.3 copy-start.27
  306.3 3.0 copy-start.14
  309.2 4.3 copy-start.8
  309.2 4.3 copy-start.10
  315.9 32.3 %copy-start.1 = (bf16[2,256,768]{2,1,0:T(8,128)(2,1)S(1)}, bf16[2,256,768]{2,1,0:T(8,128)(2,1)}, u32[]{:S(2)}) copy-start(bf16[2,256,768]{2,1,0:T(8,128)(2,1)} %get-tuple-element.64) | copy-start | bytes 2359300
  348.2 2.5 copy-start.6
  348.5 3.6 copy-start.26
  350.7 2.1 copy-start.9
  352.9 3.0 copy-start.13
  355.9 1.1 copy-start.3
  363.5 6.1 %copy-start = (f32[3,256,768]{2,1,0:T(8,128)S(1)}, f32[3,256,768]{2,1,0:T(8,128)}, u32[]{:S(2)}) copy-start(f32[3,256,768]{2,1,0:T(8,128)} %get-tuple-element.79) | copy-start | bytes 7077892
  374.9 6.6 %copy-start.15 = (f32[3,2,8,256]{3,2,1,0:T(8,128)S(1)}, f32[3,2,8,256]{3,2,1,0:T(8,128)}, u32[]{:S(2)}) copy-start(f32[3,2,8,256]{3,2,1,0:T(8,128)} %get-tuple-element.80) | copy-start | bytes 147460
  382.5 63.2 %slice-start.2 = ((s8[4718592]{0:T(1024)(128)(4,1)}), s8[524288]{0:T(1024)(128)(4,1)S(1)}, s32[]{:S(2)}) async-start(s8[4718592]{0:T(1024)(128)(4,1)} %bitcast.125), calls=%async_computation.2 | async-start | bytes 1048576
  440.2 3.9 copy-start.7
  440.2 6.1 %slice-start.3 = ((s8[4718592]{0:T(1024)(128)(4,1)}), s8[4194304]{0:T(1024)(128)(4,1)S(1)}, s32[]{:S(2)}) async-start(s8[4718592]{0:T(1024)(128)(4,1)} %bitcast.125), calls=%async_computation.3 | async-start | bytes 8388608
  444.1 5.1 %slice-start = ((s8[4718592]{0:T(1024)(128)(4,1)}), s8[4194304]{0:T(1024)(128)(4,1)S(1)}, s32[]{:S(2)}) async-start(s8[4718592]{0:T(1024)(128)(4,1)} %bitcast.123), calls=%async_computation | async-start | bytes 8388608
  446.3 3.2 slice-start.1

commit v3 on v2

--- a/solution.py
+++ b/solution.py
@@ -60,7 +60,7 @@
 
 
 def mod(value, size):
-    return lax.rem(value + 2 * size, size)
+    return lax.rem(value + 4 * size, size)
 
 
 class Place:
@@ -89,11 +89,11 @@
         ]
 
     def block(self, j, h=None):
-        return mod((self.h if h is None else h) + 2 * j, 4)
+        return mod((self.h if h is None else h) + 2 * (j + self.s), 4)
 
 
 def params(**more):
-    return pltpu.CompilerParams(has_side_effects=True, vmem_limit_bytes=56 * 2**20, **more)
+    return pltpu.CompilerParams(has_side_effects=True, vmem_limit_bytes=60 * 2**20, **more)
 
 
 def line_gather(me, own, whole, sems, slot):
@@ -246,7 +246,7 @@
 
     owns = lax.rem(mod(h - s, 4), 2) == 0
     target = jnp.where(owns, h, me.near)
-    which = lax.div(mod(target - s, 4), 2)
+    turned = lax.div(mod(s - target, 4), 2)
     first = jnp.where(owns, 0, half)
 
     def chunk(c):
@@ -256,6 +256,7 @@
         for i in range(1, seqs):
             to = mod(s + i, seqs)
             rows = chunk(first + c)
+            which = lax.rem(turned + to, 2)
             send(
                 tok.at[per * to + which, rows],
                 tok_all.at[which, s, rows],
@@ -340,7 +341,7 @@
     def _(n):
         hop, j = lax.div(n, per), lax.rem(n, per)
         source = jnp.where(hop == 0, h, jnp.where(hop == 1, me.across, jnp.where(hop == 2, me.near, me.near_across)))
-        block = mod(source + 2 * j, 4)
+        block = me.block(j, source)
 
         @pl.when((hop >= 2) & (block != s))
         def _():
@@ -387,7 +388,7 @@
             mixed = jnp.dot(part, value, preferred_element_type=F32)
             out[unit, :, head * HEAD_DIM : (head + 1) * HEAD_DIM] = mixed.astype(BF16)
         pltpu.make_async_copy(slot.at[turn], probs.at[j, :, rows, :], p_sem.at[turn]).start()
-        owner = mod(block - 2 * j, 4)
+        owner = mod(block - 2 * (j + s), 4)
         away = mod(owner - h, 4)
 
         @pl.when(away == 0)
@@ -403,6 +404,7 @@
             @pl.when(unit == i - 1)
             def _():
                 to = mod(s + i, seqs)
+                which = lax.rem(turned + to, 2)
                 half_rows = pl.ds(pl.multiple_of(first * part_rows, part_rows), half * part_rows)
                 send(
                     cot.at[per * to + which, half_rows],
@@ -718,35 +720,44 @@
     per = own.shape[0]
     turn = mod(s - h, 4)
     mine = lax.rem(turn, 2) == 0
-    which = lax.div(turn, 2)
-
-    def start():
-        for j in range(per):
-            to = me.block(j)
-
-            @pl.when(to != s)
-            def _():
-                send(own.at[j], home.at[per * s + j], z_send.at[j], z_recv.at[s], seq=to)
-
-            @pl.when(to == s)
-            def _():
-                pltpu.make_async_copy(own.at[j], home.at[per * s + j], ls).start()
-
-    def forward():
+    turned = lax.div(turn, 2)
+
+    def sources(j, across):
+        return [lax.rem(turned + j + across, 2) + 2 * k for k in range(seqs // 2)]
+
+    def start(j):
+        to = me.block(j)
+
+        @pl.when(to != s)
+        def _():
+            send(own.at[j], home.at[per * s + j], z_send.at[j], z_recv.at[s], seq=to)
+
+        @pl.when(to == s)
+        def _():
+            pltpu.make_async_copy(own.at[j], home.at[per * s + j], ls).start()
+
+    def pass_on(j):
         @pl.when(mine)
         def _():
-            for i in range(seqs):
-                source = mod(s + i, seqs)
-                here = home.at[per * source + which]
-                if i == 0:
+            for source in sources(j, 0):
+                here = home.at[per * source + j]
+
+                @pl.when(source == s)
+                def _():
                     pltpu.make_async_copy(here, here, ls).wait()
-                else:
+
+                @pl.when(source != s)
+                def _():
                     arrived(here, z_recv.at[source])
+
                 send(here, here, h_send.at[0, source], h_recv.at[0, source], head=me.across)
                 send(here, here, h_send.at[1, source], h_recv.at[1, source], head=me.near)
-            for i in range(seqs):
-                source = mod(s + i, seqs)
-                there = home.at[per * source + 1 - which]
+
+    def pass_near(j):
+        @pl.when(mine)
+        def _():
+            for source in sources(j, 1):
+                there = home.at[per * source + j]
                 arrived(there, h_recv.at[0, source])
                 send(there, there, h_send.at[2, source], h_recv.at[2, source], head=me.near)
 
@@ -770,299 +781,408 @@
                 arrived(home.at[per * source], h_recv.at[1, source])
                 arrived(home.at[per * source + 1], h_recv.at[2, source])
 
-    return start, forward, finish
+    return start, pass_on, pass_near, finish
 
 
 def home_sems(per, seqs):
     return [DMA(()), DMA((per,)), DMA((seqs,)), DMA((3, seqs)), DMA((3, seqs))]
 
 
-def grads_kernel(seqs, dps, grad, result, grad_all, home, ls, a_send, a_recv, *sems):
+def add_groups(me, parts, dp_take, seq_take, result, dp_send, dp_recv, seq_send, seq_recv):
+    s, d, seqs, dps = me.s, me.d, me.seqs, me.dps
+
+    def start():
+        for i in range(1, dps):
+            to = mod(d + i, dps)
+            send(parts.at[to], dp_take.at[i - 1], dp_send.at[i - 1], dp_recv.at[i - 1], dp=to)
+
+    def middle():
+        for i in range(1, dps):
+            arrived(dp_take.at[i - 1], dp_recv.at[i - 1])
+        for n in range(seqs):
+            to = mod(s + n, seqs)
+            total = parts[d, to].astype(F32)
+            for i in range(1, dps):
+                total = total + dp_take[i - 1, to].astype(F32)
+            parts[d, to] = total.astype(parts.dtype)
+            if n:
+                send(parts.at[d, to], seq_take.at[n - 1], seq_send.at[n - 1], seq_recv.at[n - 1], seq=to)
+
+    def end():
+        total = parts[d, s].astype(F32)
+        for n in range(1, seqs):
+            arrived(seq_take.at[n - 1], seq_recv.at[n - 1])
+            total = total + seq_take[n - 1].astype(F32)
+        result[...] = total
+        for i in range(1, dps):
+            pltpu.make_async_copy(dp_take.at[0], dp_take.at[0], dp_send.at[i - 1]).wait()
+        for n in range(1, seqs):
+            pltpu.make_async_copy(seq_take.at[0], seq_take.at[0], seq_send.at[n - 1]).wait()
+
+    return start, middle, end
+
+
+def group_scratch(seqs, dps, shape, dtype):
+    return [
+        pltpu.VMEM((dps, seqs) + shape, dtype),
+        pltpu.VMEM((max(1, dps - 1), seqs) + shape, dtype),
+        pltpu.VMEM((seqs - 1,) + shape, dtype),
+    ]
+
+
+def group_sems(seqs, dps):
+    return [DMA((max(1, dps - 1),))] * 2 + [DMA((seqs - 1,))] * 2
+
+
+def back_kernel(
+    seqs, dps, heads,
+    attn_grad, result, hidden_grad, own_tok, heads_all, wo_all, split, probs, attn_input, weights, gains, router, gain_f,
+    output, tokens_home, w_sum, small_sum, wo_sum, gain_sum, bias_sum,
+    hsend, grad_all, slot, ext, made, dk_sum, dv_sum, w_acc, x_out, x_near, x_far, tg, wo_part, wo_near, wo_far,
+    w_parts, w_dp, w_seq, wo_parts, wo_dp, wo_seq, g_parts, g_dp, g_seq, g_acc, bias, bias_take, small, gsmall,
+    p_sem, a_send, a_recv, n_send, n_recv, f_send, f_recv, on_send, on_recv, of_send, of_recv,
+    b_send, b_recv, s_send, s_recv, t_send, t_recv, *sems
+):
     me = Place(seqs, dps)
-    h = me.h
-    per = result.shape[0]
-    start, forward, finish = send_home(me, result, home, *sems)
-    greet(me.seq_peers() + [{"head": mod(h + i, 4)} for i in range(1, 4)])
-    copies = []
-    for i in range(1, 4):
-        to = mod(h + i, 4)
-        for j in range(per):
-            copies.append(
+    h, s, d = me.h, me.s, me.d
+    per, span, width = attn_grad.shape
+    blocks = seqs
+    length = blocks * span
+    local = heads * HEAD_DIM
+    groups = seqs * dps
+    shard = width // groups
+    padded = w_sum.shape[0]
+    lanes = weights.shape[1]
+    experts = router.shape[1]
+    buckets = 32
+    others = [(i, j) for i in range(seqs) for j in range(dps) if i or j]
+    order = (h, me.near, me.across, me.near_across)
+    greet(me.group_peers() + [{"head": mod(h + i, 4)} for i in range(1, 4)])
+    out_home = send_home(me, result, output, *sems[0:5])
+    grad_home = send_home(me, tg, tokens_home, *sems[5:10])
+    w_group = add_groups(me, w_parts, w_dp, w_seq, w_sum, *sems[10:14])
+    wo_group = add_groups(me, wo_parts, wo_dp, wo_seq, wo_sum, *sems[14:18])
+    g_group = add_groups(me, g_parts, g_dp, g_seq, gain_sum, *sems[18:22])
+
+    def fetch(j, n):
+        q = jnp.where(n == 0, h, jnp.where(n == 1, me.near, jnp.where(n == 2, me.across, me.near_across)))
+        block = me.block(j, q)
+        rows = pl.ds(pl.multiple_of(block * span, span), span)
+        turn = lax.rem(n, 2)
+        return q, block, rows, turn, pltpu.make_async_copy(probs.at[j, :, rows, :], slot.at[turn], p_sem.at[turn])
+
+    fetch(0, 0)[4].start()
+    for j in range(per):
+        for i in (1, 2, 3, 0):
+            to = mod(h + i, 4)
+            grad = contract(attn_grad[j], wo_all[to], 1, 1).astype(BF16)
+            if i:
+                hsend[j, i - 1] = grad
                 send(
-                    grad.at[to, j],
+                    hsend.at[j, i - 1],
                     grad_all.at[j, me.block(j)],
                     a_send.at[i - 1, j],
                     a_recv.at[i - 1, j],
                     head=to,
                 )
-            )
-    own_copies = [pltpu.make_async_copy(grad.at[h, j], grad_all.at[j, me.block(j)], ls.at[j]) for j in range(per)]
-    for copy in own_copies:
-        copy.start()
-    start()
-    forward()
-    finish()
-    for copy in own_copies:
-        copy.wait()
-    for copy in copies:
-        copy.wait_send()
-    for i in range(1, 4):
-        source = mod(h - i, 4)
+            else:
+                grad_all[j, me.block(j)] = grad
+    for k, q in enumerate((me.near_across, me.near, me.across, h)):
+        total = jnp.zeros((local, width), F32)
         for j in range(per):
-            arrived(grad_all.at[j, me.block(j, source)], a_recv.at[i - 1, j])
-
-
-def gather_grads(grad, result, seqs, dps):
-    _, per, span, width = grad.shape
-    return pl.pallas_call(
-        functools.partial(grads_kernel, seqs, dps),
-        out_shape=(
-            jax.ShapeDtypeStruct((per, seqs, span, width), BF16),
-            jax.ShapeDtypeStruct((per * seqs,) + result.shape[1:], BF16),
+            total = total + contract(heads_all[q, j], attn_grad[j], 0, 0)
+        wo_part[k] = total.astype(BF16)
+        if k < 2:
+            send(wo_part.at[k], wo_near.at[k], on_send.at[k], on_recv.at[k], head=me.near)
+    for j in range(per):
+        out_home[0](j)
+    ext[...] = jnp.zeros_like(ext)
+    made[...] = jnp.zeros_like(made)
+
+    def wo_across():
+        arrived(wo_near.at[0], on_recv.at[0])
+        wo_part[2] = (wo_part[2].astype(F32) + wo_near[0].astype(F32)).astype(BF16)
+        send(wo_part.at[2], wo_far, of_send, of_recv, head=me.across)
+
+    def wo_total():
+        arrived(wo_near.at[1], on_recv.at[1])
+        arrived(wo_far, of_recv)
+        total = (wo_part[3].astype(F32) + wo_near[1].astype(F32) + wo_far[...].astype(F32)).astype(BF16)
+        for g in range(groups):
+            hot = spread_hot(g * shard, shard, width)
+            wo_parts[g % dps, g // dps] = contract(total, hot, 1, 1).astype(BF16)
+        wo_group[0]()
+
+    def x_partial(j):
+        for k, q in enumerate((me.near_across, me.near, me.across, h)):
+            rows = pl.ds(pl.multiple_of(me.block(j, q) * span, span), span)
+            x_out[j, k] = contract(made[j, rows, :], weights[...], 1, 1).astype(BF16)
+            if k < 2:
+                send(x_out.at[j, k], x_near.at[j, k], n_send.at[j, k], n_recv.at[j, k], head=me.near)
+
+    def x_across(j):
+        arrived(x_near.at[j, 0], n_recv.at[j, 0])
+        x_out[j, 2] = (x_out[j, 2].astype(F32) + x_near[j, 0].astype(F32)).astype(BF16)
+        send(x_out.at[j, 2], x_far.at[j], f_send.at[j], f_recv.at[j], head=me.across)
+
+    def x_total(j):
+        arrived(x_near.at[j, 1], n_recv.at[j, 1])
+        arrived(x_far.at[j], f_recv.at[j])
+        grad = x_out[j, 3].astype(F32) + x_near[j, 1].astype(F32) + x_far[j].astype(F32)
+        v = own_tok[j].astype(F32)
+        inverse = lax.rsqrt(jnp.mean(v * v, axis=-1, keepdims=True) + EPS)
+        r = v * inverse
+        u = grad * gains[0:1, :]
+        back = (u - r * jnp.mean(u * r, axis=-1, keepdims=True)) * inverse
+        tg[j] = (hidden_grad[j] + back).astype(BF16)
+        grad_home[0](j)
+        g_acc[0:1, :] += jnp.sum(grad * r, axis=0, keepdims=True)
+
+    def attention(j, service):
+        @pl.loop(0, blocks)
+        def _(n):
+            q, block, rows, turn, copy = fetch(j, n)
+            away = mod(h - q, 4)
+
+            @pl.when(away > 0)
+            def _():
+                arrived(grad_all.at[j, block], a_recv.at[away - 1, j])
+
+            copy.wait()
+
+            @pl.when(n < blocks - 1)
+            def _():
+                fetch(j, n + 1)[4].start()
+
+            if j < per - 1:
+
+                @pl.when(n == blocks - 1)
+                def _():
+                    fetch(j + 1, 0)[4].start()
+
+            window = pl.ds(pl.multiple_of((blocks - 1 - block) * span, span), length)
+            for head in range(heads):
+                cols = slice(head * HEAD_DIM, (head + 1) * HEAD_DIM)
+                query = split[j, head, rows, :]
+                key, value = split[j, heads + head], split[j, 2 * heads + head]
+                grad = grad_all[j, block, :, cols]
+                part = slot[turn, head]
+                prob_grad = contract(grad, value, 1, 1)
+                wide = part.astype(F32)
+                delta = jnp.sum(wide * prob_grad, axis=-1, keepdims=True)
+                score_grad = wide * (prob_grad - delta)
+                ext[head, :, window] += score_grad
+                low = score_grad.astype(BF16)
+                made[j, rows, cols] = jnp.dot(low, key, preferred_element_type=F32).astype(BF16)
+                dk = contract(low, query, 0, 0)
+                dv = contract(part, grad, 0, 0)
+
+                @pl.when(n == 0)
+                def _():
+                    dk_sum[head] = dk
+                    dv_sum[head] = dv
+
+                @pl.when(n > 0)
+                def _():
+                    dk_sum[head] += dk
+                    dv_sum[head] += dv
+
+            for k, call in enumerate(service):
+
+                @pl.when(n == k)
+                def _():
+                    for act in call:
+                        act()
+
+        for head in range(heads):
+            cols = slice(local + head * HEAD_DIM, local + (head + 1) * HEAD_DIM)
+            made[j, :, cols] = dk_sum[head].astype(BF16)
+            cols = slice(2 * local + head * HEAD_DIM, 2 * local + (head + 1) * HEAD_DIM)
+            made[j, :, cols] = dv_sum[head].astype(BF16)
+        x_partial(j)
+        total = contract(attn_input[j], made[j], 0, 0)
+        if j == 0:
+            w_acc[...] = total
+        else:
+            w_acc[...] += total
+
+    g_acc[...] = jnp.zeros_like(g_acc)
+    g_acc[1:2, :] = gain_f[...]
+    attention(
+        0,
+        (
+            (wo_across,),
+            (lambda: out_home[1](0),),
+            (wo_total, lambda: out_home[1](1)),
+            (lambda: out_home[2](0), lambda: out_home[2](1)),
         ),
-        in_specs=[ANY] * 2,
-        out_specs=[ANY] * 2,
-        scratch_shapes=[DMA((per,)), DMA((3, per)), DMA((3, per))] + home_sems(per, seqs),
-        compiler_params=params(collective_id=4),
-        name="gather_grads",
-    )(grad, result)
-
-
-def input_kernel(
-    seqs, dps, partial, weight, total, weight_out, own, near, far_out, far_in, wown, wnear, wfar_out, wfar_in,
-    ls, n_send, n_recv, x_send, x_recv, wls, wn_send, wn_recv, wx_send, wx_recv
-):
-    me = Place(seqs, dps)
-    h = me.h
-    per = total.shape[0]
-    greet(me.head_pair())
-    for j in range(per):
-        for k, head in enumerate((me.near_across, me.near)):
-            send(partial.at[j, me.block(j, head)], near.at[k, j], n_send.at[k, j], n_recv.at[k, j], head=me.near)
-        for k, head in enumerate((me.across, h)):
-            pltpu.make_async_copy(partial.at[j, me.block(j, head)], own.at[k, j], ls.at[k, j]).start()
-    for k, head in enumerate((me.near_across, me.near)):
-        send(weight.at[head], wnear.at[k], wn_send.at[k], wn_recv.at[k], head=me.near)
-    for k, head in enumerate((me.across, h)):
-        pltpu.make_async_copy(weight.at[head], wown.at[k], wls.at[k]).start()
-    for j in range(per):
-        arrived(near.at[0, j], n_recv.at[0, j])
-        pltpu.make_async_copy(own.at[0, j], own.at[0, j], ls.at[0, j]).wait()
-        far_out[j] = (own[0, j].astype(F32) + near[0, j].astype(F32)).astype(BF16)
-        send(far_out.at[j], far_in.at[j], x_send.at[j], x_recv.at[j], head=me.across)
-    arrived(wnear.at[0], wn_recv.at[0])
-    pltpu.make_async_copy(wown.at[0], wown.at[0], wls.at[0]).wait()
-    wfar_out[...] = (wown[0].astype(F32) + wnear[0].astype(F32)).astype(BF16)
-    send(wfar_out, wfar_in, wx_send, wx_recv, head=me.across)
-    for j in range(per):
-        arrived(near.at[1, j], n_recv.at[1, j])
-        pltpu.make_async_copy(own.at[1, j], own.at[1, j], ls.at[1, j]).wait()
-        arrived(far_in.at[j], x_recv.at[j])
-        total[j] = own[1, j].astype(F32) + near[1, j].astype(F32) + far_in[j].astype(F32)
-    arrived(wnear.at[1], wn_recv.at[1])
-    pltpu.make_async_copy(wown.at[1], wown.at[1], wls.at[1]).wait()
-    arrived(wfar_in, wx_recv)
-    weight_out[...] = wown[1].astype(F32) + wnear[1].astype(F32) + wfar_in[...].astype(F32)
-    for j in range(per):
-        for k in range(2):
-            pltpu.make_async_copy(near.at[k, j], near.at[k, j], n_send.at[k, j]).wait()
-        pltpu.make_async_copy(far_out.at[j], far_out.at[j], x_send.at[j]).wait()
-    for k in range(2):
-        pltpu.make_async_copy(wnear.at[k], wnear.at[k], wn_send.at[k]).wait()
-    pltpu.make_async_copy(wfar_out, wfar_out, wx_send).wait()
-
-
-def add_heads(partial, weight, seqs, dps):
-    per, _, span, width = partial.shape
-    block = (per, span, width)
-    wblock = weight.shape[1:]
-    return pl.pallas_call(
-        functools.partial(input_kernel, seqs, dps),
-        out_shape=(jax.ShapeDtypeStruct(block, F32), jax.ShapeDtypeStruct(wblock, F32)),
-        in_specs=[ANY] * 2,
-        out_specs=[VMEM] * 2,
-        scratch_shapes=[
-            pltpu.VMEM((2,) + block, BF16),
-            pltpu.VMEM((2,) + block, BF16),
-            pltpu.VMEM(block, BF16),
-            pltpu.VMEM(block, BF16),
-            pltpu.VMEM((2,) + wblock, BF16),
-            pltpu.VMEM((2,) + wblock, BF16),
-            pltpu.VMEM(wblock, BF16),
-            pltpu.VMEM(wblock, BF16),
-        ]
-        + [DMA((2, per))] * 3
-        + [DMA((per,))] * 2
-        + [DMA((2,))] * 3
-        + [DMA(())] * 2,
-        compiler_params=params(collective_id=5),
-        name="add_heads",
-    )(partial, weight)
-
-
-def last_kernel(
-    seqs, dps, grad, weights, bias, home, weights_sum, bias_sum, wsum, wtake, ytake, btake, small,
-    ls, y_send, y_recv, w_send, w_recv, b_send, b_recv, s_send, s_recv, *sems
-):
-    me = Place(seqs, dps)
-    h, s, d = me.h, me.s, me.d
-    start, forward, finish = send_home(me, grad, home, *sems)
-    others = [(i, j) for i in range(seqs) for j in range(dps) if i or j]
-    greet(me.group_peers() + [{"head": mod(h + i, 4)} for i in range(1, 4)])
-    for i in range(1, dps):
-        to = mod(d + i, dps)
-        send(weights.at[to], ytake.at[i - 1], y_send.at[i - 1], y_recv.at[i - 1], dp=to)
-    mine_y = pltpu.make_async_copy(weights.at[d], wsum, ls)
-    mine_y.start()
+    )
+    attention(
+        1,
+        (
+            (lambda: x_across(0), wo_group[1]),
+            (lambda: x_total(0),),
+            (lambda: grad_home[1](0),),
+            (lambda: grad_home[2](0),),
+        ),
+    )
+    x_across(1)
+    w_acc[:, 3 * local : 3 * local + experts] = router[...]
+    low = w_acc[...].astype(BF16)
+    if shard % 16:
+        low = contract(squeeze_hot(shard, padded, width, groups), low, 0, 0).astype(BF16)
+    for g in range(groups):
+        w_parts[g % dps, g // dps] = low[g * padded : (g + 1) * padded, :]
+    w_group[0]()
+    turn = lax.broadcasted_iota(jnp.int32, (4 * span, 128), 0)
+    bucket = bucket_of(jnp.where(turn < 3 * span, turn, turn - 4 * span) - span, buckets)
+    hot = (bucket == lax.broadcasted_iota(jnp.int32, (4 * span, 128), 1)).astype(F32)
+    lane = lax.broadcasted_iota(jnp.int32, (1, 128), 1)
+    head_row = lax.broadcasted_iota(jnp.int32, (8, 4 * span), 0)
+    diagonals = jnp.zeros((8, 4 * span), F32)
+    far_row = lax.broadcasted_iota(jnp.int32, (8, 128), 0)
+    far = jnp.zeros((8, 128), F32)
+    for head in range(heads):
+        eight = jnp.zeros((8, 4 * span), F32)
+        for group in range(span // 8):
+            piece = ext[head, group * 8 : (group + 1) * 8, 2 * span : 5 * span]
+            piece = jnp.concatenate([piece, jnp.zeros((8, span), F32)], axis=1)
+            eight = eight + pltpu.roll(piece, (4 * span - 8 * group) % (4 * span), 1)
+        one = jnp.zeros((8, 4 * span), F32)
+        for i in range(8):
+            line = jnp.broadcast_to(eight[i : i + 1, :], (8, 4 * span))
+            one = one + pltpu.roll(line, (4 * span - i) % (4 * span), 1)
+        diagonals = jnp.where(head_row == head, one, diagonals)
+        left, right = jnp.sum(ext[head, :, : 2 * span]), jnp.sum(ext[head, :, 5 * span :])
+        sides = jnp.where(lane == buckets // 2 - 1, left, jnp.where(lane == buckets - 1, right, 0.0))
+        far = jnp.where(far_row == head, sides, far)
+    bias[...] = far + jnp.dot(diagonals, hot, preferred_element_type=F32, precision=lax.Precision.HIGHEST)
     for n, (i, j) in enumerate(others):
-        send(bias, btake.at[n], b_send.at[n], b_recv.at[n], seq=mod(s + i, seqs), dp=mod(d + j, dps))
-    start()
-    mine_y.wait()
-    for i in range(1, dps):
-        arrived(ytake.at[i - 1], y_recv.at[i - 1])
-    for t in range(seqs):
-        acc = wsum[t].astype(F32)
-        for i in range(1, dps):
-            acc = acc + ytake[i - 1, t].astype(F32)
-        wsum[t] = acc.astype(BF16)
-    for i in range(1, seqs):
-        to = mod(s + i, seqs)
-        send(wsum.at[to], wtake.at[i - 1], w_send.at[i - 1], w_recv.at[i - 1], seq=to)
-    forward()
-    acc = wsum[s].astype(F32)
-    for i in range(1, seqs):
-        arrived(wtake.at[i - 1], w_recv.at[i - 1])
-        acc = acc + wtake[i - 1].astype(F32)
-    weights_sum[...] = acc
-    lanes = small.shape[-1]
-    small[0] = acc[:, acc.shape[-1] - lanes :]
+        send(bias, bias_take.at[n], b_send.at[n], b_recv.at[n], seq=mod(s + i, seqs), dp=mod(d + j, dps))
+    w_group[1]()
+    x_total(1)
+    g_rows = g_acc[...].astype(BF16)
+    for g in range(groups):
+        g_parts[g % dps, g // dps] = contract(g_rows, spread_hot(g * shard, shard, width), 1, 1)
+    g_group[0]()
+    g_group[1]()
+    w_group[2]()
+    small[0] = w_sum[:, lanes - small.shape[-1] :]
     for i in range(1, 4):
         send(small.at[0], small.at[i], s_send.at[i - 1], s_recv.at[i - 1], head=mod(h + i, 4))
+    grad_home[1](1)
+    g_group[2]()
+    gsmall[0] = gain_sum[...]
+    for i in range(1, 4):
+        send(gsmall.at[0], gsmall.at[i], t_send.at[i - 1], t_recv.at[i - 1], head=mod(h + i, 4))
+    grad_home[2](1)
+    wo_group[2]()
     total = bias[...]
     for n in range(len(others)):
-        arrived(btake.at[n], b_recv.at[n])
-        total = total + btake[n]
+        arrived(bias_take.at[n], b_recv.at[n])
+        total = total + bias_take[n]
     bias_sum[...] = total
-    tail = small[0]
+    total, gain_total = small[0], gsmall[0]
     for i in range(1, 4):
         arrived(small.at[i], s_recv.at[i - 1])
-        tail = tail + small[i]
-    weights_sum[:, acc.shape[-1] - lanes :] = tail
-    for i in range(1, 4):
-        pltpu.make_async_copy(small.at[0], small.at[0], s_send.at[i - 1]).wait()
-    for i in range(1, dps):
-        pltpu.make_async_copy(ytake.at[0], ytake.at[0], y_send.at[i - 1]).wait()
-    for i in range(1, seqs):
-        pltpu.make_async_copy(wsum.at[0], wsum.at[0], w_send.at[i - 1]).wait()
+        arrived(gsmall.at[i], t_recv.at[i - 1])
+        total = total + small[i]
+        gain_total = gain_total + gsmall[i]
+    small_sum[...] = total
+    gain_sum[...] = gain_total
+    out_home[3]()
+    grad_home[3]()
+    for j in range(per):
+        for i in range(3):
+            pltpu.make_async_copy(hsend.at[0, 0], hsend.at[0, 0], a_send.at[i, j]).wait()
+        for k in range(2):
+            pltpu.make_async_copy(x_near.at[0, 0], x_near.at[0, 0], n_send.at[j, k]).wait()
+        pltpu.make_async_copy(x_near.at[0, 0], x_near.at[0, 0], f_send.at[j]).wait()
+    for k in range(2):
+        pltpu.make_async_copy(wo_far, wo_far, on_send.at[k]).wait()
+    pltpu.make_async_copy(wo_far, wo_far, of_send).wait()
+    for i in range(3):
+        pltpu.make_async_copy(small.at[0], small.at[0], s_send.at[i]).wait()
+        pltpu.make_async_copy(gsmall.at[0], gsmall.at[0], t_send.at[i]).wait()
     for n in range(len(others)):
-        pltpu.make_async_copy(btake.at[0], btake.at[0], b_send.at[n]).wait()
-    finish()
-
-
-def finish_grads(grad, weights, bias, seqs, dps, small):
-    per, span, width = grad.shape
-    _, _, rows, lanes = weights.shape
+        pltpu.make_async_copy(bias, bias, b_send.at[n]).wait()
+
+
+def back_pass(
+    attn_grad, result, hidden_grad, own_tok, heads_all, wo_all, split, probs, attn_input, weights, gains, router, gain_f,
+    seqs, dps
+):
+    per, span, width = attn_grad.shape
+    length = seqs * span
+    heads = probs.shape[1]
+    local = heads * HEAD_DIM
     groups = seqs * dps
+    shard = width // groups
+    padded = up_to(shard, 16)
+    lanes = weights.shape[1]
+    block = (span, width)
     return pl.pallas_call(
-        functools.partial(last_kernel, seqs, dps),
+        functools.partial(back_kernel, seqs, dps, heads),
         out_shape=(
-            jax.ShapeDtypeStruct((per * seqs, span, width), BF16),
-            jax.ShapeDtypeStruct((rows, lanes), F32),
-            jax.ShapeDtypeStruct(bias.shape, F32),
+            jax.ShapeDtypeStruct((per * seqs,) + block, BF16),
+            jax.ShapeDtypeStruct((per * seqs,) + block, BF16),
+            jax.ShapeDtypeStruct((padded, lanes), F32),
+            jax.ShapeDtypeStruct((padded, 128 * (lanes // 128 - 3 * local // 128)), F32),
+            jax.ShapeDtypeStruct((local, 128), F32),
+            jax.ShapeDtypeStruct((8, 128), F32),
+            jax.ShapeDtypeStruct((8, 128), F32),
         ),
-        in_specs=[ANY, ANY, VMEM],
-        out_specs=[ANY, VMEM, VMEM],
+        in_specs=[VMEM, ANY] + [VMEM] * 5 + [ANY] + [VMEM] * 5,
+        out_specs=[ANY] * 2 + [VMEM] * 5,
         scratch_shapes=[
-            pltpu.VMEM((seqs, rows, lanes), BF16),
-            pltpu.VMEM((seqs - 1, rows, lanes), BF16),
-            pltpu.VMEM((max(1, dps - 1), seqs, rows, lanes), BF16),
-            pltpu.VMEM((groups - 1,) + bias.shape, F32),
-            pltpu.VMEM((4, rows, small), F32),
+            pltpu.VMEM((per, 3, span, local), BF16),
+            pltpu.VMEM((per, seqs, span, local), BF16),
+            pltpu.VMEM((2, heads, span, length), BF16),
+            pltpu.VMEM((heads, span, 7 * span), F32),
+            pltpu.VMEM((per, length, lanes), BF16),
+            pltpu.VMEM((heads, length, HEAD_DIM), F32),
+            pltpu.VMEM((heads, length, HEAD_DIM), F32),
+            pltpu.VMEM((width, lanes), F32),
+            pltpu.VMEM((per, 4) + block, BF16),
+            pltpu.VMEM((per, 2) + block, BF16),
+            pltpu.VMEM((per,) + block, BF16),
+            pltpu.VMEM((per,) + block, BF16),
+            pltpu.VMEM((4, local, width), BF16),
+            pltpu.VMEM((2, local, width), BF16),
+            pltpu.VMEM((local, width), BF16),
+        ]
+        + group_scratch(seqs, dps, (padded, lanes), BF16)
+        + group_scratch(seqs, dps, (local, 128), BF16)
+        + group_scratch(seqs, dps, (8, 128), F32)
+        + [
+            pltpu.VMEM((8, width), F32),
+            pltpu.VMEM((8, 128), F32),
+            pltpu.VMEM((groups - 1, 8, 128), F32),
+            pltpu.VMEM((4, padded, 128 * (lanes // 128 - 3 * local // 128)), F32),
+            pltpu.VMEM((4, 8, 128), F32),
+            DMA((2,)),
+            DMA((3, per)),
+            DMA((3, per)),
+            DMA((per, 2)),
+            DMA((per, 2)),
+            DMA((per,)),
+            DMA((per,)),
+            DMA((2,)),
+            DMA((2,)),
             DMA(()),
-            DMA((max(1, dps - 1),)),
-            DMA((max(1, dps - 1),)),
-            DMA((seqs - 1,)),
-            DMA((seqs - 1,)),
+            DMA(()),
             DMA((groups - 1,)),
             DMA((groups - 1,)),
             DMA((3,)),
             DMA((3,)),
+            DMA((3,)),
+            DMA((3,)),
         ]
-        + home_sems(per, seqs),
-        compiler_params=params(collective_id=6),
-        name="finish_grads",
-    )(grad, weights, bias)
-
-
-def attend_back_kernel(
-    heads, blocks, span, s_ref, g_ref, p_ref, dq_ref, dk_ref, dv_ref, band_ref, far_ref, dk_sum, dv_sum
-):
-    first = pl.program_id(0) == 0
-    for head in range(heads):
-        cols = slice(head * HEAD_DIM, (head + 1) * HEAD_DIM)
-        key = s_ref[0, heads + head]
-        value = s_ref[0, 2 * heads + head]
-        for q_block in range(blocks):
-            rows = slice(q_block * span, (q_block + 1) * span)
-            query = s_ref[0, head, rows, :]
-            grad = g_ref[0, rows, cols]
-            weights = p_ref[0, head, rows, :]
-            prob_grad = lax.dot_general(grad, value, (((1,), (1,)), ((), ())), preferred_element_type=F32)
-            wide = weights.astype(F32)
-            delta = jnp.sum(wide * prob_grad, axis=-1, keepdims=True)
-            score_grad = wide * (prob_grad - delta)
-            for k_block in range(blocks):
-                part = score_grad[:, k_block * span : (k_block + 1) * span]
-                step = k_block - q_block
-                if abs(step) <= 1:
-                    where = (head, slice(None), slice((step + 1) * span, (step + 2) * span))
-                    begin = first & (q_block == (1 if step < 0 else 0))
-                    old = band_ref[where]
-                    band_ref[where] = jnp.where(begin, 0.0, old) + part
-                else:
-                    side = 0 if step < 0 else 1
-                    begin = first & ((q_block, k_block) == ((2, 0) if side == 0 else (0, 2)))
-                    flat = jnp.sum(part.reshape(span // 8, 8, span), axis=0)
-                    old = far_ref[head, side]
-                    far_ref[head, side] = jnp.where(begin, 0.0, old) + flat
-            low = score_grad.astype(BF16)
-            dq_ref[0, rows, cols] = jnp.dot(low, key, preferred_element_type=F32).astype(BF16)
-            dk = lax.dot_general(low, query, (((0,), (0,)), ((), ())), preferred_element_type=F32)
-            dv = lax.dot_general(weights, grad, (((0,), (0,)), ((), ())), preferred_element_type=F32)
-            if q_block == 0:
-                dk_sum[...] = dk
-                dv_sum[...] = dv
-            else:
-                dk_sum[...] += dk
-                dv_sum[...] += dv
-        dk_ref[0, :, cols] = dk_sum[...].astype(BF16)
-        dv_ref[0, :, cols] = dv_sum[...].astype(BF16)
-
-
-def attend_back(split, grads, probs, heads, blocks, span):
-    per, length, width = grads.shape
-    whole = pl.BlockSpec((1, length, width), lambda j: (j, 0, 0))
-    return pl.pallas_call(
-        functools.partial(attend_back_kernel, heads, blocks, span),
-        grid=(per,),
-        out_shape=(
-            jax.ShapeDtypeStruct((per, length, width), BF16),
-            jax.ShapeDtypeStruct((per, length, width), BF16),
-            jax.ShapeDtypeStruct((per, length, width), BF16),
-            jax.ShapeDtypeStruct((heads, span, 3 * span), F32),
-            jax.ShapeDtypeStruct((heads, 2, 8, span), F32),
-        ),
-        in_specs=[pl.BlockSpec((1,) + split.shape[1:], lambda j: (j, 0, 0, 0)), whole]
-        + [pl.BlockSpec((1, heads, length, length), lambda j: (j, 0, 0, 0))],
-        out_specs=[whole] * 3
-        + [
-            pl.BlockSpec((heads, span, 3 * span), lambda j: (0, 0, 0)),
-            pl.BlockSpec((heads, 2, 8, span), lambda j: (0, 0, 0, 0)),
-        ],
-        scratch_shapes=[pltpu.VMEM((length, HEAD_DIM), F32)] * 2,
-        compiler_params=pltpu.CompilerParams(vmem_limit_bytes=56 * 2**20),
-        name="attend_back",
-    )(split, grads, probs)
+        + home_sems(per, seqs) * 2
+        + group_sems(seqs, dps) * 3,
+        compiler_params=params(collective_id=4),
+        name="back",
+    )(attn_grad, result, hidden_grad, own_tok, heads_all, wo_all, split, probs, attn_input, weights, gains, router, gain_f)
 
 
 def up_to(value, unit):
@@ -1116,14 +1236,10 @@
         seqs,
         dps,
     )
-    project_weight = weights[:, : 3 * local_width]
     router_full = weights[:, 3 * local_width : 3 * local_width + experts]
-    gain_one, gain_two = gains[0], gains[1]
-    attn_input = attn_input.reshape(count, width)
-    offset = jnp.arange(3 * span, dtype=jnp.int32)[None, :] - span - jnp.arange(span, dtype=jnp.int32)[:, None]
-    bucket = bucket_of(offset, bucket_count)
+    gain_two = gains[1]
     heads_all = heads_all.reshape(4, own_rows, local_width)
-    own_blocks = [lax.rem(head_at + 2 * j, 4) for j in range(per)]
+    own_blocks = [lax.rem(head_at + 2 * (j + seq_at), 4) for j in range(per)]
     own_inputs = own_tok.reshape(own_rows, width).astype(F32)
     attention = jnp.einsum("htk,hkd->td", heads_all, out_weight, preferred_element_type=F32)
     hidden = own_inputs + attention
@@ -1172,53 +1288,35 @@
     hidden_norm_grad, gain_two_grad = norm_pull(ffn_input_grad)
     hidden_grad = grad_out + hidden_norm_grad
     attn_grad = hidden_grad.astype(BF16)
-    heads_grad = jnp.einsum("td,hkd->htk", attn_grad, out_weight, preferred_element_type=F32).astype(BF16)
-    grad_all, output = gather_grads(
-        heads_grad.reshape(4, per, span, local_width), result.reshape(per, span, width), seqs, dps
+    output, tokens_grad, w_sum, small_sum, wo_sum, gain_sum, bias_sum = back_pass(
+        attn_grad.reshape(per, span, width),
+        result.reshape(per, span, width),
+        hidden_grad.reshape(per, span, width),
+        own_tok,
+        heads_all.reshape(4, per, span, local_width),
+        out_weight,
+        split,
+        probs,
+        attn_input,
+        weights,
+        gains,
+        router_grad,
+        gain_two_grad[None, :],
+        seqs,
+        dps,
     )
-    out_w_part = jnp.einsum("td,htk->hdk", attn_grad, heads_all, preferred_element_type=F32).astype(BF16)
-
-    query_grad, key_grad, value_grad, band_grad, far_grad = attend_back(
-        split, grad_all.reshape(per, length, local_width), probs, heads, seqs, span
-    )
-    bias_grad = jnp.stack(
-        [jnp.sum(jnp.where((bucket == b)[None], band_grad, 0.0), axis=(1, 2)) for b in range(bucket_count)]
-    )
-    far_sum = jnp.sum(far_grad, axis=(2, 3))
-    bias_grad = bias_grad.at[bucket_count // 2 - 1].add(far_sum[:, 0]).at[bucket_count - 1].add(far_sum[:, 1])
-    made_grad = jnp.concatenate([query_grad, key_grad, value_grad], axis=-1).reshape(count, 3 * local_width)
-    project_grad = jnp.einsum("td,tk->dk", attn_input, made_grad, preferred_element_type=F32).astype(BF16)
-    input_part = jnp.einsum("tk,dk->td", made_grad, project_weight, preferred_element_type=F32).astype(BF16)
-    attn_input_grad, out_w_sum = add_heads(input_part.reshape(per, seqs, span, width), out_w_part, seqs, dps)
-    _, first_pull = jax.vjp(normalize, own_inputs, gain_one)
-    input_norm_grad, gain_one_grad = first_pull(attn_input_grad.reshape(own_rows, width))
-    tokens_grad = (hidden_grad + input_norm_grad).astype(BF16).reshape(per, span, width)
-
-    tail = jnp.concatenate(
-        [
-            router_grad,
-            gain_one_grad[:, None],
-            gain_two_grad[:, None],
-            jnp.zeros((width, up_to(experts + 2, 128) - experts - 2), F32),
-        ],
-        axis=1,
-    ).astype(BF16)
-    weights = jnp.concatenate([project_grad, out_w_sum.astype(BF16), tail], axis=1)
-    weights = jnp.swapaxes(weights.reshape(seqs, dps, shard, weights.shape[-1]), 0, 1)
-    bias_pad = jnp.pad(bias_grad, ((0, 0), (0, 128 - heads)))
-    tokens_grad, weights_sum, bias_sum = finish_grads(tokens_grad, weights, bias_pad, seqs, dps, tail.shape[1])
-    at = 4 * local_width
+    at = 3 * local_width - (w_sum.shape[1] - small_sum.shape[1])
     return (
         output,
         tokens_grad,
-        weights_sum[:, at + experts],
-        weights_sum[:, :local_width],
-        weights_sum[:, local_width : 2 * local_width],
-        weights_sum[:, 2 * local_width : 3 * local_width],
-        weights_sum[:, 3 * local_width : at].T,
-        bias_sum[:, :heads],
-        weights_sum[:, at + experts + 1],
-        weights_sum[:, at : at + experts],
+        gain_sum[0, :shard],
+        w_sum[:shard, :local_width],
+        w_sum[:shard, local_width : 2 * local_width],
+        w_sum[:shard, 2 * local_width : 3 * local_width],
+        wo_sum[:, :shard],
+        bias_sum[:heads, :bucket_count].T,
+        gain_sum[1, :shard],
+        small_sum[:shard, at : at + experts],
         up_grad,
         down_grad,
     )

time: 460 us -> 394 us (0.86); the launches traced: 452 us -> 392 us
  other arithmetic: 27.3 us -> 3.99 us
  Pallas kernels: 356 us -> 341 us
  local copies, waits for them, and re-layouts: 47.8 us -> 34.2 us
  matrix products: 19.1 us -> 11.2 us
    pallas_call x4 -> x1, Pallas kernels: 152 us -> 126 us  [back_pass(): pl.pallas_call(functools.partial(back_kernel, seqs, dps, heads), out_shap...]
    reduce_sum x5 -> x0, other arithmetic: 14.3 us -> none  [the longest x2 11.8 us: body(): jnp.sum(jnp.where((bucket == b)[None], band_grad, 0.0), axis=(1, 2))]
    pallas_call x1, Pallas kernels: 118 us -> 128 us  [run_experts(): pl.pallas_call(functools.partial(experts_kernel, seqs, dps, per_expert),...]
    dot_general x4 -> x0, matrix products: 8.94 us -> none  [the longest x1 4.28 us: body(): jnp.einsum('tk,dk->td', made_grad, project_weight, preferred_element_type...]
    eq x1 -> x0, other arithmetic: 6.09 us -> none  [body(): bucket == b]
    concatenate x2 -> x0, local copies, waits for them, and re-layouts: 5.03 us -> none  [body(): jnp.concatenate([project_grad, out_w_sum.astype(BF16), tail], axis=1)]
    unnamed x80 -> x53, local copies, waits for them, and re-layouts: 21.4 us -> 16.4 us
where the time goes in v3:
time: 394 us; the launch traced here: 392 us
  Pallas kernels  341 us (87%)
  local copies, waits for them, and re-layouts  34.2 us (9%)
  matrix products  11.2 us (3%)
  other arithmetic  3.99 us (1%)
    pallas_call x1, Pallas kernels, run_experts(): pl.pallas_call(functools.partial(experts_kernel, seqs, dps, per_expert),...  128 us
    pallas_call x1, Pallas kernels, back_pass(): pl.pallas_call(functools.partial(back_kernel, seqs, dps, heads), out_shap...  126 us
    pallas_call x1, Pallas kernels, front(): pl.pallas_call(functools.partial(front_kernel, seqs, dps, heads), out_sha...  86.6 us
    unnamed x53, local copies, waits for them, and re-layouts  16.4 us

profile of v3, /device:TPU:0, one launch (start us, length us, event | category | flops | bytes accessed | tf_op | source)
XLA Modules:
  0.0 391.8 jit_solution(15304149720076086132)
XLA Ops:
  0.7 1.3 copy.62
  2.0 1.4 copy.46.table
  3.4 1.4 copy.45.router
  4.8 86.6 %front.1 = (bf16[2,1024,768]{2,1,0:T(8,128)(2,1)}, bf16[768,640]{1,0:T(8,128)(2,1)}, bf16[2,9,1024,64]{3,2,1,0:T(8,128)(2,1)}, bf16[2,3,1024,1024]{3,2,1,0:T(8,1...) custom-call(bf16[8,256,768]{2,1,0:T(8,128)(2,1)} %tok.1, ...), custom_call_target="tpu_custom_call" | custom-call | tf_op jit(solution)/shard_map/front/pallas_call | solution.py:482
  91.4 0.7 dynamic-slice_bitcast_fusion.1
  92.1 0.2 convert_reduce_fusion
  92.4 0.0 copy-start.14
  92.4 0.8 slice_reduce_fusion
  93.2 2.7 multiply_reduce_fusion.2
  95.9 0.0 copy-start.10
  95.9 0.6 copy-done.10
  96.5 0.2 multiply_convert_fusion
  96.7 0.0 copy-start.2
  96.7 1.6 fusion.27
  98.4 0.0 copy-start.5
  98.4 0.6 copy-done.5
  99.0 0.6 copy-done.8
  99.6 0.0 copy-done
  99.6 0.2 fusion
  99.8 2.5 convolution_convert_fusion
  102.3 4.2 %reshape.165 = bf16[8,80,2,768]{3,2,1,0:T(2,128)(2,1)S(1)} reshape(bf16[640,1536]{1,0:T(8,128)(2,1)} %convolution_convert_fusion) | data formatting | bytes 3932160 | tf_op jit(solution)/shard_map/reshape | solution.py:1275
  106.6 1.5 copy.61
  108.1 128.2 %experts.1 = (bf16[8,2,80,768]{3,2,1,0:T(8,128)(2,1)}, f32[2,768,768]{2,1,0:T(8,128)}, f32[2,768,768]{2,1,0:T(8,128)}) custom-call(bf16[8,2,80,768]{3,2,1,0:T(8,128)(2,1)} %bitcast.50, bf16[2,768,768]{2,1,0:T(8,128)(2,1)} %up.1, bf16[2,768,768]{2,1,0:T(8,128)(2,1)} %down.1), custom_call_target="tpu_custom_call" | custom-call | tf_op jit(solution)/shard_map/experts/pallas_call | solution.py:688
  236.3 3.2 copy.49
  239.5 0.0 copy-start.15
  239.5 0.3 copy.58
  239.8 0.3 copy-done.15
  240.2 1.4 fusion.5
  241.6 0.0 copy-start.6
  241.6 0.0 copy-start.11
  241.6 1.3 add_convert_fusion
  243.0 0.0 copy-start.3
  243.0 0.0 copy-start.13
  243.0 1.8 multiply_reduce_fusion
  244.8 1.2 fusion.24.router
  245.9 0.6 reshape.170.gain_f
  246.5 1.9 fusion.25
  248.4 126.2 %back.1 = (bf16[8,256,768]{2,1,0:T(8,128)(2,1)}, bf16[8,256,768]{2,1,0:T(8,128)(2,1)}, f32[96,640]{1,0:T(8,128)}, f32[96,128]{1,0:T(8,128)}, f32[192,128]{1,0:T(...) custom-call(bf16[2,256,768]{2,1,0:T(8,128)(2,1)} %bitcast.57, bf16[2,256,768]{2,1,0:T(8,128)(2,1)} %bitcast.58, ...), custom_call_target="tpu_custom_call" | custom-call | tf_op jit(solution)/shard_map/back/pallas_call | solution.py:1124
  374.6 1.3 slice_bitcast_fusion.1
  375.9 1.3 slice_bitcast_fusion
  377.2 0.9 slice.47
  378.1 0.7 copy.51
  378.8 1.9 fusion.26
  380.7 3.9 copy.68
  384.6 1.7 copy.69
  386.3 0.6 copy.70
  386.9 2.2 copy.71
  389.1 2.2 copy.72
  (40 shorter events, 0.2 us)
Async XLA Ops:
  92.4 7.4 %copy-start.14 = (s32[512]{0:T(512)}, s32[512]{0:T(512)S(1)}, u32[]{:S(2)}) copy-start(s32[512]{0:T(512)S(1)} %fusion.15) | copy-start | bytes 6148
  95.9 2.5 copy-start.12
  95.9 0.6 copy-start.10
  96.5 3.1 copy-start
  96.7 3.1 copy-start.2
  98.4 0.6 copy-start.5
  99.0 0.6 copy-start.8
  239.5 0.7 copy-start.15
  240.2 1.5 copy-start.1
  240.2 1.5 copy-start.9
  241.6 1.3 copy-start.6
  241.6 1.3 copy-start.11
  243.0 1.8 copy-start.3
  243.0 3.5 copy-start.13
  377.2 9.8 %slice-start.2 = ((s8[4718592]{0:T(1024)(128)(4,1)}), s8[524288]{0:T(1024)(128)(4,1)S(1)}, s32[]{:S(2)}) async-start(s8[4718592]{0:T(1024)(128)(4,1)} %bitcast.55), calls=%async_computation.2 | async-start | bytes 1048576
  378.8 5.8 %copy-start.4 = (bf16[8,256,768]{2,1,0:T(8,128)(2,1)S(1)}, bf16[8,256,768]{2,1,0:T(8,128)(2,1)}, u32[]{:S(2)}) copy-start(bf16[8,256,768]{2,1,0:T(8,128)(2,1)} %get-tuple-element.133) | copy-start | bytes 9437188
  380.7 6.2 %slice-start.3 = ((s8[4718592]{0:T(1024)(128)(4,1)}), s8[4194304]{0:T(1024)(128)(4,1)S(1)}, s32[]{:S(2)}) async-start(s8[4718592]{0:T(1024)(128)(4,1)} %bitcast.55), calls=%async_computation.3 | async-start | bytes 8388608
  384.6 1.7 copy-start.7
  384.6 4.5 %slice-start = ((s8[4718592]{0:T(1024)(128)(4,1)}), s8[4194304]{0:T(1024)(128)(4,1)S(1)}, s32[]{:S(2)}) async-start(s8[4718592]{0:T(1024)(128)(4,1)} %bitcast.53), calls=%async_computation | async-start | bytes 8388608
  386.9 2.2 slice-start.1
